TPU v7x, 256 devices: a whole 4x4x8 slice. The times are simulated.
256 devices in a mesh: ctx: 64 (over x, z, core), tp: 4 (over y).
Axes of the slice: x: 4, y: 4, z: 8, core: 2. Of those that a mesh axis runs over, the one named last changes fastest.
Arguments:
- tokens: bfloat16 [16384, 7168], P('ctx', 'tp'), may hold values from -6 to 6
- router_weight: bfloat16 [7168], P('tp'), may hold values from -0.0625 to 0.0625
- queries: bfloat16 [16384, 3584], P('ctx', 'tp'), may hold values from -48 to 48
- keys_values: bfloat16 [16384, 2, 512], P('ctx', None, 'tp'), may hold values from -12 to 12
- routed_grad: bfloat16 [16384, 3584], P('ctx', 'tp'), may hold values from -6 to 6
- chosen: int32 [64, 64], P('ctx'), may hold values from 0 to 255, as said below
- counts: int32 [64], replicated, may hold values from 1 to 64, 2048 in all
Outputs:
- routed: bfloat16 [16384, 3584], P('ctx', 'tp')
- d_queries: bfloat16 [16384, 3584], P('ctx', 'tp')
- key_value_gradient: bfloat16 [16384, 2, 512], P('ctx', None, 'tp')
- router_grad: float32 [7168], P('tp')
Inputs may be any that keep to these rules, and one draw needn't show every extreme that they name: `chosen`: row c holds 64 distinct positions of shard c in increasing order; its first counts[c] entries are the routed tokens. The counts sum to 2048; the largest equals 64.
All inputs are finite; a program needn't handle non-finite values.
Results may differ from a plain program's by a relative error of at most 0.011.
Values may be sent and summed in bfloat16 or wider, within the bound.
No kernel may reach another device: no remote copies, remote signals or barrier semaphores. Data moves between devices by JAX's collectives and lax.ppermute only.
A program may use at most 64 MiB of HBM per device.

v0:
```python
import jax
import jax.numpy as jnp
from jax import lax
from jax.sharding import PartitionSpec as P

HEAD_SIZE = 128


def score_block(query_block, key_rows, key_rank, key_valid, query_rank):
    scores = jnp.einsum(
        "bhgd,khd->hgbk", query_block, key_rows, preferred_element_type=jnp.float32
    ) * HEAD_SIZE ** (-0.5)
    allowed = key_valid[None, None, None, :] & (
        key_rank[None, None, None, :] <= query_rank[None, None, :, None]
    )
    return jnp.where(allowed, scores, -jnp.inf)


def split_blocks(query_rows, kv_heads):
    row_count = query_rows.shape[0]
    block_rows = min(row_count, 64)
    blocks = row_count // block_rows
    query_group_width = query_rows.shape[1] // (kv_heads * HEAD_SIZE)
    return (blocks, block_rows, query_group_width)


def attend_forward(query_rows, query_rank, key_rows, value_rows, key_rank, key_valid):
    kv_heads = key_rows.shape[1]
    blocks, block_rows, query_group_width = split_blocks(query_rows, kv_heads)
    query_blocks = query_rows.reshape(blocks, block_rows, kv_heads, query_group_width, HEAD_SIZE)
    rank_blocks = query_rank.reshape(blocks, block_rows)

    def forward_block(pieces):
        query_block, rank_block = pieces
        scores = score_block(query_block, key_rows, key_rank, key_valid, rank_block)
        row_max = jnp.max(scores, axis=-1, keepdims=True)
        weights = jnp.exp(scores - row_max)
        row_sum = jnp.sum(weights, axis=-1, keepdims=True)
        weights_low = (weights / row_sum).astype(jnp.bfloat16)
        mixture = jnp.einsum(
            "hgbk,khd->bhgd", weights_low, value_rows, preferred_element_type=jnp.float32
        )
        return (mixture.astype(jnp.bfloat16).reshape(block_rows, -1), row_max, row_sum)

    attended, row_maxes, row_sums = lax.map(forward_block, (query_blocks, rank_blocks))
    return (attended.reshape(query_rows.shape[0], -1), row_maxes, row_sums)


def attend_backward(
    query_rows, query_rank, d_rows, key_rows, value_rows, key_rank, key_valid, row_maxes, row_sums
):
    kv_heads = key_rows.shape[1]
    blocks, block_rows, query_group_width = split_blocks(query_rows, kv_heads)
    query_blocks = query_rows.reshape(blocks, block_rows, kv_heads, query_group_width, HEAD_SIZE)
    rank_blocks = query_rank.reshape(blocks, block_rows)
    d_blocks = d_rows.reshape(blocks, block_rows, kv_heads, query_group_width, HEAD_SIZE)
    scale_value = HEAD_SIZE ** (-0.5)

    def backward_block(totals, pieces):
        d_keys, d_values = totals
        query_block, rank_block, d_block, row_max, row_sum = pieces
        scores = score_block(query_block, key_rows, key_rank, key_valid, rank_block)
        probs = jnp.exp(scores - row_max) / row_sum
        weights_low = probs.astype(jnp.bfloat16)
        d_values = d_values + jnp.einsum(
            "hgbk,bhgd->khd", weights_low, d_block, preferred_element_type=jnp.float32
        )
        d_probs = jnp.einsum(
            "bhgd,khd->hgbk", d_block, value_rows, preferred_element_type=jnp.float32
        )
        row_delta = jnp.sum(probs * d_probs, axis=-1, keepdims=True)
        d_scores = (probs * (d_probs - row_delta)).astype(jnp.bfloat16)
        d_query = (
            jnp.einsum("hgbk,khd->bhgd", d_scores, key_rows, preferred_element_type=jnp.float32)
            * scale_value
        )
        d_keys = (
            d_keys
            + jnp.einsum(
                "hgbk,bhgd->khd", d_scores, query_block, preferred_element_type=jnp.float32
            )
            * scale_value
        )
        return ((d_keys, d_values), d_query.astype(jnp.bfloat16).reshape(block_rows, -1))

    empty = jnp.zeros(key_rows.shape, jnp.float32)
    (d_keys, d_values), d_queries = lax.scan(
        backward_block, (empty, empty), (query_blocks, rank_blocks, d_blocks, row_maxes, row_sums)
    )
    return (d_queries.reshape(query_rows.shape[0], -1), d_keys, d_values)


def split_pairs(all_pairs, kv_heads):
    key_count = all_pairs.shape[0]
    kv_width = kv_heads * HEAD_SIZE
    key_rows = all_pairs[:, :kv_width].reshape(key_count, kv_heads, HEAD_SIZE)
    value_rows = all_pairs[:, kv_width:].reshape(key_count, kv_heads, HEAD_SIZE)
    return (key_rows, value_rows)


def join_pairs(d_keys, d_values):
    key_count = d_keys.shape[0]
    return jnp.concatenate((d_keys.reshape(key_count, -1), d_values.reshape(key_count, -1)), axis=1)


def on_device(tokens, router_weight, queries, keys_values, routed_grad, chosen, counts):
    shards = lax.axis_size("ctx")
    this_shard = lax.axis_index("ctx")
    capacity = chosen.shape[1]
    local_rows = chosen[0]
    kv_heads = keys_values.shape[2] // HEAD_SIZE
    slot_ids = jnp.arange(capacity, dtype=jnp.int32)
    shard_ids = jnp.arange(shards, dtype=jnp.int32)
    offsets = jnp.cumsum(counts) - counts
    is_mine = shard_ids == this_shard
    my_offset = jnp.sum(jnp.where(is_mine, offsets, 0))
    my_count = jnp.sum(jnp.where(is_mine, counts, 0))
    is_live = slot_ids < my_count
    feature_rows = tokens[local_rows]
    logit_part = jnp.dot(feature_rows, router_weight, preferred_element_type=jnp.float32)
    logits = lax.psum(logit_part, "tp")
    gate_value = jax.nn.sigmoid(logits)
    query_rows = queries[local_rows]
    key_value_rows = keys_values[local_rows].reshape(capacity, -1)
    all_pairs = lax.all_gather(key_value_rows, "ctx", axis=0, tiled=True)
    key_rows, value_rows = split_pairs(all_pairs, kv_heads)
    key_rank = (offsets[:, None] + slot_ids[None, :]).reshape(-1)
    key_valid = (slot_ids[None, :] < counts[:, None]).reshape(-1)
    query_rank = jnp.where(is_live, my_offset + slot_ids, 1 << 30)
    attended, row_maxes, row_sums = attend_forward(
        query_rows, query_rank, key_rows, value_rows, key_rank, key_valid
    )
    routed_rows = (gate_value[:, None] * attended.astype(jnp.float32)).astype(jnp.bfloat16)
    grad_rows = routed_grad[local_rows].astype(jnp.float32)
    gate_part = jnp.sum(grad_rows * attended.astype(jnp.float32), axis=1)
    d_gate = lax.psum(gate_part, "tp")
    d_attended = jnp.where(is_live[:, None], gate_value[:, None] * grad_rows, 0.0).astype(
        jnp.bfloat16
    )
    d_logit = jnp.where(is_live, d_gate * gate_value * (1.0 - gate_value), 0.0)
    routed_rows, d_attended, d_logit = (routed_rows, d_attended, d_logit)
    d_query, d_keys, d_values = attend_backward(
        query_rows,
        query_rank,
        d_attended,
        key_rows,
        value_rows,
        key_rank,
        key_valid,
        row_maxes,
        row_sums,
    )
    own_pairs = lax.psum_scatter(
        join_pairs(d_keys, d_values), "ctx", scatter_dimension=0, tiled=True
    ).astype(jnp.bfloat16)
    live_column = is_live[:, None]
    routed = (
        jnp.zeros(queries.shape, jnp.bfloat16)
        .at[local_rows]
        .set(jnp.where(live_column, routed_rows, 0))
    )
    d_queries = (
        jnp.zeros(queries.shape, jnp.bfloat16)
        .at[local_rows]
        .set(jnp.where(live_column, d_query, 0))
    )
    pair_update = jnp.where(live_column, own_pairs, 0).reshape(capacity, 2, -1)
    key_value_gradient = jnp.zeros(keys_values.shape, jnp.bfloat16).at[local_rows].set(pair_update)
    router_part = jnp.sum(feature_rows.astype(jnp.float32) * d_logit[:, None], axis=0)
    router_grad = lax.psum(router_part, "ctx")
    return (routed, d_queries, key_value_gradient, router_grad)


def solution(mesh):
    placed = (
        P("ctx", "tp"),
        P("tp"),
        P("ctx", "tp"),
        P("ctx", None, "tp"),
        P("ctx", "tp"),
        P("ctx", None),
        P(),
    )
    return jax.shard_map(
        on_device,
        mesh=mesh,
        in_specs=placed,
        out_specs=(P("ctx", "tp"), P("ctx", "tp"), P("ctx", None, "tp"), P("tp")),
        check_vma=False,
    )
```

profile of v0, /device:TPU:2, one launch (start us, length us, event | category | flops | bytes accessed | tf_op | source)
XLA Modules:
  0.0 279.3 jit_solution(14079482696437200401)
XLA Ops:
  7.2 0.7 fusion.50
  8.0 1.6 gather_fusion.1
  9.5 0.6 copy.76
  10.2 0.0 reduce-scatter.4.cloned.1.call-start
  10.2 1.9 gather_fusion.3
  12.1 0.8 reshape.317
  12.9 0.7 copy.34
  13.7 0.1 reduce-window.9
  13.8 0.1 reduce.4
  13.9 1.4 fusion.49
  15.2 0.1 iota_add_fusion
  15.3 0.1 add.63
  15.4 0.7 iota_compare_fusion
  16.1 0.1 lt.56
  16.2 1.9 gather_fusion.2
  18.1 0.7 gather_fusion
  18.8 0.7 reshape.376
  19.5 0.6 iota_compare_fusion.1
  20.2 1.3 add_select_fusion
  21.4 0.1 convolution_bitcast_fusion.2
  21.6 1.0 compare_and_fusion
  22.6 68.1 %all-gather.2.cloned.1.call-done = bf16[4096,256]{1,0:T(8,128)(2,1)} async-done(((bf16[64,256]{1,0:T(8,128)(2,1)}), bf16[4096,256]{1,0:T(8,128)(2,1)}) %all-gather.2.cloned.1.call-update) | async-done | bytes 2097168 | tf_op jit(solution)/shard_map/all_gather | solution.py:125
  90.7 2.8 %fusion.55 = (f32[7,64]{1,0:T(8,128)S(1)}, f32[1,7,64,4096]{3,2,1,0:T(8,128)S(1)}) fusion(bf16[4096,256]{1,0:T(8,128)(2,1)} %all-gather.2.cloned.1.call-done, pred[64,4096]{1,0:T(8,128)(4,1)} %compare_and_fusion, bf16[64,896]{1,0:T(8,128)(2,1)S(1)} %gather_fusion.2), kind=kOutput, calls=%fused_computation.79 | convolution fusion | flops 475266624 | bytes 8767232 | tf_op jit(solution)/shard_map/while/body/eval_jaxpr/bhgd,khd->hgbk/dot_general | solution.py:10
  93.5 1.1 fusion.4
  94.6 2.1 fusion.31
  96.7 10.7 %all-reduce = (f32[64]{0:T(128)S(1)}, f32[64]{0:T(128)S(1)}) all-reduce(f32[64]{0:T(128)S(1)} %convolution_bitcast_fusion.2, f32[64]{0:T(128)S(1)} %get-tuple-element.69), channel_id=1, replica_groups=mesh['ctx'=64,'tp'=4] {'tp'}, use_global_device_ids=true, to_apply=%region_1.2 | all-reduce | flops 128 | bytes 1024 | tf_op jit(solution)/shard_map/psum | solution.py:121
  107.4 0.6 multiply_select_fusion
  108.0 4.9 %convolution_bitcast_fusion = f32[4096,128]{0,1:T(8,128)S(1)} fusion(f32[64]{0:T(128)S(1)} %get-tuple-element.50, pred[64]{0:T(512)(128)(4,1)S(1)} %iota_compare_fusion.1, f32[1,7,64,4096]{3,2,1,0:T(8,128)} %copy-done.2, f32[7,64]{1,0:T(8,128)S(1)} %fusion.4, f32[7,64]{1,0:T(8,128)S(1)} %get-tuple-element.67, bf16[64,896]{1,0:T(8,128)(2,1)S(1)} %gather_fusion.3), kind=kOutput, calls=%fused_computation.16 | convolution fusion | flops 475496448 | bytes 9555776 | tf_op jit(solution)/shard_map/while/body/eval_jaxpr/hgbk,bhgd->khd/dot_general | solution.py:65
  112.9 0.3 copy-done.3
  113.2 2.0 fusion
  115.2 2.7 fusion.7
  117.9 1.9 copy-done.1
  119.7 0.7 fusion.6
  120.5 2.3 pad_maximum_fusion
  122.8 5.6 %copy.42 = f32[4096,256]{1,0:T(8,128)} copy(f32[4096,256]{0,1:T(8,128)} %pad_maximum_fusion) | data formatting | bytes 8388608
  128.4 1.1 copy.36
  129.5 3.1 %fusion.26 = bf16[64,1,7,128]{3,0,2,1:T(8,128)(2,1)S(1)} fusion(bf16[7,64,4096]{2,1,0:T(8,128)(2,1)} %copy-done.1, bf16[4096,256]{1,0:T(8,128)(2,1)S(1)} %copy-done.4), kind=kOutput, calls=%fused_computation.33 | convolution fusion | flops 469876736 | bytes 4833280 | tf_op jit(solution)/shard_map/while/body/eval_jaxpr/hgbk,khd->bhgd/dot_general | solution.py:74
  132.6 0.1 copy.38
  132.7 1.8 scatter_custom_fusion
  134.5 1.7 scatter_custom_fusion.1
  136.2 0.1 multiply_reduce_fusion
  136.3 108.4 %psum.23 = f32[1792]{0:T(1024)} all-reduce(f32[1792]{0:T(1024)S(1)} %multiply_reduce_fusion), channel_id=1, replica_groups=mesh['ctx'=64,'tp'=4] {'ctx'}, use_global_device_ids=true, to_apply=%region_14.15 | all-reduce | flops 1792 | bytes 14336 | tf_op jit(solution)/shard_map/psum | solution.py:170
  244.8 23.4 %reduce-scatter.4.cloned.1.call-done = f32[64,256]{1,0:T(8,128)} async-done(((f32[4096,256]{1,0:T(8,128)}), f32[64,256]{1,0:T(8,128)}) %reduce-scatter.4.cloned.1.call-update) | async-done | bytes 65552
  268.2 0.9 copy.43
  269.1 0.1 copy.40
  269.2 0.1 broadcast_in_dim.121
  269.3 2.5 scatter_fusion
  271.8 0.6 copy-done.6
  (16 shorter events, 0.1 us)
Async XLA Ops:
  7.2 10.9 %copy-start = (bf16[256,1792]{1,0:T(8,128)(2,1)S(1)}, bf16[256,1792]{1,0:T(8,128)(2,1)}, u32[]{:S(2)}) copy-start(bf16[256,1792]{1,0:T(8,128)(2,1)} %param.7) | copy-start | bytes 2752516
  7.2 83.5 %all-gather.2.cloned.1.call-start = ((), (), s32[]{:S(2)}) async-start(), calls=%async_computation.1 | async-start | bytes 2129920 | tf_op jit(solution)/shard_map/all_gather | solution.py:125
  10.2 258.0 %reduce-scatter.4.cloned.1.call-start = ((), (), s32[]{:S(2)}) async-start(), calls=%async_computation.2 | async-start | bytes 4259840
  90.7 3.9 %copy-start.4 = (bf16[4096,256]{1,0:T(8,128)(2,1)S(1)}, bf16[4096,256]{1,0:T(8,128)(2,1)}, u32[]{:S(2)}) copy-start(bf16[4096,256]{1,0:T(8,128)(2,1)} %all-gather.2.cloned.1.call-done) | copy-start | bytes 6291460
  90.7 3.9 %copy-start.5 = (f32[64,1,7,128]{3,2,0,1:T(8,128)S(1)}, f32[64,1,7,128]{3,2,0,1:T(8,128)}, u32[]{:S(2)}) copy-start(f32[64,1,7,128]{3,2,0,1:T(8,128)} %reshape.317) | copy-start | bytes 688132
  93.5 3.2 %copy-start.2 = (f32[1,7,64,4096]{3,2,1,0:T(8,128)}, f32[1,7,64,4096]{3,2,1,0:T(8,128)S(1)}, u32[]{:S(2)}) copy-start(f32[1,7,64,4096]{3,2,1,0:T(8,128)S(1)} %get-tuple-element.68) | copy-start | bytes 22020100
  108.0 5.2 %copy-start.3 = (f32[1,7,64,4096]{3,2,1,0:T(8,128)S(1)}, f32[1,7,64,4096]{3,2,1,0:T(8,128)}, u32[]{:S(2)}) copy-start(f32[1,7,64,4096]{3,2,1,0:T(8,128)} %copy-done.2) | copy-start | bytes 22020100
  117.9 1.9 copy-start.1
  271.8 0.7 copy-start.6
Sparse Core Ops, SparseCore 0:
  11.4 79.2 all-gather.1
  128.5 139.6 reduce-scatter.3
where the time goes:
time: 281 us; the launch traced here: 279 us
  blocking collectives  119 us (42%)
  waiting for transfers between devices  91.5 us (33%)
  local copies, waits for them, and re-layouts  22.3 us (8%)
  other arithmetic  16.3 us (6%)
  matrix products  15.8 us (6%)
  between operations  14.2 us (5%)
    psum x1, blocking collectives, on_device(): router_grad = lax.psum(router_part, 'ctx')  108 us
    all_gather x1, waiting for transfers between devices, on_device(): all_pairs = lax.all_gather(key_value_rows, 'ctx', axis=0, tiled=True)  68.1 us
    unnamed x3, waiting for transfers between devices  23.4 us
    unnamed x18, local copies, waits for them, and re-layouts  10.7 us
    psum x1, blocking collectives, on_device(): logits = lax.psum(logit_part, 'tp')  10.7 us
  transfers between devices with their start and end apart: 2, of which 2 were waited for; matrix products, arithmetic and copies ran while one was open for 7% of the time, Pallas kernels for 0%

commit v1 on v0

--- a/solution.py
+++ b/solution.py
@@ -4,6 +4,87 @@
 from jax.sharding import PartitionSpec as P
 
 HEAD_SIZE = 128
+NX, NZ = 4, 8
+
+
+def shard_of(x, z, c):
+    return (x * NZ + z) * 2 + c
+
+
+def move(value, target):
+    pairs = [
+        (shard_of(x, z, c), shard_of(*target(x, z, c)))
+        for x in range(NX)
+        for z in range(NZ)
+        for c in range(2)
+    ]
+    return lax.ppermute(value, "ctx", pairs)
+
+
+def by_x(k):
+    return lambda x, z, c: ((x + k) % NX, z, c)
+
+
+def by_z(k):
+    return lambda x, z, c: (x, (z + k) % NZ, c)
+
+
+def flip_z(x, z, c):
+    return (x, z ^ 1, c)
+
+
+def flip_core(x, z, c):
+    return (x, z, c ^ 1)
+
+
+def gather_shards(rows):
+    rows = jnp.concatenate([rows, move(rows, flip_z)])
+    rows = jnp.concatenate([rows] + [move(rows, by_z(k)) for k in (2, 4, 6)])
+    rows = jnp.concatenate([rows] + [move(rows, by_x(k)) for k in (1, 2, 3)])
+    return jnp.concatenate([rows, move(rows, flip_core)])
+
+
+def block_shards(this_shard):
+    core = this_shard % 2
+    z = (this_shard // 2) % NZ
+    x = this_shard // (2 * NZ)
+    blocks = jnp.arange(2 * NX * NZ, dtype=jnp.int32)
+    z_flip, z_shift, x_shift, core_flip = (
+        blocks % 2,
+        (blocks // 2) % 4,
+        (blocks // 8) % 4,
+        blocks // 32,
+    )
+    return shard_of(
+        (x - x_shift + NX) % NX, ((z ^ z_flip) - 2 * z_shift + NZ) % NZ, core ^ core_flip
+    )
+
+
+def sum_parts(parts):
+    total = parts[0].astype(jnp.float32)
+    for part in parts[1:]:
+        total = total + part.astype(jnp.float32)
+    return total
+
+
+def reduce_step(total, targets):
+    low = total.astype(jnp.bfloat16)
+    return sum_parts([total[0]] + [move(low[i + 1], t) for i, t in enumerate(targets)])
+
+
+def reduce_shards(total):
+    total = total.reshape(2, 4, 4, 2, -1, total.shape[-1])
+    total = reduce_step(total, [flip_core])
+    total = reduce_step(total, [by_x(-k) for k in (1, 2, 3)])
+    total = reduce_step(total, [by_z(-k) for k in (2, 4, 6)])
+    return reduce_step(total, [flip_z])
+
+
+def sum_over_ctx(part):
+    part = part + move(part, flip_core)
+    part = part + sum_parts([move(part, by_x(k)) for k in (1, 2, 3)])
+    part = part + move(part, flip_z)
+    return part + sum_parts([move(part, by_z(k)) for k in (2, 4, 6)])
 
 
 def score_block(query_block, key_rows, key_rank, key_valid, query_rank):
@@ -122,10 +203,11 @@
     gate_value = jax.nn.sigmoid(logits)
     query_rows = queries[local_rows]
     key_value_rows = keys_values[local_rows].reshape(capacity, -1)
-    all_pairs = lax.all_gather(key_value_rows, "ctx", axis=0, tiled=True)
+    all_pairs = gather_shards(key_value_rows)
+    block_ids = block_shards(this_shard)
     key_rows, value_rows = split_pairs(all_pairs, kv_heads)
-    key_rank = (offsets[:, None] + slot_ids[None, :]).reshape(-1)
-    key_valid = (slot_ids[None, :] < counts[:, None]).reshape(-1)
+    key_rank = (offsets[block_ids][:, None] + slot_ids[None, :]).reshape(-1)
+    key_valid = (slot_ids[None, :] < counts[block_ids][:, None]).reshape(-1)
     query_rank = jnp.where(is_live, my_offset + slot_ids, 1 << 30)
     attended, row_maxes, row_sums = attend_forward(
         query_rows, query_rank, key_rows, value_rows, key_rank, key_valid
@@ -150,9 +232,7 @@
         row_maxes,
         row_sums,
     )
-    own_pairs = lax.psum_scatter(
-        join_pairs(d_keys, d_values), "ctx", scatter_dimension=0, tiled=True
-    ).astype(jnp.bfloat16)
+    own_pairs = reduce_shards(join_pairs(d_keys, d_values)).astype(jnp.bfloat16)
     live_column = is_live[:, None]
     routed = (
         jnp.zeros(queries.shape, jnp.bfloat16)
@@ -167,7 +247,7 @@
     pair_update = jnp.where(live_column, own_pairs, 0).reshape(capacity, 2, -1)
     key_value_gradient = jnp.zeros(keys_values.shape, jnp.bfloat16).at[local_rows].set(pair_update)
     router_part = jnp.sum(feature_rows.astype(jnp.float32) * d_logit[:, None], axis=0)
-    router_grad = lax.psum(router_part, "ctx")
+    router_grad = sum_over_ctx(router_part)
     return (routed, d_queries, key_value_gradient, router_grad)
 
 

time: 281 us -> 145 us (0.52)
  blocking collectives: 119 us -> 10.9 us
  waiting for transfers between devices: 91.5 us -> 26.8 us
  starting transfers between devices: 0.08 us -> 41.3 us
  between operations: 14.2 us -> 1 us
  matrix products: 15.8 us -> 19.5 us
  local copies, waits for them, and re-layouts: 22.3 us -> 25.7 us
  other arithmetic: 16.3 us -> 19.2 us
    psum x1 -> x0, blocking collectives: 108 us -> none  [on_device(): router_grad = lax.psum(router_part, 'ctx')]
    all_gather x1 -> x0, waiting for transfers between devices: 68.1 us -> none  [on_device(): all_pairs = lax.all_gather(key_value_rows, 'ctx', axis=0, tiled=True)]
    ppermute x0 -> x24, starting transfers between devices: none -> 41.3 us  [move(): return lax.ppermute(value, 'ctx', pairs)]
    ppermute x0 -> x24, waiting for transfers between devices: none -> 26.8 us  [move(): return lax.ppermute(value, 'ctx', pairs)]
    unnamed x3 -> x0, waiting for transfers between devices: 23.4 us -> none
    another operation x1 -> x3, local copies, waits for them, and re-layouts: 0.74 us -> 5.26 us
    dot_general x1, matrix products: 2.02 us -> 5.49 us  [backward_block(): jnp.einsum('bhgd,khd->hgbk', d_block, value_rows, preferred_element_type=...]
    unnamed x18 -> x31, local copies, waits for them, and re-layouts: 10.7 us -> 7.55 us
  transfers between devices with their start and end apart: 2 -> 24, of which waited for: 2 -> 9; matrix products, arithmetic and copies ran while one was open for 7% -> 16% of each run, Pallas kernels for 0% -> 0%
where the time goes in v1:
time: 145 us; the launch traced here: 144 us
  starting transfers between devices  41.3 us (28%)
  waiting for transfers between devices  26.8 us (18%)
  local copies, waits for them, and re-layouts  25.7 us (18%)
  matrix products  19.5 us (13%)
  other arithmetic  19.2 us (13%)
  blocking collectives  10.9 us (8%)
    ppermute x24, starting transfers between devices, move(): return lax.ppermute(value, 'ctx', pairs)  41.3 us
    ppermute x24, waiting for transfers between devices, move(): return lax.ppermute(value, 'ctx', pairs)  26.8 us
    psum x1, blocking collectives, on_device(): logits = lax.psum(logit_part, 'tp')  10.9 us
    unnamed x31, local copies, waits for them, and re-layouts  7.55 us
    dot_general x1, matrix products, backward_block(): jnp.einsum('bhgd,khd->hgbk', d_block, value_rows, preferred_element_type=...  5.49 us
    another operation x3, local copies, waits for them, and re-layouts  5.26 us
    dot_general x1, matrix products, backward_block(): jnp.einsum('hgbk,bhgd->khd', weights_low, d_block, preferred_element_type...  3.44 us
    dot_general x1, matrix products, forward_block(): jnp.einsum('hgbk,khd->bhgd', weights_low, value_rows, preferred_element_t...  3.26 us
  transfers between devices with their start and end apart: 24, of which 9 were waited for; matrix products, arithmetic and copies ran while one was open for 16% of the time, Pallas kernels for 0%

profile of v1, /device:TPU:2, one launch (start us, length us, event | category | flops | bytes accessed | tf_op | source)
XLA Modules:
  0.0 144.4 jit_solution(7955498786465178305)
XLA Ops:
  1.5 1.6 %gather_fusion.1 = bf16[64,2,128]{2,1,0:T(2,128)(2,1)S(1)} fusion(bf16[256,2,128]{2,1,0:T(2,128)(2,1)} %param.10, s32[1024]{0:T(1024)S(1)} %get-tuple-element.124), kind=kCustom, calls=%fused_computation.1 | custom fusion | bytes 65792 | tf_op jit(solution)/shard_map/gather | solution.py:205
  3.0 2.0 %collective-permute-start = (bf16[64,256]{1,0:T(8,128)(2,1)S(1)}, bf16[64,256]{1,0:T(8,128)(2,1)S(1)}, u32[]{:S(2)}, u32[]{:S(2)}) collective-permute-start(bf16[64,256]{1,0:T(8,128)(2,1)S(1)} %bitcast.209), channel_id=1, source_target_pairs={{0,8},{4,12},{8,0},{12,4},{16,24},{20,28},{24,16},{28,20},{32,40},... | collective-permute-start | bytes 98312 | tf_op jit(solution)/shard_map/ppermute | solution.py:21
  6.6 1.3 fusion.62
  9.4 3.3 %collective-permute-start.1 = (bf16[128,256]{1,0:T(8,128)(2,1)S(1)}, bf16[128,256]{1,0:T(8,128)(2,1)S(1)}, u32[]{:S(2)}, u32[]{:S(2)}) collective-permute-start(bf16[128,256]{1,0:T(8,128)(2,1)S(1)} %get-tuple-element.107), channel_id=1, source_target_pairs={{0,16},{4,20},{8,24},{12,28},{16,32},{20,36},{24,40},{28,44},{32,4... | collective-permute-start | bytes 196616 | tf_op jit(solution)/shard_map/ppermute | solution.py:21
  12.7 1.4 gather_fusion.2
  14.1 4.6 %collective-permute-start.2 = (bf16[128,256]{1,0:T(8,128)(2,1)S(1)}, bf16[128,256]{1,0:T(8,128)(2,1)S(1)}, u32[]{:S(2)}, u32[]{:S(2)}) collective-permute-start(bf16[128,256]{1,0:T(8,128)(2,1)S(1)} %get-tuple-element.107), channel_id=1, source_target_pairs={{0,32},{4,36},{8,40},{12,44},{16,48},{20,52},{24,56},{28,60},{32,0... | collective-permute-start | bytes 196616 | tf_op jit(solution)/shard_map/ppermute | solution.py:21
  18.7 2.7 %collective-permute-start.3 = (bf16[128,256]{1,0:T(8,128)(2,1)S(1)}, bf16[128,256]{1,0:T(8,128)(2,1)S(1)}, u32[]{:S(2)}, u32[]{:S(2)}) collective-permute-start(bf16[128,256]{1,0:T(8,128)(2,1)S(1)} %get-tuple-element.107), channel_id=1, source_target_pairs={{0,48},{4,52},{8,56},{12,60},{16,0},{20,4},{24,8},{28,12},{32,16},... | collective-permute-start | bytes 196616 | tf_op jit(solution)/shard_map/ppermute | solution.py:21
  23.8 1.2 collective-permute-done.3
  25.7 1.5 %collective-permute-start.4 = (bf16[512,256]{1,0:T(8,128)(2,1)S(1)}, bf16[512,256]{1,0:T(8,128)(2,1)S(1)}, u32[]{:S(2)}, u32[]{:S(2)}) collective-permute-start(bf16[512,256]{1,0:T(8,128)(2,1)S(1)} %get-tuple-element.97), channel_id=1, source_target_pairs={{0,64},{4,68},{8,72},{12,76},{16,80},{20,84},{24,88},{28,92},{32,9... | collective-permute-start | bytes 786440 | tf_op jit(solution)/shard_map/ppermute | solution.py:21
  27.2 1.1 collective-permute-start.5
  28.4 2.2 %collective-permute-start.6 = (bf16[512,256]{1,0:T(8,128)(2,1)S(1)}, bf16[512,256]{1,0:T(8,128)(2,1)S(1)}, u32[]{:S(2)}, u32[]{:S(2)}) collective-permute-start(bf16[512,256]{1,0:T(8,128)(2,1)S(1)} %get-tuple-element.97), channel_id=1, source_target_pairs={{0,192},{4,196},{8,200},{12,204},{16,208},{20,212},{24,216},{28,22... | collective-permute-start | bytes 786440 | tf_op jit(solution)/shard_map/ppermute | solution.py:21
  31.2 3.7 %collective-permute-done.4 = bf16[512,256]{1,0:T(8,128)(2,1)S(1)} collective-permute-done((bf16[512,256]{1,0:T(8,128)(2,1)S(1)}, bf16[512,256]{1,0:T(8,128)(2,1)S(1)}, u32[]{:S(2)}, u32[]{:S(2)}) %collective-permute-start.4) | collective-permute-done | bytes 262176 | tf_op jit(solution)/shard_map/ppermute | solution.py:21
  35.8 2.0 %collective-permute-done.5 = bf16[512,256]{1,0:T(8,128)(2,1)S(1)} collective-permute-done((bf16[512,256]{1,0:T(8,128)(2,1)S(1)}, bf16[512,256]{1,0:T(8,128)(2,1)S(1)}, u32[]{:S(2)}, u32[]{:S(2)}) %collective-permute-start.5) | collective-permute-done | bytes 262176 | tf_op jit(solution)/shard_map/ppermute | solution.py:21
  38.6 1.4 collective-permute-done.6
  40.9 1.3 add_select_fusion
  46.2 2.6 %fusion.84 = (f32[7,64]{1,0:T(8,128)S(1)}, f32[1,7,64,4096]{3,2,1,0:T(8,128)S(1)}) fusion(bf16[4096,256]{1,0:T(8,128)(2,1)} %constant_dynamic-update-slice_fusion.15, pred[64,4096]{1,0:T(8,128)(4,1)S(1)} %compare_and_fusion, bf16[64,896]{1,0:T(8,128)(2,1)S(1)} %gather_fusion.4), kind=kOutput, calls=%fused_computation.170 | convolution fusion | flops 475266624 | bytes 8767232 | tf_op jit(solution)/shard_map/while/body/eval_jaxpr/bhgd,khd->hgbk/dot_general | solution.py:91
  48.8 1.1 fusion.4
  49.9 1.9 %copy-done.3 = f32[1,7,64,4096]{3,2,1,0:T(8,128)} copy-done((f32[1,7,64,4096]{3,2,1,0:T(8,128)}, f32[1,7,64,4096]{3,2,1,0:T(8,128)S(1)}, u32[]{:S(2)}) %copy-start.3) | copy-done | bytes 7340056
  51.8 3.3 %fusion.35 = (f32[64]{0:T(128)S(1)}, f32[64,1,7,128]{3,0,2,1:T(8,128)}) fusion(f32[64,1,7,128]{3,2,0,1:T(8,128)S(1)} %reshape.597, f32[7,64]{1,0:T(8,128)S(1)} %fusion.4, f32[1,7,64,4096]{3,2,1,0:T(8,128)S(1)} %get-tuple-element.114, f32[7,64]{1,0:T(8,128)S(1)} %get-tuple-element.113, bf16[4096,256]{1,0:T(8,128)(2,1)} %constant_dynamic-update-slice_fusion.15), kind=kOutput, calls=%fused_computation.59 | convolution fusion | flops 475496384 | bytes 8851200 | tf_op jit(solution)/shard_map/while/body/eval_jaxpr/hgbk,khd->bhgd/dot_general | solution.py:121
  55.1 10.9 %all-reduce = (f32[64]{0:T(128)S(1)}, f32[64]{0:T(128)S(1)}) all-reduce(f32[64]{0:T(128)S(1)} %convolution_bitcast_fusion.1, f32[64]{0:T(128)S(1)} %get-tuple-element.115), channel_id=1, replica_groups=mesh['ctx'=64,'tp'=4] {'tp'}, use_global_device_ids=true, to_apply=%region_1.2 | all-reduce | flops 128 | bytes 1024 | tf_op jit(solution)/shard_map/psum | solution.py:202
  66.7 5.5 %fusion = (f32[7,64]{1,0:T(8,128)S(1)}, f32[4096,64,7]{0,1,2:T(8,128)S(1)}) fusion(f32[7,64]{1,0:T(8,128)S(1)} %fusion.4, f32[1,7,64,4096]{3,2,1,0:T(8,128)} %copy-done.3, f32[7,64]{1,0:T(8,128)S(1)} %get-tuple-element.113, f32[64]{0:T(128)S(1)} %get-tuple-element.50, pred[64]{0:T(512)(128)(4,1)S(1)} %iota_compare_fusion.1, ...), kind=kOutput, calls=%fused_computation.12 | convolution fusion | flops 477331008 | bytes 15849024 | tf_op jit(solution)/shard_map/while/body/eval_jaxpr/bhgd,khd->hgbk/dot_general | solution.py:149
  72.2 3.4 %bitcast_convert_fusion = (bf16[4096,1,128]{0,2,1:T(8,128)(2,1)}, f32[128,4096,1]{1,0,2:T(8,128)}) fusion(f32[7,64]{1,0:T(8,128)S(1)} %fusion.4, f32[1,7,64,4096]{3,2,1,0:T(8,128)S(1)} %copy-done.4, f32[7,64]{1,0:T(8,128)S(1)} %get-tuple-element.113, f32[64]{0:T(128)S(1)} %get-tuple-element.50, pred[64]{0:T(512)(128)(4,1)S(1)} %iota_compare_fusion.1, ...), kind=kOutput, calls=%fused_computation.26 | convolution fusion | flops 476020736 | bytes 10604352 | tf_op jit(solution)/shard_map/while/body/eval_jaxpr/hgbk,bhgd->khd/dot_general | solution.py:146
  75.7 2.6 %fusion.6 = bf16[7,64,4096]{2,1,0:T(8,128)(2,1)S(1)} fusion(f32[4096,64,7]{0,1,2:T(8,128)S(1)} %get-tuple-element.118, f32[7,64]{1,0:T(8,128)S(1)} %get-tuple-element.117, f32[7,64]{1,0:T(8,128)S(1)} %fusion.4, f32[1,7,64,4096]{3,2,1,0:T(8,128)S(1)} %copy-done.4, f32[7,64]{1,0:T(8,128)S(1)} %get-tuple-element.113), kind=kLoop, calls=%fused_computation.20 | loop fusion | flops 9175040 | bytes 18355456 | tf_op jit(solution)/shard_map/reshape.54
  78.3 2.2 %bitcast_convert_fusion.1 = (bf16[4096,1,128]{0,2,1:T(8,128)(2,1)}, f32[128,4096]{1,0:T(8,128)S(1)}) fusion(bf16[7,64,4096]{2,1,0:T(8,128)(2,1)S(1)} %fusion.6, bf16[64,896]{1,0:T(8,128)(2,1)S(1)} %gather_fusion.4), kind=kOutput, calls=%fused_computation.27 | convolution fusion | flops 470810624 | bytes 6930432 | tf_op jit(solution)/shard_map/while/body/eval_jaxpr/hgbk,bhgd->khd/dot_general | solution.py:160
  80.5 2.3 %copy.42 = bf16[4096,1,128]{2,0,1:T(8,128)(2,1)} copy(bf16[4096,1,128]{0,2,1:T(8,128)(2,1)} %get-tuple-element.119) | data formatting | bytes 2097152 | tf_op jit(solution)/shard_map/convert.9
  82.8 2.3 %copy.41 = bf16[4096,1,128]{2,0,1:T(8,128)(2,1)} copy(bf16[4096,1,128]{0,2,1:T(8,128)(2,1)} %get-tuple-element.121) | data formatting | bytes 2097152 | tf_op jit(solution)/shard_map/convert.10
  85.1 2.5 %fusion.27 = bf16[4,4,2,64,256]{4,3,2,1,0:T(8,128)(2,1)} fusion(bf16[2,4,4,2,64,128]{5,4,3,2,1,0:T(8,128)(2,1)} %bitcast.202, bf16[2,4,4,2,64,128]{5,4,3,2,1,0:T(8,128)(2,1)} %bitcast.203), kind=kLoop, calls=%fused_computation.40 | loop fusion | flops 2097152 | bytes 3145728 | tf_op jit(solution)/shard_map/squeeze | solution.py:72
  87.6 1.5 %pad_maximum_fusion = f32[2048,256]{0,1:T(8,128)} fusion(f32[4096,128]{0,1:T(8,128)S(1)} %bitcast.204, f32[4096,128]{0,1:T(8,128)S(1)} %bitcast.200), kind=kLoop, calls=%fused_computation.25 | loop fusion | flops 524288 | bytes 6291456 | tf_op jit(solution)/shard_map/concatenate | solution.py:184
  89.1 1.9 %copy.40 = f32[2048,256]{1,0:T(8,128)S(1)} copy(f32[2048,256]{0,1:T(8,128)} %pad_maximum_fusion) | data formatting | bytes 4194304 | tf_op jit(solution)/shard_map/slice | solution.py:72
  91.0 1.6 %fusion.83 = (bf16[4,4,2,64,256]{4,3,2,1,0:T(8,128)(2,1)S(1)}, f32[4,4,2,64,256]{4,3,2,1,0:T(8,128)S(1)}) fusion(f32[4,4,2,64,256]{4,3,2,1,0:T(8,128)S(1)} %bitcast.201, bf16[4,4,2,64,256]{4,3,2,1,0:T(8,128)(2,1)} %collective-permute-done.8), kind=kLoop, calls=%fused_computation.169 | loop fusion | flops 1572864 | bytes 6291456 | tf_op jit(solution)/shard_map/convert_element_type | solution.py:71
  92.7 1.2 collective-permute-start.11
  93.9 2.3 %collective-permute-start.10 = (bf16[4,2,64,256]{3,2,1,0:T(8,128)(2,1)S(1)}, bf16[4,2,64,256]{3,2,1,0:T(8,128)(2,1)S(1)}, u32[]{:S(2)}, u32[]{:S(2)}) collective-permute-start(bf16[4,2,64,256]{3,2,1,0:T(8,128)(2,1)S(1)} %get-tuple-element.72), channel_id=1, source_target_pairs={{0,128},{4,132},{8,136},{12,140},{16,144},{20,148},{24,152},{28,15... | collective-permute-start | bytes 786440 | tf_op jit(solution)/shard_map/ppermute | solution.py:21
  97.3 1.2 collective-permute-done.16
  98.5 1.6 %collective-permute-start.19 = (f32[1792]{0:T(1024)S(1)}, f32[1792]{0:T(1024)S(1)}, u32[]{:S(2)}, u32[]{:S(2)}) collective-permute-start(f32[1792]{0:T(1024)S(1)} %add.272), channel_id=1, source_target_pairs={{0,192},{4,196},{8,200},{12,204},{16,208},{20,212},{24,216},{28,22... | collective-permute-start | bytes 21512 | tf_op jit(solution)/shard_map/ppermute | solution.py:21
  100.5 9.2 %collective-permute-done.19 = f32[1792]{0:T(1024)S(1)} collective-permute-done((f32[1792]{0:T(1024)S(1)}, f32[1792]{0:T(1024)S(1)}, u32[]{:S(2)}, u32[]{:S(2)}) %collective-permute-start.19) | collective-permute-done | bytes 7200 | tf_op jit(solution)/shard_map/ppermute | solution.py:21
  109.7 2.3 %collective-permute-start.18 = (f32[1792]{0:T(1024)S(1)}, f32[1792]{0:T(1024)S(1)}, u32[]{:S(2)}, u32[]{:S(2)}) collective-permute-start(f32[1792]{0:T(1024)S(1)} %add.272), channel_id=1, source_target_pairs={{0,128},{4,132},{8,136},{12,140},{16,144},{20,148},{24,152},{28,15... | collective-permute-start | bytes 21512 | tf_op jit(solution)/shard_map/ppermute | solution.py:21
  112.0 2.8 %collective-permute-done.18 = f32[1792]{0:T(1024)S(1)} collective-permute-done((f32[1792]{0:T(1024)S(1)}, f32[1792]{0:T(1024)S(1)}, u32[]{:S(2)}, u32[]{:S(2)}) %collective-permute-start.18) | collective-permute-done | bytes 7200 | tf_op jit(solution)/shard_map/ppermute | solution.py:21
  115.6 2.2 %collective-permute-start.14 = (bf16[2,64,256]{2,1,0:T(8,128)(2,1)S(1)}, bf16[2,64,256]{2,1,0:T(8,128)(2,1)S(1)}, u32[]{:S(2)}, u32[]{:S(2)}) collective-permute-start(bf16[2,64,256]{2,1,0:T(8,128)(2,1)S(1)} %get-tuple-element.74), channel_id=1, source_target_pairs={{0,16},{4,20},{8,24},{12,28},{16,32},{20,36},{24,40},{28,44},{32,4... | collective-permute-start | bytes 196616 | tf_op jit(solution)/shard_map/ppermute | solution.py:21
  117.8 3.8 %collective-permute-start.13 = (bf16[2,64,256]{2,1,0:T(8,128)(2,1)S(1)}, bf16[2,64,256]{2,1,0:T(8,128)(2,1)S(1)}, u32[]{:S(2)}, u32[]{:S(2)}) collective-permute-start(bf16[2,64,256]{2,1,0:T(8,128)(2,1)S(1)} %get-tuple-element.75), channel_id=1, source_target_pairs={{0,32},{4,36},{8,40},{12,44},{16,48},{20,52},{24,56},{28,60},{32,0... | collective-permute-start | bytes 196616 | tf_op jit(solution)/shard_map/ppermute | solution.py:21
  121.5 2.4 %collective-permute-start.12 = (bf16[2,64,256]{2,1,0:T(8,128)(2,1)S(1)}, bf16[2,64,256]{2,1,0:T(8,128)(2,1)S(1)}, u32[]{:S(2)}, u32[]{:S(2)}) collective-permute-start(bf16[2,64,256]{2,1,0:T(8,128)(2,1)S(1)} %get-tuple-element.73), channel_id=1, source_target_pairs={{0,48},{4,52},{8,56},{12,60},{16,0},{20,4},{24,8},{28,12},{32,16},... | collective-permute-start | bytes 196616 | tf_op jit(solution)/shard_map/ppermute | solution.py:21
  123.9 2.3 %fusion.26 = bf16[64,1,7,128]{3,0,2,1:T(8,128)(2,1)S(1)} fusion(bf16[7,64,4096]{2,1,0:T(8,128)(2,1)S(1)} %copy-done.2, bf16[4096,256]{1,0:T(8,128)(2,1)} %constant_dynamic-update-slice_fusion.15), kind=kOutput, calls=%fused_computation.37 | convolution fusion | flops 469876736 | bytes 4833280 | tf_op jit(solution)/shard_map/while/body/eval_jaxpr/hgbk,khd->bhgd/dot_general | solution.py:155
  126.5 1.8 %scatter_custom_fusion = bf16[256,896]{1,0:T(8,128)(2,1)} fusion(s32[64]{0:T(128)S(1)} %fusion.75, bf16[]{:T(256)} %constant.163.clone.1, f32[8,8,7,128]{3,2,1,0:T(8,128)S(1)} %bitcast.205, f32[64]{0:T(128)S(1)} %get-tuple-element.50, pred[64]{0:T(512)(128)(4,1)S(1)} %iota_compare_fusion.1), kind=kCustom, calls=%fused_computation.62 | custom fusion | flops 172032 | bytes 722944 | tf_op jit(solution)/shard_map/scatter | solution.py:240
  128.3 1.7 %scatter_custom_fusion.1 = bf16[256,896]{1,0:T(8,128)(2,1)} fusion(s32[64]{0:T(128)S(1)} %fusion.75, bf16[]{:T(256)} %constant.163.clone.1, bf16[8,8,7,128]{3,2,1,0:T(8,128)(2,1)S(1)} %bitcast.206, pred[64]{0:T(512)(128)(4,1)S(1)} %iota_compare_fusion.1), kind=kCustom, calls=%fused_computation.60 | custom fusion | flops 57344 | bytes 591360 | tf_op jit(solution)/shard_map/scatter | solution.py:245
  130.4 2.5 %collective-permute-start.21 = (f32[1792]{0:T(1024)S(1)}, f32[1792]{0:T(1024)S(1)}, u32[]{:S(2)}, u32[]{:S(2)}) collective-permute-start(f32[1792]{0:T(1024)S(1)} %add.276), channel_id=1, source_target_pairs={{0,16},{4,20},{8,24},{12,28},{16,32},{20,36},{24,40},{28,44},{32,4... | collective-permute-start | bytes 21512 | tf_op jit(solution)/shard_map/ppermute | solution.py:21
  132.9 1.8 %collective-permute-start.22 = (f32[1792]{0:T(1024)S(1)}, f32[1792]{0:T(1024)S(1)}, u32[]{:S(2)}, u32[]{:S(2)}) collective-permute-start(f32[1792]{0:T(1024)S(1)} %add.276), channel_id=1, source_target_pairs={{0,32},{4,36},{8,40},{12,44},{16,48},{20,52},{24,56},{28,60},{32,0... | collective-permute-start | bytes 21512 | tf_op jit(solution)/shard_map/ppermute | solution.py:21
  134.8 1.5 %collective-permute-start.15 = (bf16[64,256]{1,0:T(8,128)(2,1)S(1)}, bf16[64,256]{1,0:T(8,128)(2,1)S(1)}, u32[]{:S(2)}, u32[]{:S(2)}) collective-permute-start(bf16[64,256]{1,0:T(8,128)(2,1)S(1)} %fusion.58), channel_id=1, source_target_pairs={{0,8},{4,12},{8,0},{12,4},{16,24},{20,28},{24,16},{28,20},{32,40},... | collective-permute-start | bytes 98312 | tf_op jit(solution)/shard_map/ppermute | solution.py:21
  136.4 4.1 %collective-permute-done.22 = f32[1792]{0:T(1024)S(1)} collective-permute-done((f32[1792]{0:T(1024)S(1)}, f32[1792]{0:T(1024)S(1)}, u32[]{:S(2)}, u32[]{:S(2)}) %collective-permute-start.22) | collective-permute-done | bytes 7200 | tf_op jit(solution)/shard_map/ppermute | solution.py:21
  141.3 2.5 %scatter_fusion = bf16[256,2,128]{2,1,0:T(2,128)(2,1)S(1)} fusion(bf16[256,2,128]{2,1,0:T(2,128)(2,1)S(1)} %broadcast_in_dim.123, s32[64]{0:T(128)S(1)} %fusion.75, bf16[64,2,128]{2,1,0:T(2,128)(2,1)S(1)} %reshape.668), kind=kCustom, calls=%fused_computation.8 | custom fusion | bytes 98560 | tf_op jit(solution)/shard_map/scatter | solution.py:248
  (89 shorter events, 19.2 us)
Async XLA Ops:
  0.6 43.3 %copy-start = (bf16[256,1792]{1,0:T(8,128)(2,1)S(1)}, bf16[256,1792]{1,0:T(8,128)(2,1)}, u32[]{:S(2)}) copy-start(bf16[256,1792]{1,0:T(8,128)(2,1)} %param.7) | copy-start | bytes 2752516
  3.0 5.7 %collective-permute-start = (bf16[64,256]{1,0:T(8,128)(2,1)S(1)}, bf16[64,256]{1,0:T(8,128)(2,1)S(1)}, u32[]{:S(2)}, u32[]{:S(2)}) collective-permute-start(bf16[64,256]{1,0:T(8,128)(2,1)S(1)} %bitcast.209), channel_id=1, source_target_pairs={{0,8},{4,12},{8,0},{12,4},{16,24},{20,28},{24,16},{28,20},{32,40},... | collective-permute-start | bytes 98312 | tf_op jit(solution)/shard_map/ppermute | solution.py:21
  7.9 34.2 %copy-start.6 = (bf16[256,896]{1,0:T(8,128)(2,1)S(1)}, bf16[256,896]{1,0:T(8,128)(2,1)}, u32[]{:S(2)}) copy-start(bf16[256,896]{1,0:T(8,128)(2,1)} %param.11) | copy-start | bytes 1376260
  9.4 12.0 %collective-permute-start.1 = (bf16[128,256]{1,0:T(8,128)(2,1)S(1)}, bf16[128,256]{1,0:T(8,128)(2,1)S(1)}, u32[]{:S(2)}, u32[]{:S(2)}) collective-permute-start(bf16[128,256]{1,0:T(8,128)(2,1)S(1)} %get-tuple-element.107), channel_id=1, source_target_pairs={{0,16},{4,20},{8,24},{12,28},{16,32},{20,36},{24,40},{28,44},{32,4... | collective-permute-start | bytes 196616 | tf_op jit(solution)/shard_map/ppermute | solution.py:21
  14.1 9.0 %collective-permute-start.2 = (bf16[128,256]{1,0:T(8,128)(2,1)S(1)}, bf16[128,256]{1,0:T(8,128)(2,1)S(1)}, u32[]{:S(2)}, u32[]{:S(2)}) collective-permute-start(bf16[128,256]{1,0:T(8,128)(2,1)S(1)} %get-tuple-element.107), channel_id=1, source_target_pairs={{0,32},{4,36},{8,40},{12,44},{16,48},{20,52},{24,56},{28,60},{32,0... | collective-permute-start | bytes 196616 | tf_op jit(solution)/shard_map/ppermute | solution.py:21
  18.7 6.3 %collective-permute-start.3 = (bf16[128,256]{1,0:T(8,128)(2,1)S(1)}, bf16[128,256]{1,0:T(8,128)(2,1)S(1)}, u32[]{:S(2)}, u32[]{:S(2)}) collective-permute-start(bf16[128,256]{1,0:T(8,128)(2,1)S(1)} %get-tuple-element.107), channel_id=1, source_target_pairs={{0,48},{4,52},{8,56},{12,60},{16,0},{20,4},{24,8},{28,12},{32,16},... | collective-permute-start | bytes 196616 | tf_op jit(solution)/shard_map/ppermute | solution.py:21
  23.8 19.4 %copy-start.7 = (bf16[256,896]{1,0:T(8,128)(2,1)S(1)}, bf16[256,896]{1,0:T(8,128)(2,1)}, u32[]{:S(2)}) copy-start(bf16[256,896]{1,0:T(8,128)(2,1)} %param.9) | copy-start | bytes 1376260
  25.7 9.2 %collective-permute-start.4 = (bf16[512,256]{1,0:T(8,128)(2,1)S(1)}, bf16[512,256]{1,0:T(8,128)(2,1)S(1)}, u32[]{:S(2)}, u32[]{:S(2)}) collective-permute-start(bf16[512,256]{1,0:T(8,128)(2,1)S(1)} %get-tuple-element.97), channel_id=1, source_target_pairs={{0,64},{4,68},{8,72},{12,76},{16,80},{20,84},{24,88},{28,92},{32,9... | collective-permute-start | bytes 786440 | tf_op jit(solution)/shard_map/ppermute | solution.py:21
  27.2 10.6 %collective-permute-start.5 = (bf16[512,256]{1,0:T(8,128)(2,1)S(1)}, bf16[512,256]{1,0:T(8,128)(2,1)S(1)}, u32[]{:S(2)}, u32[]{:S(2)}) collective-permute-start(bf16[512,256]{1,0:T(8,128)(2,1)S(1)} %get-tuple-element.97), channel_id=1, source_target_pairs={{0,128},{4,132},{8,136},{12,140},{16,144},{20,148},{24,152},{28,15... | collective-permute-start | bytes 786440 | tf_op jit(solution)/shard_map/ppermute | solution.py:21
  28.4 11.7 %collective-permute-start.6 = (bf16[512,256]{1,0:T(8,128)(2,1)S(1)}, bf16[512,256]{1,0:T(8,128)(2,1)S(1)}, u32[]{:S(2)}, u32[]{:S(2)}) collective-permute-start(bf16[512,256]{1,0:T(8,128)(2,1)S(1)} %get-tuple-element.97), channel_id=1, source_target_pairs={{0,192},{4,196},{8,200},{12,204},{16,208},{20,212},{24,216},{28,22... | collective-permute-start | bytes 786440 | tf_op jit(solution)/shard_map/ppermute | solution.py:21
  40.9 4.3 %collective-permute-start.7 = (bf16[2048,256]{1,0:T(8,128)(2,1)}, bf16[2048,256]{1,0:T(8,128)(2,1)S(1)}, u32[]{:S(2)}, u32[]{:S(2)}) collective-permute-start(bf16[2048,256]{1,0:T(8,128)(2,1)} %get-tuple-element.76), channel_id=1, source_target_pairs={{0,4},{4,0},{8,12},{12,8},{16,20},{20,16},{24,28},{28,24},{32,36},... | collective-permute-start | bytes 3145736 | tf_op jit(solution)/shard_map/ppermute | solution.py:21
  42.2 2.5 %copy-start.10 = (bf16[1792]{0:T(1024)(128)(2,1)S(1)}, bf16[1792]{0:T(1024)(128)(2,1)}, u32[]{:S(2)}) copy-start(bf16[1792]{0:T(1024)(128)(2,1)} %param.8) | copy-start | bytes 10756
  48.8 3.0 %copy-start.3 = (f32[1,7,64,4096]{3,2,1,0:T(8,128)}, f32[1,7,64,4096]{3,2,1,0:T(8,128)S(1)}, u32[]{:S(2)}) copy-start(f32[1,7,64,4096]{3,2,1,0:T(8,128)S(1)} %get-tuple-element.114) | copy-start | bytes 22020100
  66.7 5.5 %copy-start.4 = (f32[1,7,64,4096]{3,2,1,0:T(8,128)S(1)}, f32[1,7,64,4096]{3,2,1,0:T(8,128)}, u32[]{:S(2)}) copy-start(f32[1,7,64,4096]{3,2,1,0:T(8,128)} %copy-done.3) | copy-start | bytes 22020100
  78.3 2.2 %copy-start.1 = (bf16[7,64,4096]{2,1,0:T(8,128)(2,1)}, bf16[7,64,4096]{2,1,0:T(8,128)(2,1)S(1)}, u32[]{:S(2)}) copy-start(bf16[7,64,4096]{2,1,0:T(8,128)(2,1)S(1)} %fusion.6) | copy-start | bytes 11010052
  85.1 2.6 %copy-start.5 = (f32[128,4096,1]{1,0,2:T(8,128)S(1)}, f32[128,4096,1]{1,0,2:T(8,128)}, u32[]{:S(2)}) copy-start(f32[128,4096,1]{1,0,2:T(8,128)} %get-tuple-element.120) | copy-start | bytes 6291460
  87.6 3.4 %collective-permute-start.8 = (bf16[4,4,2,64,256]{4,3,2,1,0:T(8,128)(2,1)}, bf16[4,4,2,64,256]{4,3,2,1,0:T(8,128)(2,1)}, u32[]{:S(2)}, u32[]{:S(2)}) collective-permute-start(bf16[4,4,2,64,256]{4,3,2,1,0:T(8,128)(2,1)} %fusion.27), channel_id=1, source_target_pairs={{0,4},{4,0},{8,12},{12,8},{16,20},{20,16},{24,28},{28,24},{32,36},... | collective-permute-start | bytes 3145736 | tf_op jit(solution)/shard_map/ppermute | solution.py:21
  92.6 31.3 %copy-start.2 = (bf16[7,64,4096]{2,1,0:T(8,128)(2,1)S(1)}, bf16[7,64,4096]{2,1,0:T(8,128)(2,1)}, u32[]{:S(2)}) copy-start(bf16[7,64,4096]{2,1,0:T(8,128)(2,1)} %copy-done.1) | copy-start | bytes 11010052
  92.7 22.7 %collective-permute-start.11 = (bf16[4,2,64,256]{3,2,1,0:T(8,128)(2,1)S(1)}, bf16[4,2,64,256]{3,2,1,0:T(8,128)(2,1)S(1)}, u32[]{:S(2)}, u32[]{:S(2)}) collective-permute-start(bf16[4,2,64,256]{3,2,1,0:T(8,128)(2,1)S(1)} %get-tuple-element.71), channel_id=1, source_target_pairs={{0,64},{4,68},{8,72},{12,76},{16,80},{20,84},{24,88},{28,92},{32,9... | collective-permute-start | bytes 786440 | tf_op jit(solution)/shard_map/ppermute | solution.py:21
  93.9 21.5 %collective-permute-start.10 = (bf16[4,2,64,256]{3,2,1,0:T(8,128)(2,1)S(1)}, bf16[4,2,64,256]{3,2,1,0:T(8,128)(2,1)S(1)}, u32[]{:S(2)}, u32[]{:S(2)}) collective-permute-start(bf16[4,2,64,256]{3,2,1,0:T(8,128)(2,1)S(1)} %get-tuple-element.72), channel_id=1, source_target_pairs={{0,128},{4,132},{8,136},{12,140},{16,144},{20,148},{24,152},{28,15... | collective-permute-start | bytes 786440 | tf_op jit(solution)/shard_map/ppermute | solution.py:21
  96.2 19.2 %collective-permute-start.9 = (bf16[4,2,64,256]{3,2,1,0:T(8,128)(2,1)S(1)}, bf16[4,2,64,256]{3,2,1,0:T(8,128)(2,1)S(1)}, u32[]{:S(2)}, u32[]{:S(2)}) collective-permute-start(bf16[4,2,64,256]{3,2,1,0:T(8,128)(2,1)S(1)} %get-tuple-element.70), channel_id=1, source_target_pairs={{0,192},{4,196},{8,200},{12,204},{16,208},{20,212},{24,216},{28,22... | collective-permute-start | bytes 786440 | tf_op jit(solution)/shard_map/ppermute | solution.py:21
  97.2 1.3 collective-permute-start.16
  98.5 11.2 %collective-permute-start.19 = (f32[1792]{0:T(1024)S(1)}, f32[1792]{0:T(1024)S(1)}, u32[]{:S(2)}, u32[]{:S(2)}) collective-permute-start(f32[1792]{0:T(1024)S(1)} %add.272), channel_id=1, source_target_pairs={{0,192},{4,196},{8,200},{12,204},{16,208},{20,212},{24,216},{28,22... | collective-permute-start | bytes 21512 | tf_op jit(solution)/shard_map/ppermute | solution.py:21
  100.0 12.0 %collective-permute-start.17 = (f32[1792]{0:T(1024)S(1)}, f32[1792]{0:T(1024)S(1)}, u32[]{:S(2)}, u32[]{:S(2)}) collective-permute-start(f32[1792]{0:T(1024)S(1)} %add.272), channel_id=1, source_target_pairs={{0,64},{4,68},{8,72},{12,76},{16,80},{20,84},{24,88},{28,92},{32,9... | collective-permute-start | bytes 21512 | tf_op jit(solution)/shard_map/ppermute | solution.py:21
  109.7 5.2 %collective-permute-start.18 = (f32[1792]{0:T(1024)S(1)}, f32[1792]{0:T(1024)S(1)}, u32[]{:S(2)}, u32[]{:S(2)}) collective-permute-start(f32[1792]{0:T(1024)S(1)} %add.272), channel_id=1, source_target_pairs={{0,128},{4,132},{8,136},{12,140},{16,144},{20,148},{24,152},{28,15... | collective-permute-start | bytes 21512 | tf_op jit(solution)/shard_map/ppermute | solution.py:21
  114.8 15.2 %collective-permute-start.20 = (f32[1792]{0:T(1024)S(1)}, f32[1792]{0:T(1024)S(1)}, u32[]{:S(2)}, u32[]{:S(2)}) collective-permute-start(f32[1792]{0:T(1024)S(1)} %add_add_fusion.1), channel_id=1, source_target_pairs={{0,8},{4,12},{8,0},{12,4},{16,24},{20,28},{24,16},{28,20},{32,40},... | collective-permute-start | bytes 21512 | tf_op jit(solution)/shard_map/ppermute | solution.py:21
  115.6 17.4 %collective-permute-start.14 = (bf16[2,64,256]{2,1,0:T(8,128)(2,1)S(1)}, bf16[2,64,256]{2,1,0:T(8,128)(2,1)S(1)}, u32[]{:S(2)}, u32[]{:S(2)}) collective-permute-start(bf16[2,64,256]{2,1,0:T(8,128)(2,1)S(1)} %get-tuple-element.74), channel_id=1, source_target_pairs={{0,16},{4,20},{8,24},{12,28},{16,32},{20,36},{24,40},{28,44},{32,4... | collective-permute-start | bytes 196616 | tf_op jit(solution)/shard_map/ppermute | solution.py:21
  117.8 17.0 %collective-permute-start.13 = (bf16[2,64,256]{2,1,0:T(8,128)(2,1)S(1)}, bf16[2,64,256]{2,1,0:T(8,128)(2,1)S(1)}, u32[]{:S(2)}, u32[]{:S(2)}) collective-permute-start(bf16[2,64,256]{2,1,0:T(8,128)(2,1)S(1)} %get-tuple-element.75), channel_id=1, source_target_pairs={{0,32},{4,36},{8,40},{12,44},{16,48},{20,52},{24,56},{28,60},{32,0... | collective-permute-start | bytes 196616 | tf_op jit(solution)/shard_map/ppermute | solution.py:21
  121.5 4.7 %copy-start.8 = (f32[64,1,7,128]{3,0,2,1:T(8,128)S(1)}, f32[64,1,7,128]{3,0,2,1:T(8,128)}, u32[]{:S(2)}) copy-start(f32[64,1,7,128]{3,0,2,1:T(8,128)} %get-tuple-element.116) | copy-start | bytes 688132
  121.5 13.2 %collective-permute-start.12 = (bf16[2,64,256]{2,1,0:T(8,128)(2,1)S(1)}, bf16[2,64,256]{2,1,0:T(8,128)(2,1)S(1)}, u32[]{:S(2)}, u32[]{:S(2)}) collective-permute-start(bf16[2,64,256]{2,1,0:T(8,128)(2,1)S(1)} %get-tuple-element.73), channel_id=1, source_target_pairs={{0,48},{4,52},{8,56},{12,60},{16,0},{20,4},{24,8},{28,12},{32,16},... | collective-permute-start | bytes 196616 | tf_op jit(solution)/shard_map/ppermute | solution.py:21
  130.0 6.3 %collective-permute-start.23 = (f32[1792]{0:T(1024)S(1)}, f32[1792]{0:T(1024)S(1)}, u32[]{:S(2)}, u32[]{:S(2)}) collective-permute-start(f32[1792]{0:T(1024)S(1)} %add.276), channel_id=1, source_target_pairs={{0,48},{4,52},{8,56},{12,60},{16,0},{20,4},{24,8},{28,12},{32,16},... | collective-permute-start | bytes 21512 | tf_op jit(solution)/shard_map/ppermute | solution.py:21
  130.4 6.0 %collective-permute-start.21 = (f32[1792]{0:T(1024)S(1)}, f32[1792]{0:T(1024)S(1)}, u32[]{:S(2)}, u32[]{:S(2)}) collective-permute-start(f32[1792]{0:T(1024)S(1)} %add.276), channel_id=1, source_target_pairs={{0,16},{4,20},{8,24},{12,28},{16,32},{20,36},{24,40},{28,44},{32,4... | collective-permute-start | bytes 21512 | tf_op jit(solution)/shard_map/ppermute | solution.py:21
  132.9 7.6 %collective-permute-start.22 = (f32[1792]{0:T(1024)S(1)}, f32[1792]{0:T(1024)S(1)}, u32[]{:S(2)}, u32[]{:S(2)}) collective-permute-start(f32[1792]{0:T(1024)S(1)} %add.276), channel_id=1, source_target_pairs={{0,32},{4,36},{8,40},{12,44},{16,48},{20,52},{24,56},{28,60},{32,0... | collective-permute-start | bytes 21512 | tf_op jit(solution)/shard_map/ppermute | solution.py:21
  134.8 6.3 %collective-permute-start.15 = (bf16[64,256]{1,0:T(8,128)(2,1)S(1)}, bf16[64,256]{1,0:T(8,128)(2,1)S(1)}, u32[]{:S(2)}, u32[]{:S(2)}) collective-permute-start(bf16[64,256]{1,0:T(8,128)(2,1)S(1)} %fusion.58), channel_id=1, source_target_pairs={{0,8},{4,12},{8,0},{12,4},{16,24},{20,28},{24,16},{28,20},{32,40},... | collective-permute-start | bytes 98312 | tf_op jit(solution)/shard_map/ppermute | solution.py:21
  143.8 0.7 copy-start.9

commit v2 on v0

v2 whole, which is shorter than its diff:
```python
import functools
import math

import jax
import jax.numpy as jnp
from jax import lax
from jax.experimental import pallas as pl
from jax.experimental.pallas import tpu as pltpu
from jax.sharding import PartitionSpec as P

HEAD_SIZE = 128
NX, NZ = 4, 8
SLOTS = 64
PAIR = 2 * SLOTS
CHUNK = NZ * SLOTS
SUB = 128
TILE = 16
SCALE = HEAD_SIZE ** -0.5
SCALE2 = SCALE * math.log2(math.e)
MASKED = -1e30
FLOPS_PER_US, BYTES_PER_US = 1153.5e6, 3.69e6
F32, BF16 = jnp.float32, jnp.bfloat16
VMEM = pl.BlockSpec(memory_space=pltpu.VMEM)
SMEM = pl.BlockSpec(memory_space=pltpu.SMEM)
ANY = pl.BlockSpec(memory_space=pl.ANY)


def shard_of(x, z, c):
    return (x * NZ + z) * 2 + c


def move(value, target):
    pairs = []
    for x in range(NX):
        for z in range(NZ):
            for c in range(2):
                place = target(x, z, c)
                if place is not None:
                    pairs.append((shard_of(x, z, c), shard_of(*place)))
    return lax.ppermute(value, "ctx", pairs)


def up_x(k):
    return lambda x, z, c: (x + k, z, c) if x + k < NX else None


def down_x(k):
    return lambda x, z, c: (x - k, z, c) if x >= k else None


def flip_x(bit):
    return lambda x, z, c: (x ^ bit, z, c)


def by_z(k):
    return lambda x, z, c: (x, (z + k) % NZ, c)


def flip_z(x, z, c):
    return (x, z ^ 1, c)


def flip_core(x, z, c):
    return (x, z, c ^ 1)


def flip_tp(value, bit):
    return lax.ppermute(value, "tp", [(i, i ^ bit) for i in range(4)])


def sum_over_tp(value):
    value = value + flip_tp(value, 1)
    return value + flip_tp(value, 2)


def call(kernel, outs, *args, specs=None, scratch=(), after=(), us=0.05):
    skip = len(after)

    def body(*refs):
        kernel(*refs[skip:])

    return pl.pallas_call(
        body,
        out_shape=outs,
        in_specs=[ANY] * skip + list(specs or [VMEM] * len(args)),
        out_specs=jax.tree.map(lambda _: VMEM, outs),
        scratch_shapes=list(scratch),
        compiler_params=pltpu.CompilerParams(vmem_limit_bytes=48 * 1024 * 1024),
        cost_estimate=pl.CostEstimate(
            flops=int(us * FLOPS_PER_US), bytes_accessed=int(us * BYTES_PER_US), transcendentals=0
        ),
    )(*after, *args)


def shape(dims, dtype):
    return jax.ShapeDtypeStruct(dims, dtype)


def dot_tn(a, b):
    return lax.dot_general(a, b, (((0,), (0,)), ((), ())), preferred_element_type=F32)


def dot_nt(a, b):
    return lax.dot_general(a, b, (((1,), (1,)), ((), ())), preferred_element_type=F32)


def dot(a, b):
    return jnp.dot(a, b, preferred_element_type=F32)


def one_hot(chosen_row, tokens, live=None):
    rows = lax.broadcasted_iota(jnp.int32, (tokens, SLOTS), 0)
    hit = rows == chosen_row
    if live is not None:
        hit = hit & (lax.broadcasted_iota(jnp.int32, (tokens, SLOTS), 1) < live)
    return jnp.where(hit, 1.0, 0.0).astype(BF16)


def half_mask(offset):
    i = lax.broadcasted_iota(jnp.int32, (SLOTS, PAIR), 0)
    j = lax.broadcasted_iota(jnp.int32, (SLOTS, PAIR), 1)
    return j == i + offset


def own_column(row, place):
    mine = half_mask((place[0] % 2) * SLOTS)
    return jnp.sum(jnp.where(mine, row, 0.0), axis=1, keepdims=True)


def pair_hot(chosen, tokens, live=SLOTS):
    both = jnp.concatenate([chosen[...], chosen[...]], axis=1)
    lane = lax.broadcasted_iota(jnp.int32, (1, PAIR), 1)
    second = lane >= SLOTS
    target = both * 2 + jnp.where(second, 1, 0)
    slot = lane - jnp.where(second, SLOTS, 0)
    target = jnp.where(slot < live, target, -1)
    rows = lax.broadcasted_iota(jnp.int32, (2 * tokens, PAIR), 0)
    return jnp.where(rows == target, 1.0, 0.0).astype(BF16)


def pick_pairs_kernel(chosen, pairs, rows):
    picked = dot_tn(pair_hot(chosen, pairs.shape[0] // 2), pairs[...]).astype(BF16)
    rows[:, :HEAD_SIZE] = picked[:SLOTS, :]
    rows[:, HEAD_SIZE:] = picked[SLOTS:, :]


def pick_rows_kernel(place, chosen, queries, grads, tokens, weight, qg_rows, t_rows, logit):
    hot = one_hot(chosen[...], queries.shape[0])
    width = queries.shape[1]
    qg_rows[:, :width] = dot_tn(hot, queries[...]).astype(BF16)
    qg_rows[:, width:] = dot_tn(hot, grads[...]).astype(BF16)
    picked = dot_tn(hot, tokens[...]).astype(BF16)
    t_rows[...] = picked
    terms = picked.astype(F32) * weight[...].astype(F32)
    column = jnp.sum(terms, axis=1, keepdims=True)
    mine = half_mask((place[0] % 2) * SLOTS)
    logit[...] = jnp.sum(jnp.where(mine, column, 0.0), axis=0, keepdims=True)


def prepare_kernel(place, own, other, logit, logit_other, qt, qs, gt, logit_sum):
    logit_sum[...] = logit[...] + logit_other[...]
    first = place[0] % 2 == 0
    lanes = qt.shape[1]
    for h in range(own.shape[1] // HEAD_SIZE):
        cols = slice(h * HEAD_SIZE, (h + 1) * HEAD_SIZE)
        mine, theirs = own[:, cols].astype(F32), other[:, cols].astype(F32)
        both = jnp.where(
            first,
            jnp.concatenate([mine, theirs], axis=0),
            jnp.concatenate([theirs, mine], axis=0),
        )
        at = h * PAIR
        if at < lanes:
            qs[at : at + PAIR, :] = both.astype(BF16)
            qt[:, at : at + PAIR] = both.T.astype(BF16)
        else:
            gt[:, at - lanes : at - lanes + PAIR] = both.T.astype(BF16)


def gate_kernel(place, counts, logit, logit_other, gt, gate, dt, ds):
    value = jax.nn.sigmoid(logit[...] + logit_other[...])
    gate[...] = value
    lane = lax.broadcasted_iota(jnp.int32, value.shape, 1)
    chip = place[0] - place[0] % 2
    live = (lane < counts[chip]) | ((lane >= SLOTS) & (lane < SLOTS + counts[chip + 1]))
    live = jnp.broadcast_to(live, (HEAD_SIZE, PAIR))
    for h in range(gt.shape[1] // PAIR):
        cols = slice(h * PAIR, (h + 1) * PAIR)
        scaled = jnp.where(live, gt[:, cols].astype(F32) * value, 0.0)
        dt[:, cols] = scaled.astype(BF16)
        ds[cols, :] = scaled.T.astype(BF16)


def join_sum_kernel(a, b, *refs):
    *refs, total = refs
    total[...] = a[...] + b[...]
    join_kernel(*refs)


def join_kernel(*refs):
    *parts, out = refs
    at = 0
    for part in parts:
        out[at : at + part.shape[0], :] = part[...]
        at += part.shape[0]


def block_plan(place, counts, shift):
    shard = place[0]
    core, chip = shard % 2, shard // 2
    z, x = chip % NZ, chip // NZ
    from_x = (x - shift + NX) % NX
    plan, first = [], jnp.int32(0)
    for j in range(NZ):
        from_z = (((z + (j % 2) * (1 - 2 * (z % 2))) - 2 * (j // 2)) + NZ) % NZ
        from_chip = from_x * NZ + from_z
        live = counts[from_chip * 2 + core]
        ahead = (chip - from_chip) * PAIR - core * SLOTS
        tiles = jnp.where(from_chip <= chip, (live + TILE - 1) // TILE, 0)
        plan.append((live, ahead, tiles, first))
        first = first + tiles
    return plan, first


def pack_rows(plan, pairs, packed, bias):
    packed[...] = jnp.zeros_like(packed)
    bias[...] = jnp.full_like(bias, MASKED)
    slot = lax.broadcasted_iota(jnp.int32, (SLOTS, PAIR), 0)
    lane = lax.broadcasted_iota(jnp.int32, (SLOTS, PAIR), 1)
    for j, (live, ahead, _, first) in enumerate(plan):
        at = pl.ds(pl.multiple_of(first * TILE, TILE), SLOTS)
        packed[at, :] = pairs[j * SLOTS : (j + 1) * SLOTS, :]
        seen = (slot < live) & (slot <= lane + ahead)
        bias[at, :] = jnp.where(seen, 0.0, MASKED)


def scores_of(keys, qt, bias):
    raw = dot(keys, qt[...])
    heads = raw.shape[1] // PAIR
    return raw * SCALE2 + jnp.concatenate([bias] * heads, axis=1)


def forward_kernel(shift, last, place, counts, pairs, qt, *refs):
    if shift == 0:
        acc, stats, packed, bias = refs
        acc[...] = jnp.zeros_like(acc)
        row = lax.broadcasted_iota(jnp.int32, stats.shape, 0)
        stats[...] = jnp.where(row == 0, MASKED, 0.0)
    else:
        if last:
            dt, gt, *refs = refs
        acc_in, stats_in, acc, stats, packed, bias = refs
        acc[...] = acc_in[...]
        stats[...] = stats_in[...]
    plan, tiles = block_plan(place, counts, shift)

    @pl.when(tiles > 0)
    def _():
        pack_rows(plan, pairs, packed, bias)

        def step(i, carry):
            at = pl.ds(pl.multiple_of(i * SUB, SUB), SUB)
            scores = scores_of(packed[at, :HEAD_SIZE], qt, bias[at, :])
            old = stats[0:1, :]
            new = jnp.maximum(old, jnp.max(scores, axis=0, keepdims=True))
            decay = jnp.exp2(old - new)
            weights = jnp.exp2(scores - new)
            stats[0:1, :] = new
            stats[1:2, :] = stats[1:2, :] * decay + jnp.sum(weights, axis=0, keepdims=True)
            mixed = dot_tn(packed[at, HEAD_SIZE:], weights.astype(BF16))
            acc[...] = acc[...] * decay + mixed
            return carry

        lax.fori_loop(0, (tiles * TILE + SUB - 1) // SUB, step, 0)

    if last:
        stats[2:3, :] = jnp.sum(acc[...] * dt[...].astype(F32), axis=0, keepdims=True)
        stats[3:4, :] = jnp.sum(acc[...] * gt[...].astype(F32), axis=0, keepdims=True)


def merge_stats(ours, theirs):
    top = jnp.maximum(ours[0:1, :], theirs[0:1, :])
    a = jnp.exp2(ours[0:1, :] - top)
    b = jnp.exp2(theirs[0:1, :] - top)
    total = ours[1:2, :] * a + theirs[1:2, :] * b
    return top, a, b, total


def backward_kernel(
    shift, place, counts, pairs, qt, qs, dt, ds, ours, theirs, *refs
):
    if shift == 1:
        out, dq, packed, bias, grads = refs
        dq[...] = jnp.zeros_like(dq)
    else:
        if shift == 2:
            part, part_other, *refs = refs
        dq_in, out, dq, *refs = refs
        if shift == 2:
            part_sum, *refs = refs
            part_sum[...] = part[...] + part_other[...]
        packed, bias, grads = refs
        dq[...] = dq_in[...]
    plan, tiles = block_plan(place, counts, shift)
    used = tiles > 0

    @pl.when(used)
    def _():
        pack_rows(plan, pairs, packed, bias)
        top, a, b, total = merge_stats(ours, theirs)
        level = top + jnp.log2(total)
        delta = (ours[2:3, :] * a + theirs[2:3, :] * b) / total

        def step(i, carry):
            at = pl.ds(pl.multiple_of(i * SUB, SUB), SUB)
            keys, values = packed[at, :HEAD_SIZE], packed[at, HEAD_SIZE:]
            probs = jnp.exp2(scores_of(keys, qt, bias[at, :]) - level)
            d_probs = dot(values, dt[...])
            d_scores = (probs * (d_probs - delta)).astype(BF16)
            grads[at, HEAD_SIZE:] = dot(probs.astype(BF16), ds[...])
            grads[at, :HEAD_SIZE] = dot(d_scores, qs[...]) * SCALE
            dq[...] += dot_tn(keys, d_scores)
            return carry

        lax.fori_loop(0, (tiles * TILE + SUB - 1) // SUB, step, 0)
        for j, (_, _, count, first) in enumerate(plan):
            for i in range(SLOTS // TILE):
                at = pl.ds(pl.multiple_of((first + i) * TILE, TILE), TILE)
                piece = jnp.where(i < count, grads[at, :], 0.0)
                out[j * SLOTS + i * TILE : j * SLOTS + (i + 1) * TILE, :] = piece.astype(out.dtype)

    @pl.when(jnp.logical_not(used))
    def _():
        out[...] = jnp.zeros_like(out)


def gate_part_kernel(ours, theirs, part):
    top, a, b, total = merge_stats(ours, theirs)
    dots = (ours[3:4, :] * a + theirs[3:4, :] * b) / total
    part[...] = sum(
        dots[:, h * PAIR : (h + 1) * PAIR] for h in range(dots.shape[1] // PAIR)
    )


def attended_kernel(
    place, counts, chosen, ours, theirs, acc_ours, acc_theirs, gate, dq, routed, dq_own, dq_send
):
    top, a, b, total = merge_stats(ours, theirs)
    a, b = a / total, b / total
    first = place[0] % 2 == 0
    hot = one_hot(chosen[...], routed.shape[0], counts[place[0]])
    factor = own_column(gate[...], place)
    for h in range(acc_ours.shape[1] // PAIR):
        cols = slice(h * PAIR, (h + 1) * PAIR)
        mixed = (acc_ours[:, cols] * a[:, cols] + acc_theirs[:, cols] * b[:, cols]).T
        rows = jnp.where(first, mixed[:SLOTS, :], mixed[SLOTS:, :]).astype(BF16).astype(F32)
        routed[:, cols] = dot(hot, (rows * factor).astype(BF16)).astype(BF16)
        both = dq[:, cols].T
        dq_own[:, cols] = jnp.where(first, both[:SLOTS, :], both[SLOTS:, :])
        dq_send[:, cols] = jnp.where(first, both[SLOTS:, :], both[:SLOTS, :])


def queries_kernel(place, counts, chosen, own, other, out, ready):
    ready[...] = own[0:1, :PAIR]
    hot = one_hot(chosen[...], out.shape[0], counts[place[0]])
    rows = ((own[...] + other[...]) * SCALE).astype(BF16)
    out[...] = dot(hot, rows).astype(BF16)


def add_kernel(a, b, out):
    out[...] = a[...] + b[...]


def router_kernel(place, counts, d_gate, d_gate_other, gate, t_rows, out):
    value = own_column(gate[...], place)
    total = own_column(d_gate[...] + d_gate_other[...], place)
    slot = lax.broadcasted_iota(jnp.int32, (SLOTS, 1), 0)
    d_logit = jnp.where(slot < counts[place[0]], total * value * (1.0 - value), 0.0)
    terms = t_rows[...].astype(F32) * d_logit
    sums = jnp.sum(terms, axis=0, keepdims=True)
    width = out.shape[1]
    out[...] = jnp.zeros_like(out)
    for r in range(sums.shape[1] // width):
        out[r : r + 1, :] = sums[:, r * width : (r + 1) * width]


def put_sum(ref, at, total):
    high = total.astype(BF16)
    ref[at : at + TILE, :] = jnp.concatenate(
        [high.astype(F32), total - high.astype(F32)], axis=0
    ).astype(BF16)


def get_sum(ref, at):
    both = ref[at : at + TILE, :].astype(F32)
    return both[: TILE // 2, :] + both[TILE // 2 :, :]


def sum_x_kernel(own, a, b, c, r0, r1, keep, keep_sum, *sends):
    size = keep.shape[0]
    router = r0[...] + r1[...]
    keep_sum[...] = router
    for i in range(4):
        at = slice(i * size, (i + 1) * size)
        total = own[at, :] + a[at, :].astype(F32) + b[at, :].astype(F32) + c[at, :].astype(F32)
        if i == 0:
            keep[...] = total
        else:
            sends[i - 1][:size, :] = total.astype(BF16)
            put_sum(sends[i - 1], size, router)


def sum_z_kernel(own, own_sum, a, b, c, keep, keep_sum, send):
    size = keep.shape[0]
    full = own.shape[0]
    parts = [ref[:full, :].astype(F32) for ref in (a, b, c)]
    total = own[...] + parts[0] + parts[1] + parts[2]
    router = own_sum[...] + get_sum(a, full) + get_sum(b, full) + get_sum(c, full)
    keep_sum[...] = router
    keep[...] = total[:size, :]
    send[:size, :] = total[size:, :].astype(BF16)
    put_sum(send, size, router)


def last_sum_kernel(own_sum, a, out):
    out[...] = own_sum[...] + get_sum(a, SLOTS)


def pairs_kernel(place, counts, chosen, own, a, out):
    hot = pair_hot(chosen, out.shape[0] // 2, counts[place[0]])
    rows = own[...] + a[:SLOTS, :].astype(F32)
    rows = jnp.concatenate([rows[:, :HEAD_SIZE], rows[:, HEAD_SIZE:]], axis=0).astype(BF16)
    out[...] = dot(hot, rows).astype(BF16)


def on_device(tokens, router_weight, queries, keys_values, routed_grad, chosen, counts):
    place = lax.axis_index("ctx").astype(jnp.int32).reshape(1)
    count = tokens.shape[0]
    width = queries.shape[1]
    lanes = width // HEAD_SIZE * PAIR
    features = tokens.shape[1]
    pair_width = 2 * HEAD_SIZE
    scalars = [SMEM, SMEM]
    packed = [pltpu.VMEM((CHUNK, pair_width), BF16), pltpu.VMEM((CHUNK, PAIR), F32)]

    own_rows = call(
        pick_pairs_kernel,
        shape((SLOTS, pair_width), BF16),
        chosen,
        keys_values.reshape(2 * count, HEAD_SIZE),
        us=0.6,
    )

    pair_row = shape((1, PAIR), F32)
    two = call(
        join_kernel, shape((2 * SLOTS, pair_width), BF16), own_rows, move(own_rows, flip_z)
    )
    neighbours = [move(two, by_z(k)) for k in (2, 4, 6)]
    qg_rows, t_rows, logit = call(
        pick_rows_kernel,
        (shape((SLOTS, 2 * width), BF16), shape((SLOTS, features), BF16), pair_row),
        place,
        chosen,
        queries,
        routed_grad,
        tokens,
        router_weight.reshape(1, features),
        specs=[SMEM] + [VMEM] * 5,
        after=(two,),
        us=0.6,
    )
    turned, stacked = shape((HEAD_SIZE, lanes), BF16), shape((lanes, HEAD_SIZE), BF16)
    qt, qs, gt, logit = call(
        prepare_kernel,
        (turned, stacked, turned, pair_row),
        place,
        qg_rows,
        move(qg_rows, flip_core),
        logit,
        flip_tp(logit, 1),
        specs=[SMEM] + [VMEM] * 4,
        us=0.25,
    )
    chunk, logit = call(
        join_sum_kernel,
        (shape((CHUNK, pair_width), BF16), pair_row),
        logit,
        move(logit, flip_core),
        two,
        *neighbours,
    )
    chunks = [chunk] + [move(chunk, up_x(k)) for k in (1, 2, 3)]

    acc_shape, stats_shape = shape((HEAD_SIZE, lanes), F32), shape((8, lanes), F32)
    state = ()
    for k in range(NX):
        extra = ()
        if k == NX - 1:
            gate, dt, ds = call(
                gate_kernel,
                (pair_row, turned, stacked),
                place,
                counts,
                logit,
                flip_tp(logit, 2),
                gt,
                specs=scalars + [VMEM] * 3,
                after=(state[1],),
                us=0.7,
            )
            extra = (dt, gt)
        state = call(
            functools.partial(forward_kernel, k, k == NX - 1),
            (acc_shape, stats_shape),
            place,
            counts,
            chunks[k],
            qt,
            *extra,
            *state,
            specs=scalars + [VMEM] * (2 + len(extra) + len(state)),
            scratch=packed,
            us=2.2,
        )
    acc, stats = state
    stats_other = move(stats, flip_core)
    acc_other = move(acc, flip_core)

    sums = shape((TILE // 2, pair_width), F32)
    part = call(gate_part_kernel, pair_row, stats, stats_other)

    received, state = {}, ()
    for k in (1, 2, 3, 0):
        extra, more, after = (), (), ()
        if k == 2:
            extra, more = (part, flip_tp(part, 1)), (pair_row,)
        if k == 0:
            router = call(
                router_kernel,
                sums,
                place,
                counts,
                part,
                flip_tp(part, 2),
                gate,
                t_rows,
                specs=scalars + [VMEM] * 4,
                after=(received[1], *state),
                us=0.7,
            )
            after = (router, received[2])
        grad, *state = call(
            functools.partial(backward_kernel, k),
            (shape((CHUNK, pair_width), F32 if k == 0 else BF16), acc_shape, *more),
            place,
            counts,
            chunks[k],
            qt,
            qs,
            dt,
            ds,
            stats,
            stats_other,
            *extra,
            *state,
            specs=scalars + [VMEM] * (7 + len(extra) + len(state)),
            scratch=packed + [pltpu.VMEM((CHUNK, pair_width), F32)],
            after=after,
            us=2.3,
        )
        if k == 2:
            part = state.pop()
        received[k] = grad if k == 0 else move(grad, down_x(k))
    dq = state[0]

    router = call(add_kernel, sums, router, move(router, flip_x(1)), after=(dq,))
    rows = shape((SLOTS, width), F32)
    routed, dq_own, dq_send = call(
        attended_kernel,
        (shape((count, width), BF16), rows, rows),
        place,
        counts,
        chosen,
        stats,
        stats_other,
        acc,
        acc_other,
        gate,
        dq,
        specs=scalars + [VMEM] * 7,
        after=(router,),
        us=1.9,
    )

    half = CHUNK // 4
    keep, keep_sum, *sends = call(
        sum_x_kernel,
        (shape((half, pair_width), F32), sums)
        + (shape((half + TILE, pair_width), BF16),) * 3,
        *[received[k] for k in range(NX)],
        router,
        move(router, flip_x(2)),
        after=(dq_own,),
        us=0.12,
    )
    d_queries, ready = call(
        queries_kernel,
        (shape((count, width), BF16), pair_row),
        place,
        counts,
        chosen,
        dq_own,
        move(dq_send, flip_core),
        specs=scalars + [VMEM] * 3,
        after=(keep,),
        us=1.0,
    )
    keep, keep_sum, send = call(
        sum_z_kernel,
        (
            shape((SLOTS, pair_width), F32),
            sums,
            shape((SLOTS + TILE, pair_width), BF16),
        ),
        keep,
        keep_sum,
        *[move(sends[i], by_z(-k)) for i, k in enumerate((2, 4, 6))],
        after=(ready,),
    )
    got = move(send, flip_z)
    router = call(last_sum_kernel, sums, keep_sum, got)
    router = router + move(router, flip_core)
    pair_grads = call(
        pairs_kernel,
        shape((2 * count, HEAD_SIZE), BF16),
        place,
        counts,
        chosen,
        keep,
        got,
        specs=scalars + [VMEM] * 3,
        us=1.6,
    )
    router_grad = router.reshape(-1)[:features]
    return routed, d_queries, pair_grads.reshape(keys_values.shape), router_grad


def solution(mesh):
    placed = (
        P("ctx", "tp"),
        P("tp"),
        P("ctx", "tp"),
        P("ctx", None, "tp"),
        P("ctx", "tp"),
        P("ctx", None),
        P(),
    )
    return jax.shard_map(
        on_device,
        mesh=mesh,
        in_specs=placed,
        out_specs=(P("ctx", "tp"), P("ctx", "tp"), P("ctx", None, "tp"), P("tp")),
        check_vma=False,
    )
```

time: 281 us -> 95.2 us (0.34)
  the two profiles are of different devices: /device:TPU:2 before, /device:TPU:1 now
where the time goes in v2:
time: 95.2 us; the launch traced here: 94.9 us
  starting transfers between devices  56.1 us (59%)
  waiting for transfers between devices  21.6 us (23%)
  Pallas kernels  14 us (15%)
  local copies, waits for them, and re-layouts  2.19 us (2%)
    ppermute x22, starting transfers between devices, move(): return lax.ppermute(value, 'ctx', pairs)  47.6 us
    ppermute x22, waiting for transfers between devices, move(): return lax.ppermute(value, 'ctx', pairs)  20.2 us
    pallas_call x23, Pallas kernels, call(): pl.pallas_call(body, out_shape=outs, in_specs=[ANY] * skip + list(specs o...  14 us
    ppermute x4, starting transfers between devices, flip_tp(): return lax.ppermute(value, 'tp', [(i, i ^ bit) for i in range(4)])  8.56 us
  transfers between devices with their start and end apart: 26, of which 12 were waited for; matrix products, arithmetic and copies ran while one was open for 0% of the time, Pallas kernels for 13%

profile of v2, /device:TPU:1, one launch (start us, length us, event | category | flops | bytes accessed | tf_op | source)
XLA Modules:
  0.0 94.9 jit_solution(3621230682011255896)
XLA Ops:
  1.3 0.9 copy-done.3
  2.5 2.6 %collective-permute-start = (bf16[64,256]{1,0:T(8,128)(2,1)S(1)}, bf16[64,256]{1,0:T(8,128)(2,1)S(1)}, u32[]{:S(2)}, u32[]{:S(2)}) collective-permute-start(bf16[64,256]{1,0:T(8,128)(2,1)S(1)} %shard_map.102.refs_0_), channel_id=1, source_target_pairs={{0,8},{4,12},{8,0},{12,4},{16,24},{20,28},{24,16},{28,20},{32,40},... | collective-permute-start | bytes 98312 | tf_op jit(solution)/shard_map/ppermute | solution.py:40
  5.1 1.3 %collective-permute-done.refs_1_ = bf16[64,256]{1,0:T(8,128)(2,1)S(1)} collective-permute-done((bf16[64,256]{1,0:T(8,128)(2,1)S(1)}, bf16[64,256]{1,0:T(8,128)(2,1)S(1)}, u32[]{:S(2)}, u32[]{:S(2)}) %collective-permute-start) | collective-permute-done | bytes 32800 | tf_op jit(solution)/shard_map/ppermute | solution.py:40
  6.9 3.5 %collective-permute-start.1 = (bf16[64,1792]{1,0:T(8,128)(2,1)S(1)}, bf16[64,1792]{1,0:T(8,128)(2,1)S(1)}, u32[]{:S(2)}, u32[]{:S(2)}) collective-permute-start(bf16[64,1792]{1,0:T(8,128)(2,1)S(1)} %get-tuple-element.46.refs_1_), channel_id=1, source_target_pairs={{0,4},{4,0},{8,12},{12,8},{16,20},{20,16},{24,28},{28,24},{32,36},... | collective-permute-start | bytes 688136 | tf_op jit(solution)/shard_map/ppermute | solution.py:40
  10.4 1.3 %collective-permute-start.4 = (bf16[128,256]{1,0:T(8,128)(2,1)S(1)}, bf16[128,256]{1,0:T(8,128)(2,1)S(1)}, u32[]{:S(2)}, u32[]{:S(2)}) collective-permute-start(bf16[128,256]{1,0:T(8,128)(2,1)S(1)} %shard_map.103.refs_0_.refs_2_), channel_id=1, source_target_pairs={{0,16},{4,20},{8,24},{12,28},{16,32},{20,36},{24,40},{28,44},{32,4... | collective-permute-start | bytes 196616 | tf_op jit(solution)/shard_map/ppermute | solution.py:40
  11.7 5.1 %collective-permute-start.5 = (bf16[128,256]{1,0:T(8,128)(2,1)S(1)}, bf16[128,256]{1,0:T(8,128)(2,1)S(1)}, u32[]{:S(2)}, u32[]{:S(2)}) collective-permute-start(bf16[128,256]{1,0:T(8,128)(2,1)S(1)} %shard_map.103.refs_0_.refs_2_), channel_id=1, source_target_pairs={{0,32},{4,36},{8,40},{12,44},{16,48},{20,52},{24,56},{28,60},{32,0... | collective-permute-start | bytes 196616 | tf_op jit(solution)/shard_map/ppermute | solution.py:40
  16.8 2.4 %collective-permute-start.6 = (bf16[128,256]{1,0:T(8,128)(2,1)S(1)}, bf16[128,256]{1,0:T(8,128)(2,1)S(1)}, u32[]{:S(2)}, u32[]{:S(2)}) collective-permute-start(bf16[128,256]{1,0:T(8,128)(2,1)S(1)} %shard_map.103.refs_0_.refs_2_), channel_id=1, source_target_pairs={{0,48},{4,52},{8,56},{12,60},{16,0},{20,4},{24,8},{28,12},{32,16},... | collective-permute-start | bytes 196616 | tf_op jit(solution)/shard_map/ppermute | solution.py:40
  19.2 1.3 %collective-permute-start.2 = (f32[1,128]{1,0:T(1,128)S(1)}, f32[1,128]{1,0:T(1,128)S(1)}, u32[]{:S(2)}, u32[]{:S(2)}) collective-permute-start(f32[1,128]{1,0:T(1,128)S(1)} %get-tuple-element.47.refs_3_), channel_id=1, source_target_pairs={{0,1},{1,0},{2,3},{3,2},{4,5},{5,4},{6,7},{7,6},{8,9},{9,8},{10,11... | collective-permute-start | bytes 1544 | tf_op jit(solution)/shard_map/ppermute | solution.py:68
  20.5 1.4 %collective-permute-done.2.refs_4_ = f32[1,128]{1,0:T(1,128)S(1)} collective-permute-done((f32[1,128]{1,0:T(1,128)S(1)}, f32[1,128]{1,0:T(1,128)S(1)}, u32[]{:S(2)}, u32[]{:S(2)}) %collective-permute-start.2) | collective-permute-done | bytes 544 | tf_op jit(solution)/shard_map/ppermute | solution.py:68
  22.1 1.9 %collective-permute-start.3 = (f32[1,128]{1,0:T(1,128)S(1)}, f32[1,128]{1,0:T(1,128)S(1)}, u32[]{:S(2)}, u32[]{:S(2)}) collective-permute-start(f32[1,128]{1,0:T(1,128)S(1)} %get-tuple-element.48.refs_0_), channel_id=1, source_target_pairs={{0,4},{4,0},{8,12},{12,8},{16,20},{20,16},{24,28},{28,24},{32,36},... | collective-permute-start | bytes 1544 | tf_op jit(solution)/shard_map/ppermute | solution.py:40
  24.0 0.8 collective-permute-done.3.refs_1_
  24.8 3.1 %collective-permute-start.7 = (bf16[512,256]{1,0:T(8,128)(2,1)S(1)}, bf16[512,256]{1,0:T(8,128)(2,1)S(1)}, u32[]{:S(2)}, u32[]{:S(2)}) collective-permute-start(bf16[512,256]{1,0:T(8,128)(2,1)S(1)} %get-tuple-element.49.refs_2_.refs_4_), channel_id=1, source_target_pairs={{0,64},{4,68},{8,72},{12,76},{16,80},{20,84},{24,88},{28,92},{32,9... | collective-permute-start | bytes 786440 | tf_op jit(solution)/shard_map/ppermute | solution.py:40
  27.9 4.4 %collective-permute-start.8 = (bf16[512,256]{1,0:T(8,128)(2,1)S(1)}, bf16[512,256]{1,0:T(8,128)(2,1)S(1)}, u32[]{:S(2)}, u32[]{:S(2)}) collective-permute-start(bf16[512,256]{1,0:T(8,128)(2,1)S(1)} %get-tuple-element.49.refs_2_.refs_4_), channel_id=1, source_target_pairs={{0,128},{4,132},{8,136},{12,140},{16,144},{20,148},{24,152},{28,15... | collective-permute-start | bytes 786440 | tf_op jit(solution)/shard_map/ppermute | solution.py:40
  32.3 1.3 %collective-permute-start.10 = (bf16[512,256]{1,0:T(8,128)(2,1)S(1)}, bf16[512,256]{1,0:T(8,128)(2,1)S(1)}, u32[]{:S(2)}, u32[]{:S(2)}) collective-permute-start(bf16[512,256]{1,0:T(8,128)(2,1)S(1)} %get-tuple-element.49.refs_2_.refs_4_), channel_id=1, source_target_pairs={{0,192},{4,196},{8,200},{12,204},{16,208},{20,212},{24,216},{28,22... | collective-permute-start | bytes 786440 | tf_op jit(solution)/shard_map/ppermute | solution.py:40
  33.6 3.0 %collective-permute-start.9 = (f32[1,128]{1,0:T(1,128)S(1)}, f32[1,128]{1,0:T(1,128)S(1)}, u32[]{:S(2)}, u32[]{:S(2)}) collective-permute-start(f32[1,128]{1,0:T(1,128)S(1)} %get-tuple-element.57.refs_3_), channel_id=1, source_target_pairs={{0,2},{1,3},{2,0},{3,1},{4,6},{5,7},{6,4},{7,5},{8,10},{9,11},{10,... | collective-permute-start | bytes 1544 | tf_op jit(solution)/shard_map/ppermute | solution.py:68
  36.6 1.2 %shard_map.107 = (f32[128,896]{1,0:T(8,128)S(1)}, f32[8,896]{1,0:T(8,128)S(1)}) custom-call(s32[1]{0:T(128)} %bitcast.refs_1_.refs_0_.refs_2_, s32[64]{0:T(128)S(1)} %copy-done.4, bf16[512,256]{1,0:T(8,128)(2,1)S(1)} %get-tuple-element.49.refs_2_.refs_4_, bf16[128,896]{1,0:T(8,128)(2,1)S(1)} %get-tuple-element.50.refs_3_.refs_5_), custom_call_target="tpu_custom_call" | custom-call | flops 2537700096 | bytes 8118000 | tf_op jit(solution)/shard_map/pallas_call | solution.py:82
  37.8 0.7 shard_map.108
  38.9 0.7 shard_map.109
  39.6 0.7 shard_map.110
  40.3 2.1 %collective-permute-done.10.refs_2_ = bf16[512,256]{1,0:T(8,128)(2,1)S(1)} collective-permute-done((bf16[512,256]{1,0:T(8,128)(2,1)S(1)}, bf16[512,256]{1,0:T(8,128)(2,1)S(1)}, u32[]{:S(2)}, u32[]{:S(2)}) %collective-permute-start.10) | collective-permute-done | bytes 262176 | tf_op jit(solution)/shard_map/ppermute | solution.py:40
  42.4 0.8 shard_map.111
  43.9 0.8 collective-permute-done.11.refs_8_.refs_1_.refs_10_.refs_5_
  44.7 1.4 %collective-permute-start.13 = (f32[1,128]{1,0:T(1,128)S(1)}, f32[1,128]{1,0:T(1,128)S(1)}, u32[]{:S(2)}, u32[]{:S(2)}) collective-permute-start(f32[1,128]{1,0:T(1,128)S(1)} %shard_map.113.refs_9_), channel_id=1, source_target_pairs={{0,1},{1,0},{2,3},{3,2},{4,5},{5,4},{6,7},{7,6},{8,9},{9,8},{10,11... | collective-permute-start | bytes 1544 | tf_op jit(solution)/shard_map/ppermute | solution.py:68
  46.1 0.7 shard_map.112
  46.7 1.3 %collective-permute-start.12 = (bf16[512,256]{1,0:T(8,128)(2,1)S(1)}, bf16[512,256]{1,0:T(8,128)(2,1)S(1)}, u32[]{:S(2)}, u32[]{:S(2)}) collective-permute-start(bf16[512,256]{1,0:T(8,128)(2,1)S(1)} %get-tuple-element.63), channel_id=1, source_target_pairs={{64,0},{68,4},{72,8},{76,12},{80,16},{84,20},{88,24},{92,28},{96,3... | collective-permute-start | bytes 786440 | tf_op jit(solution)/shard_map/ppermute | solution.py:40
  48.0 0.7 shard_map.114
  48.7 2.9 %collective-permute-start.14 = (f32[1,128]{1,0:T(1,128)S(1)}, f32[1,128]{1,0:T(1,128)S(1)}, u32[]{:S(2)}, u32[]{:S(2)}) collective-permute-start(f32[1,128]{1,0:T(1,128)S(1)} %get-tuple-element.67.refs_4_), channel_id=1, source_target_pairs={{0,2},{1,3},{2,0},{3,1},{4,6},{5,7},{6,4},{7,5},{8,10},{9,11},{10,... | collective-permute-start | bytes 1544 | tf_op jit(solution)/shard_map/ppermute | solution.py:68
  51.6 1.3 %collective-permute-start.15 = (bf16[512,256]{1,0:T(8,128)(2,1)S(1)}, bf16[512,256]{1,0:T(8,128)(2,1)S(1)}, u32[]{:S(2)}, u32[]{:S(2)}) collective-permute-start(bf16[512,256]{1,0:T(8,128)(2,1)S(1)} %get-tuple-element.70), channel_id=1, source_target_pairs={{128,0},{132,4},{136,8},{140,12},{144,16},{148,20},{152,24},{156,2... | collective-permute-start | bytes 786440 | tf_op jit(solution)/shard_map/ppermute | solution.py:40
  52.9 0.7 shard_map.115
  53.6 1.3 %collective-permute-start.18 = (bf16[512,256]{1,0:T(8,128)(2,1)S(1)}, bf16[512,256]{1,0:T(8,128)(2,1)S(1)}, u32[]{:S(2)}, u32[]{:S(2)}) collective-permute-start(bf16[512,256]{1,0:T(8,128)(2,1)S(1)} %get-tuple-element.76), channel_id=1, source_target_pairs={{192,0},{196,4},{200,8},{204,12},{208,16},{212,20},{216,24},{220,2... | collective-permute-start | bytes 786440 | tf_op jit(solution)/shard_map/ppermute | solution.py:40
  54.9 1.0 %collective-permute-done.12.refs_0_.refs_2_ = bf16[512,256]{1,0:T(8,128)(2,1)S(1)} collective-permute-done((bf16[512,256]{1,0:T(8,128)(2,1)S(1)}, bf16[512,256]{1,0:T(8,128)(2,1)S(1)}, u32[]{:S(2)}, u32[]{:S(2)}) %collective-permute-start.12) | collective-permute-done | bytes 262176 | tf_op jit(solution)/shard_map/ppermute | solution.py:40
  55.8 0.7 shard_map.116.refs_0_.refs_1_
  56.5 4.1 %collective-permute-start.16 = (f32[8,256]{1,0:T(8,128)S(1)}, f32[8,256]{1,0:T(8,128)S(1)}, u32[]{:S(2)}, u32[]{:S(2)}) collective-permute-start(f32[8,256]{1,0:T(8,128)S(1)} %shard_map.116.refs_0_.refs_1_), channel_id=1, source_target_pairs={{0,64},{4,68},{8,72},{12,76},{16,80},{20,84},{24,88},{28,92},{32,9... | collective-permute-start | bytes 24584 | tf_op jit(solution)/shard_map/ppermute | solution.py:40
  60.6 5.5 %collective-permute-done.15.refs_1_.refs_3_ = bf16[512,256]{1,0:T(8,128)(2,1)S(1)} collective-permute-done((bf16[512,256]{1,0:T(8,128)(2,1)S(1)}, bf16[512,256]{1,0:T(8,128)(2,1)S(1)}, u32[]{:S(2)}, u32[]{:S(2)}) %collective-permute-start.15) | collective-permute-done | bytes 262176 | tf_op jit(solution)/shard_map/ppermute | solution.py:40
  66.2 1.3 %shard_map.117 = (f32[512,256]{1,0:T(8,128)S(1)}, f32[128,896]{1,0:T(8,128)S(1)}) custom-call(f32[8,256]{1,0:T(8,128)S(1)} %shard_map.116.refs_0_.refs_1_, bf16[512,256]{1,0:T(8,128)(2,1)S(1)} %collective-permute-done.15.refs_1_.refs_3_, s32[1]{0:T(128)} %bitcast.refs_1_.refs_0_.refs_2_, s32[64]{0:T(128)S(1)} %copy-done.4, ...), custom_call_target="tpu_custom_call" | custom-call | flops 2653050112 | bytes 8487000 | tf_op jit(solution)/shard_map/pallas_call | solution.py:82
  67.5 1.7 %shard_map.119 = (bf16[256,896]{1,0:T(8,128)(2,1)}, f32[64,896]{1,0:T(8,128)S(1)}, f32[64,896]{1,0:T(8,128)S(1)}) custom-call(f32[8,256]{1,0:T(8,128)S(1)} %shard_map.118.refs_0_.refs_5_, s32[1]{0:T(128)} %bitcast.refs_1_.refs_0_.refs_2_, s32[64]{0:T(128)S(1)} %copy-done.4, s32[1,64]{1,0:T(1,128)S(1)} %copy-done.5, ...), custom_call_target="tpu_custom_call" | custom-call | flops 2191650048 | bytes 7011000 | tf_op jit(solution)/shard_map/pallas_call | solution.py:82
  69.2 1.7 %collective-permute-start.20 = (f32[64,896]{1,0:T(8,128)S(1)}, f32[64,896]{1,0:T(8,128)S(1)}, u32[]{:S(2)}, u32[]{:S(2)}) collective-permute-start(f32[64,896]{1,0:T(8,128)S(1)} %get-tuple-element.78), channel_id=1, source_target_pairs={{0,4},{4,0},{8,12},{12,8},{16,20},{20,16},{24,28},{28,24},{32,36},... | collective-permute-start | bytes 688136 | tf_op jit(solution)/shard_map/ppermute | solution.py:40
  71.4 1.4 %collective-permute-done.18.refs_4_ = bf16[512,256]{1,0:T(8,128)(2,1)S(1)} collective-permute-done((bf16[512,256]{1,0:T(8,128)(2,1)S(1)}, bf16[512,256]{1,0:T(8,128)(2,1)S(1)}, u32[]{:S(2)}, u32[]{:S(2)}) %collective-permute-start.18) | collective-permute-done | bytes 262176 | tf_op jit(solution)/shard_map/ppermute | solution.py:40
  72.8 2.1 %collective-permute-done.19.refs_6_ = f32[8,256]{1,0:T(8,128)S(1)} collective-permute-done((f32[8,256]{1,0:T(8,128)S(1)}, f32[8,256]{1,0:T(8,128)S(1)}, u32[]{:S(2)}, u32[]{:S(2)}) %collective-permute-start.19) | collective-permute-done | bytes 8224 | tf_op jit(solution)/shard_map/ppermute | solution.py:40
  75.0 2.1 %collective-permute-start.21 = (bf16[144,256]{1,0:T(8,128)(2,1)S(1)}, bf16[144,256]{1,0:T(8,128)(2,1)S(1)}, u32[]{:S(2)}, u32[]{:S(2)}) collective-permute-start(bf16[144,256]{1,0:T(8,128)(2,1)S(1)} %get-tuple-element.82), channel_id=1, source_target_pairs={{0,48},{4,52},{8,56},{12,60},{16,0},{20,4},{24,8},{28,12},{32,16},... | collective-permute-start | bytes 221192 | tf_op jit(solution)/shard_map/ppermute | solution.py:40
  77.1 1.4 %collective-permute-start.22 = (bf16[144,256]{1,0:T(8,128)(2,1)S(1)}, bf16[144,256]{1,0:T(8,128)(2,1)S(1)}, u32[]{:S(2)}, u32[]{:S(2)}) collective-permute-start(bf16[144,256]{1,0:T(8,128)(2,1)S(1)} %get-tuple-element.83), channel_id=1, source_target_pairs={{0,32},{4,36},{8,40},{12,44},{16,48},{20,52},{24,56},{28,60},{32,0... | collective-permute-start | bytes 221192 | tf_op jit(solution)/shard_map/ppermute | solution.py:40
  78.5 1.5 %collective-permute-start.23 = (bf16[144,256]{1,0:T(8,128)(2,1)S(1)}, bf16[144,256]{1,0:T(8,128)(2,1)S(1)}, u32[]{:S(2)}, u32[]{:S(2)}) collective-permute-start(bf16[144,256]{1,0:T(8,128)(2,1)S(1)} %get-tuple-element.84), channel_id=1, source_target_pairs={{0,16},{4,20},{8,24},{12,28},{16,32},{20,36},{24,40},{28,44},{32,4... | collective-permute-start | bytes 221192 | tf_op jit(solution)/shard_map/ppermute | solution.py:40
  80.0 1.6 %shard_map.121 = (bf16[256,896]{1,0:T(8,128)(2,1)}, f32[1,128]{1,0:T(1,128)S(1)}) custom-call(f32[128,256]{1,0:T(8,128)S(1)} %get-tuple-element.77.refs_0_.refs_1_, s32[1]{0:T(128)} %bitcast.refs_1_.refs_0_.refs_2_, s32[64]{0:T(128)S(1)} %copy-done.4, s32[1,64]{1,0:T(1,128)S(1)} %copy-done.5, f32[64,896]{1,0:T(8,128)S(1)} %get-tuple-element.74.refs_0_.refs_4_, ...), custom_call_target="tpu_custom_call" | custom-call | flops 1153500032 | bytes 3690000 | tf_op jit(solution)/shard_map/pallas_call | solution.py:82
  81.6 3.5 %collective-permute-done.22.refs_4_ = bf16[144,256]{1,0:T(8,128)(2,1)S(1)} collective-permute-done((bf16[144,256]{1,0:T(8,128)(2,1)S(1)}, bf16[144,256]{1,0:T(8,128)(2,1)S(1)}, u32[]{:S(2)}, u32[]{:S(2)}) %collective-permute-start.22) | collective-permute-done | bytes 73760 | tf_op jit(solution)/shard_map/ppermute | solution.py:40
  85.1 4.9 %collective-permute-start.24 = (bf16[80,256]{1,0:T(8,128)(2,1)S(1)}, bf16[80,256]{1,0:T(8,128)(2,1)S(1)}, u32[]{:S(2)}, u32[]{:S(2)}) collective-permute-start(bf16[80,256]{1,0:T(8,128)(2,1)S(1)} %get-tuple-element.86), channel_id=1, source_target_pairs={{0,8},{4,12},{8,0},{12,4},{16,24},{20,28},{24,16},{28,20},{32,40},... | collective-permute-start | bytes 122888 | tf_op jit(solution)/shard_map/ppermute | solution.py:40
  90.1 1.4 %collective-permute-done.24.refs_4_.refs_1_ = bf16[80,256]{1,0:T(8,128)(2,1)S(1)} collective-permute-done((bf16[80,256]{1,0:T(8,128)(2,1)S(1)}, bf16[80,256]{1,0:T(8,128)(2,1)S(1)}, u32[]{:S(2)}, u32[]{:S(2)}) %collective-permute-start.24) | collective-permute-done | bytes 40992 | tf_op jit(solution)/shard_map/ppermute | solution.py:40
  91.5 1.4 %collective-permute-start.25 = (f32[8,256]{1,0:T(8,128)S(1)}, f32[8,256]{1,0:T(8,128)S(1)}, u32[]{:S(2)}, u32[]{:S(2)}) collective-permute-start(f32[8,256]{1,0:T(8,128)S(1)} %shard_map.124), channel_id=1, source_target_pairs={{0,4},{4,0},{8,12},{12,8},{16,20},{20,16},{24,28},{28,24},{32,36},... | collective-permute-start | bytes 24584 | tf_op jit(solution)/shard_map/ppermute | solution.py:40
  92.8 1.4 %shard_map.123 = bf16[512,128]{1,0:T(8,128)(2,1)} custom-call(s32[1]{0:T(128)} %bitcast.refs_1_.refs_0_.refs_2_, s32[64]{0:T(128)S(1)} %copy-done.4, s32[1,64]{1,0:T(1,128)S(1)} %copy-done.5, f32[64,256]{1,0:T(8,128)S(1)} %get-tuple-element.85.refs_3_, bf16[80,256]{1,0:T(8,128)(2,1)S(1)} %collective-permute-done.24.refs_4_.refs_1_), custom_call_target="tpu_custom_call" | custom-call | flops 1845600000 | bytes 5904000 | tf_op jit(solution)/shard_map/pallas_call | solution.py:82
  (44 shorter events, 4.2 us)
Async XLA Ops:
  0.6 0.7 copy-start.5
  1.3 0.9 copy-start.3
  2.2 4.2 %copy-start = (bf16[256,1792]{1,0:T(8,128)(2,1)S(1)}, bf16[256,1792]{1,0:T(8,128)(2,1)}, u32[]{:S(2)}) copy-start(bf16[256,1792]{1,0:T(8,128)(2,1)} %refs_5_.1) | copy-start | bytes 2752516
  2.2 4.2 %copy-start.1 = (bf16[256,896]{1,0:T(8,128)(2,1)S(1)}, bf16[256,896]{1,0:T(8,128)(2,1)}, u32[]{:S(2)}) copy-start(bf16[256,896]{1,0:T(8,128)(2,1)} %refs_3_.5) | copy-start | bytes 1376260
  2.2 4.2 %copy-start.2 = (bf16[256,896]{1,0:T(8,128)(2,1)S(1)}, bf16[256,896]{1,0:T(8,128)(2,1)}, u32[]{:S(2)}) copy-start(bf16[256,896]{1,0:T(8,128)(2,1)} %refs_4_.1) | copy-start | bytes 1376260
  2.5 2.6 %copy-start.6 = (bf16[1792]{0:T(1024)(128)(2,1)S(1)}, bf16[1792]{0:T(1024)(128)(2,1)}, u32[]{:S(2)}) copy-start(bf16[1792]{0:T(1024)(128)(2,1)} %param.8) | copy-start | bytes 10756
  2.5 3.9 %collective-permute-start = (bf16[64,256]{1,0:T(8,128)(2,1)S(1)}, bf16[64,256]{1,0:T(8,128)(2,1)S(1)}, u32[]{:S(2)}, u32[]{:S(2)}) collective-permute-start(bf16[64,256]{1,0:T(8,128)(2,1)S(1)} %shard_map.102.refs_0_), channel_id=1, source_target_pairs={{0,8},{4,12},{8,0},{12,4},{16,24},{20,28},{24,16},{28,20},{32,40},... | collective-permute-start | bytes 98312 | tf_op jit(solution)/shard_map/ppermute | solution.py:40
  6.9 14.9 %collective-permute-start.1 = (bf16[64,1792]{1,0:T(8,128)(2,1)S(1)}, bf16[64,1792]{1,0:T(8,128)(2,1)S(1)}, u32[]{:S(2)}, u32[]{:S(2)}) collective-permute-start(bf16[64,1792]{1,0:T(8,128)(2,1)S(1)} %get-tuple-element.46.refs_1_), channel_id=1, source_target_pairs={{0,4},{4,0},{8,12},{12,8},{16,20},{20,16},{24,28},{28,24},{32,36},... | collective-permute-start | bytes 688136 | tf_op jit(solution)/shard_map/ppermute | solution.py:40
  10.4 13.5 %collective-permute-start.4 = (bf16[128,256]{1,0:T(8,128)(2,1)S(1)}, bf16[128,256]{1,0:T(8,128)(2,1)S(1)}, u32[]{:S(2)}, u32[]{:S(2)}) collective-permute-start(bf16[128,256]{1,0:T(8,128)(2,1)S(1)} %shard_map.103.refs_0_.refs_2_), channel_id=1, source_target_pairs={{0,16},{4,20},{8,24},{12,28},{16,32},{20,36},{24,40},{28,44},{32,4... | collective-permute-start | bytes 196616 | tf_op jit(solution)/shard_map/ppermute | solution.py:40
  11.7 12.3 %collective-permute-start.5 = (bf16[128,256]{1,0:T(8,128)(2,1)S(1)}, bf16[128,256]{1,0:T(8,128)(2,1)S(1)}, u32[]{:S(2)}, u32[]{:S(2)}) collective-permute-start(bf16[128,256]{1,0:T(8,128)(2,1)S(1)} %shard_map.103.refs_0_.refs_2_), channel_id=1, source_target_pairs={{0,32},{4,36},{8,40},{12,44},{16,48},{20,52},{24,56},{28,60},{32,0... | collective-permute-start | bytes 196616 | tf_op jit(solution)/shard_map/ppermute | solution.py:40
  16.8 7.2 %collective-permute-start.6 = (bf16[128,256]{1,0:T(8,128)(2,1)S(1)}, bf16[128,256]{1,0:T(8,128)(2,1)S(1)}, u32[]{:S(2)}, u32[]{:S(2)}) collective-permute-start(bf16[128,256]{1,0:T(8,128)(2,1)S(1)} %shard_map.103.refs_0_.refs_2_), channel_id=1, source_target_pairs={{0,48},{4,52},{8,56},{12,60},{16,0},{20,4},{24,8},{28,12},{32,16},... | collective-permute-start | bytes 196616 | tf_op jit(solution)/shard_map/ppermute | solution.py:40
  19.2 2.7 %collective-permute-start.2 = (f32[1,128]{1,0:T(1,128)S(1)}, f32[1,128]{1,0:T(1,128)S(1)}, u32[]{:S(2)}, u32[]{:S(2)}) collective-permute-start(f32[1,128]{1,0:T(1,128)S(1)} %get-tuple-element.47.refs_3_), channel_id=1, source_target_pairs={{0,1},{1,0},{2,3},{3,2},{4,5},{5,4},{6,7},{7,6},{8,9},{9,8},{10,11... | collective-permute-start | bytes 1544 | tf_op jit(solution)/shard_map/ppermute | solution.py:68
  22.1 2.7 %collective-permute-start.3 = (f32[1,128]{1,0:T(1,128)S(1)}, f32[1,128]{1,0:T(1,128)S(1)}, u32[]{:S(2)}, u32[]{:S(2)}) collective-permute-start(f32[1,128]{1,0:T(1,128)S(1)} %get-tuple-element.48.refs_0_), channel_id=1, source_target_pairs={{0,4},{4,0},{8,12},{12,8},{16,20},{20,16},{24,28},{28,24},{32,36},... | collective-permute-start | bytes 1544 | tf_op jit(solution)/shard_map/ppermute | solution.py:40
  24.8 13.0 %collective-permute-start.7 = (bf16[512,256]{1,0:T(8,128)(2,1)S(1)}, bf16[512,256]{1,0:T(8,128)(2,1)S(1)}, u32[]{:S(2)}, u32[]{:S(2)}) collective-permute-start(bf16[512,256]{1,0:T(8,128)(2,1)S(1)} %get-tuple-element.49.refs_2_.refs_4_), channel_id=1, source_target_pairs={{0,64},{4,68},{8,72},{12,76},{16,80},{20,84},{24,88},{28,92},{32,9... | collective-permute-start | bytes 786440 | tf_op jit(solution)/shard_map/ppermute | solution.py:40
  27.9 11.0 %collective-permute-start.8 = (bf16[512,256]{1,0:T(8,128)(2,1)S(1)}, bf16[512,256]{1,0:T(8,128)(2,1)S(1)}, u32[]{:S(2)}, u32[]{:S(2)}) collective-permute-start(bf16[512,256]{1,0:T(8,128)(2,1)S(1)} %get-tuple-element.49.refs_2_.refs_4_), channel_id=1, source_target_pairs={{0,128},{4,132},{8,136},{12,140},{16,144},{20,148},{24,152},{28,15... | collective-permute-start | bytes 786440 | tf_op jit(solution)/shard_map/ppermute | solution.py:40
  32.3 10.1 %collective-permute-start.10 = (bf16[512,256]{1,0:T(8,128)(2,1)S(1)}, bf16[512,256]{1,0:T(8,128)(2,1)S(1)}, u32[]{:S(2)}, u32[]{:S(2)}) collective-permute-start(bf16[512,256]{1,0:T(8,128)(2,1)S(1)} %get-tuple-element.49.refs_2_.refs_4_), channel_id=1, source_target_pairs={{0,192},{4,196},{8,200},{12,204},{16,208},{20,212},{24,216},{28,22... | collective-permute-start | bytes 786440 | tf_op jit(solution)/shard_map/ppermute | solution.py:40
  33.6 3.0 %copy-start.4 = (s32[64]{0:T(128)S(1)}, s32[64]{0:T(128)}, u32[]{:S(2)}) copy-start(s32[64]{0:T(128)} %refs_1_.15) | copy-start | bytes 772
  33.6 5.9 %collective-permute-start.9 = (f32[1,128]{1,0:T(1,128)S(1)}, f32[1,128]{1,0:T(1,128)S(1)}, u32[]{:S(2)}, u32[]{:S(2)}) collective-permute-start(f32[1,128]{1,0:T(1,128)S(1)} %get-tuple-element.57.refs_3_), channel_id=1, source_target_pairs={{0,2},{1,3},{2,0},{3,1},{4,6},{5,7},{6,4},{7,5},{8,10},{9,11},{10,... | collective-permute-start | bytes 1544 | tf_op jit(solution)/shard_map/ppermute | solution.py:68
  43.2 1.4 %collective-permute-start.11 = (f32[8,896]{1,0:T(8,128)S(1)}, f32[8,896]{1,0:T(8,128)S(1)}, u32[]{:S(2)}, u32[]{:S(2)}) collective-permute-start(f32[8,896]{1,0:T(8,128)S(1)} %get-tuple-element.62.refs_7_.refs_0_.refs_9_.refs_4_), channel_id=1, source_target_pairs={{0,4},{4,0},{8,12},{12,8},{16,20},{20,16},{24,28},{28,24},{32,36},... | collective-permute-start | bytes 86024 | tf_op jit(solution)/shard_map/ppermute | solution.py:40
  43.8 23.7 %collective-permute-start.17 = (f32[128,896]{1,0:T(8,128)S(1)}, f32[128,896]{1,0:T(8,128)S(1)}, u32[]{:S(2)}, u32[]{:S(2)}) collective-permute-start(f32[128,896]{1,0:T(8,128)S(1)} %get-tuple-element.72.refs_6_), channel_id=1, source_target_pairs={{0,4},{4,0},{8,12},{12,8},{16,20},{20,16},{24,28},{28,24},{32,36},... | collective-permute-start | bytes 1376264 | tf_op jit(solution)/shard_map/ppermute | solution.py:40
  44.7 3.4 %collective-permute-start.13 = (f32[1,128]{1,0:T(1,128)S(1)}, f32[1,128]{1,0:T(1,128)S(1)}, u32[]{:S(2)}, u32[]{:S(2)}) collective-permute-start(f32[1,128]{1,0:T(1,128)S(1)} %shard_map.113.refs_9_), channel_id=1, source_target_pairs={{0,1},{1,0},{2,3},{3,2},{4,5},{5,4},{6,7},{7,6},{8,9},{9,8},{10,11... | collective-permute-start | bytes 1544 | tf_op jit(solution)/shard_map/ppermute | solution.py:68
  46.7 9.1 %collective-permute-start.12 = (bf16[512,256]{1,0:T(8,128)(2,1)S(1)}, bf16[512,256]{1,0:T(8,128)(2,1)S(1)}, u32[]{:S(2)}, u32[]{:S(2)}) collective-permute-start(bf16[512,256]{1,0:T(8,128)(2,1)S(1)} %get-tuple-element.63), channel_id=1, source_target_pairs={{64,0},{68,4},{72,8},{76,12},{80,16},{84,20},{88,24},{92,28},{96,3... | collective-permute-start | bytes 786440 | tf_op jit(solution)/shard_map/ppermute | solution.py:40
  48.7 6.2 %collective-permute-start.14 = (f32[1,128]{1,0:T(1,128)S(1)}, f32[1,128]{1,0:T(1,128)S(1)}, u32[]{:S(2)}, u32[]{:S(2)}) collective-permute-start(f32[1,128]{1,0:T(1,128)S(1)} %get-tuple-element.67.refs_4_), channel_id=1, source_target_pairs={{0,2},{1,3},{2,0},{3,1},{4,6},{5,7},{6,4},{7,5},{8,10},{9,11},{10,... | collective-permute-start | bytes 1544 | tf_op jit(solution)/shard_map/ppermute | solution.py:68
  51.6 14.6 %collective-permute-start.15 = (bf16[512,256]{1,0:T(8,128)(2,1)S(1)}, bf16[512,256]{1,0:T(8,128)(2,1)S(1)}, u32[]{:S(2)}, u32[]{:S(2)}) collective-permute-start(bf16[512,256]{1,0:T(8,128)(2,1)S(1)} %get-tuple-element.70), channel_id=1, source_target_pairs={{128,0},{132,4},{136,8},{140,12},{144,16},{148,20},{152,24},{156,2... | collective-permute-start | bytes 786440 | tf_op jit(solution)/shard_map/ppermute | solution.py:40
  53.6 19.3 %collective-permute-start.18 = (bf16[512,256]{1,0:T(8,128)(2,1)S(1)}, bf16[512,256]{1,0:T(8,128)(2,1)S(1)}, u32[]{:S(2)}, u32[]{:S(2)}) collective-permute-start(bf16[512,256]{1,0:T(8,128)(2,1)S(1)} %get-tuple-element.76), channel_id=1, source_target_pairs={{192,0},{196,4},{200,8},{204,12},{208,16},{212,20},{216,24},{220,2... | collective-permute-start | bytes 786440 | tf_op jit(solution)/shard_map/ppermute | solution.py:40
  56.5 10.9 %collective-permute-start.16 = (f32[8,256]{1,0:T(8,128)S(1)}, f32[8,256]{1,0:T(8,128)S(1)}, u32[]{:S(2)}, u32[]{:S(2)}) collective-permute-start(f32[8,256]{1,0:T(8,128)S(1)} %shard_map.116.refs_0_.refs_1_), channel_id=1, source_target_pairs={{0,64},{4,68},{8,72},{12,76},{16,80},{20,84},{24,88},{28,92},{32,9... | collective-permute-start | bytes 24584 | tf_op jit(solution)/shard_map/ppermute | solution.py:40
  69.2 10.8 %collective-permute-start.20 = (f32[64,896]{1,0:T(8,128)S(1)}, f32[64,896]{1,0:T(8,128)S(1)}, u32[]{:S(2)}, u32[]{:S(2)}) collective-permute-start(f32[64,896]{1,0:T(8,128)S(1)} %get-tuple-element.78), channel_id=1, source_target_pairs={{0,4},{4,0},{8,12},{12,8},{16,20},{20,16},{24,28},{28,24},{32,36},... | collective-permute-start | bytes 688136 | tf_op jit(solution)/shard_map/ppermute | solution.py:40
  70.9 4.0 %collective-permute-start.19 = (f32[8,256]{1,0:T(8,128)S(1)}, f32[8,256]{1,0:T(8,128)S(1)}, u32[]{:S(2)}, u32[]{:S(2)}) collective-permute-start(f32[8,256]{1,0:T(8,128)S(1)} %shard_map.118.refs_0_.refs_5_), channel_id=1, source_target_pairs={{0,128},{4,132},{8,136},{12,140},{16,144},{20,148},{24,152},{28,15... | collective-permute-start | bytes 24584 | tf_op jit(solution)/shard_map/ppermute | solution.py:40
  75.0 6.6 %collective-permute-start.21 = (bf16[144,256]{1,0:T(8,128)(2,1)S(1)}, bf16[144,256]{1,0:T(8,128)(2,1)S(1)}, u32[]{:S(2)}, u32[]{:S(2)}) collective-permute-start(bf16[144,256]{1,0:T(8,128)(2,1)S(1)} %get-tuple-element.82), channel_id=1, source_target_pairs={{0,48},{4,52},{8,56},{12,60},{16,0},{20,4},{24,8},{28,12},{32,16},... | collective-permute-start | bytes 221192 | tf_op jit(solution)/shard_map/ppermute | solution.py:40
  77.1 8.0 %collective-permute-start.22 = (bf16[144,256]{1,0:T(8,128)(2,1)S(1)}, bf16[144,256]{1,0:T(8,128)(2,1)S(1)}, u32[]{:S(2)}, u32[]{:S(2)}) collective-permute-start(bf16[144,256]{1,0:T(8,128)(2,1)S(1)} %get-tuple-element.83), channel_id=1, source_target_pairs={{0,32},{4,36},{8,40},{12,44},{16,48},{20,52},{24,56},{28,60},{32,0... | collective-permute-start | bytes 221192 | tf_op jit(solution)/shard_map/ppermute | solution.py:40
  78.5 6.6 %collective-permute-start.23 = (bf16[144,256]{1,0:T(8,128)(2,1)S(1)}, bf16[144,256]{1,0:T(8,128)(2,1)S(1)}, u32[]{:S(2)}, u32[]{:S(2)}) collective-permute-start(bf16[144,256]{1,0:T(8,128)(2,1)S(1)} %get-tuple-element.84), channel_id=1, source_target_pairs={{0,16},{4,20},{8,24},{12,28},{16,32},{20,36},{24,40},{28,44},{32,4... | collective-permute-start | bytes 221192 | tf_op jit(solution)/shard_map/ppermute | solution.py:40
  85.1 6.3 %collective-permute-start.24 = (bf16[80,256]{1,0:T(8,128)(2,1)S(1)}, bf16[80,256]{1,0:T(8,128)(2,1)S(1)}, u32[]{:S(2)}, u32[]{:S(2)}) collective-permute-start(bf16[80,256]{1,0:T(8,128)(2,1)S(1)} %get-tuple-element.86), channel_id=1, source_target_pairs={{0,8},{4,12},{8,0},{12,4},{16,24},{20,28},{24,16},{28,20},{32,40},... | collective-permute-start | bytes 122888 | tf_op jit(solution)/shard_map/ppermute | solution.py:40
  91.5 2.8 %collective-permute-start.25 = (f32[8,256]{1,0:T(8,128)S(1)}, f32[8,256]{1,0:T(8,128)S(1)}, u32[]{:S(2)}, u32[]{:S(2)}) collective-permute-start(f32[8,256]{1,0:T(8,128)S(1)} %shard_map.124), channel_id=1, source_target_pairs={{0,4},{4,0},{8,12},{12,8},{16,20},{20,16},{24,28},{28,24},{32,36},... | collective-permute-start | bytes 24584 | tf_op jit(solution)/shard_map/ppermute | solution.py:40

commit v3 on v2

v3 whole, which is shorter than its diff:
```python
import functools
import math

import jax
import jax.numpy as jnp
from jax import lax
from jax.experimental import pallas as pl
from jax.experimental.pallas import tpu as pltpu
from jax.sharding import PartitionSpec as P

HEAD_SIZE = 128
NX, NZ = 4, 8
SLOTS = 64
PAIR = 2 * SLOTS
CHUNK = NZ * SLOTS
GROUP = 256
TILE = 16
SCALE = HEAD_SIZE ** -0.5
SCALE2 = SCALE * math.log2(math.e)
MASKED = -1e30
FLOPS_PER_US, BYTES_PER_US = 1153.5e6, 3.69e6
F32, BF16 = jnp.float32, jnp.bfloat16
VMEM = pl.BlockSpec(memory_space=pltpu.VMEM)
SMEM = pl.BlockSpec(memory_space=pltpu.SMEM)
ANY = pl.BlockSpec(memory_space=pl.ANY)


def shard_of(x, z, c):
    return (x * NZ + z) * 2 + c


def move(value, target):
    pairs = []
    for x in range(NX):
        for z in range(NZ):
            for c in range(2):
                place = target(x, z, c)
                if place is not None:
                    pairs.append((shard_of(x, z, c), shard_of(*place)))
    return lax.ppermute(value, "ctx", pairs)


def up_x(k):
    return lambda x, z, c: (x + k, z, c) if x + k < NX else None


def down_x(k):
    return lambda x, z, c: (x - k, z, c) if x >= k else None


def flip_x(bit):
    return lambda x, z, c: (x ^ bit, z, c)


def by_z(k):
    return lambda x, z, c: (x, (z + k) % NZ, c)


def flip_z(x, z, c):
    return (x, z ^ 1, c)


def flip_core(x, z, c):
    return (x, z, c ^ 1)


def flip_both(x, z, c):
    return (x, z ^ 1, c ^ 1)


def flip_tp(value, bit):
    return lax.ppermute(value, "tp", [(i, i ^ bit) for i in range(4)])


def sum_over_tp(value):
    value = value + flip_tp(value, 1)
    return value + flip_tp(value, 2)


def call(kernel, outs, *args, specs=None, scratch=(), after=(), us=0.05):
    skip = len(after)

    def body(*refs):
        kernel(*refs[skip:])

    return pl.pallas_call(
        body,
        out_shape=outs,
        in_specs=[ANY] * skip + list(specs or [VMEM] * len(args)),
        out_specs=jax.tree.map(lambda _: VMEM, outs),
        scratch_shapes=list(scratch),
        compiler_params=pltpu.CompilerParams(vmem_limit_bytes=48 * 1024 * 1024),
        cost_estimate=pl.CostEstimate(
            flops=int(us * FLOPS_PER_US), bytes_accessed=int(us * BYTES_PER_US), transcendentals=0
        ),
    )(*after, *args)


def shape(dims, dtype):
    return jax.ShapeDtypeStruct(dims, dtype)


def dot_tn(a, b):
    return lax.dot_general(a, b, (((0,), (0,)), ((), ())), preferred_element_type=F32)


def dot_nt(a, b):
    return lax.dot_general(a, b, (((1,), (1,)), ((), ())), preferred_element_type=F32)


def dot(a, b):
    return jnp.dot(a, b, preferred_element_type=F32)


def one_hot(chosen_row, tokens, live=None):
    rows = lax.broadcasted_iota(jnp.int32, (tokens, SLOTS), 0)
    hit = rows == chosen_row
    if live is not None:
        hit = hit & (lax.broadcasted_iota(jnp.int32, (tokens, SLOTS), 1) < live)
    return jnp.where(hit, 1.0, 0.0).astype(BF16)


def half_mask(offset):
    i = lax.broadcasted_iota(jnp.int32, (SLOTS, PAIR), 0)
    j = lax.broadcasted_iota(jnp.int32, (SLOTS, PAIR), 1)
    return j == i + offset


def here():
    shard = lax.axis_index("ctx")
    return shard // (2 * NZ), (shard // 2) % NZ, shard % 2


def own_column(row):
    mine = half_mask(here()[2] * SLOTS)
    return jnp.sum(jnp.where(mine, row, 0.0), axis=1, keepdims=True)


def pair_hot(chosen, tokens, live=SLOTS):
    both = jnp.concatenate([chosen[...], chosen[...]], axis=1)
    lane = lax.broadcasted_iota(jnp.int32, (1, PAIR), 1)
    second = lane >= SLOTS
    target = both * 2 + jnp.where(second, 1, 0)
    slot = lane - jnp.where(second, SLOTS, 0)
    target = jnp.where(slot < live, target, -1)
    rows = lax.broadcasted_iota(jnp.int32, (2 * tokens, PAIR), 0)
    return jnp.where(rows == target, 1.0, 0.0).astype(BF16)


def pick_pairs_kernel(chosen, pairs, rows):
    picked = dot_tn(pair_hot(chosen, pairs.shape[0] // 2), pairs[...]).astype(BF16)
    rows[:, :HEAD_SIZE] = picked[:SLOTS, :]
    rows[:, HEAD_SIZE:] = picked[SLOTS:, :]


def pick_rows_kernel(chosen, queries, grads, tokens, weight, qg_rows, t_rows, logit):
    hot = one_hot(chosen[...], queries.shape[0])
    width = queries.shape[1]
    qg_rows[:, :width] = dot_tn(hot, queries[...]).astype(BF16)
    qg_rows[:, width:] = dot_tn(hot, grads[...]).astype(BF16)
    picked = dot_tn(hot, tokens[...]).astype(BF16)
    t_rows[...] = picked
    terms = picked.astype(F32) * weight[...].astype(F32)
    column = jnp.sum(terms, axis=1, keepdims=True)
    mine = half_mask(here()[2] * SLOTS)
    logit[...] = jnp.sum(jnp.where(mine, column, 0.0), axis=0, keepdims=True)


def prepare_kernel(own, other, logit, logit_other, qt, qs, gt, logit_sum):
    logit_sum[...] = logit[...] + logit_other[...]
    first = here()[2] == 0
    lanes = qt.shape[1]
    for h in range(own.shape[1] // HEAD_SIZE):
        cols = slice(h * HEAD_SIZE, (h + 1) * HEAD_SIZE)
        mine, theirs = own[:, cols].astype(F32), other[:, cols].astype(F32)
        both = jnp.where(
            first,
            jnp.concatenate([mine, theirs], axis=0),
            jnp.concatenate([theirs, mine], axis=0),
        )
        at = h * PAIR
        if at < lanes:
            qs[at : at + PAIR, :] = both.astype(BF16)
            qt[:, at : at + PAIR] = both.T.astype(BF16)
        else:
            gt[:, at - lanes : at - lanes + PAIR] = both.T.astype(BF16)


def gate_kernel(live, logit, logit_other, gt, gate, dt, ds):
    value = jax.nn.sigmoid(logit[...] + logit_other[...])
    gate[...] = value
    kept = jnp.broadcast_to(live[...] > 0.0, (HEAD_SIZE, PAIR))
    for h in range(gt.shape[1] // PAIR):
        cols = slice(h * PAIR, (h + 1) * PAIR)
        scaled = jnp.where(kept, gt[:, cols].astype(F32) * value, 0.0)
        dt[:, cols] = scaled.astype(BF16)
        ds[cols, :] = scaled.T.astype(BF16)


def join_sum_kernel(a, b, *refs):
    *refs, total = refs
    total[...] = a[...] + b[...]
    join_kernel(*refs)


def join_kernel(*refs):
    *parts, out = refs
    at = 0
    for part in parts:
        out[at : at + part.shape[0], :] = part[...]
        at += part.shape[0]


def masks_kernel(counts, chosen, live, hot, both_hot, *biases):
    x, z, core = here()
    chip = x * NZ + z
    lane = lax.broadcasted_iota(jnp.int32, live.shape, 1)
    seen = lane < counts[2 * chip]
    seen = seen | ((lane >= SLOTS) & (lane < SLOTS + counts[2 * chip + 1]))
    live[...] = jnp.where(seen, 1.0, 0.0)
    own = counts[2 * chip + core]
    hot[...] = one_hot(chosen[...], hot.shape[0], own)
    both_hot[...] = pair_hot(chosen, both_hot.shape[0] // 2, own)
    slot = lax.broadcasted_iota(jnp.int32, (SLOTS, PAIR), 0)
    lane = lax.broadcasted_iota(jnp.int32, (SLOTS, PAIR), 1)
    for shift, bias in enumerate(biases):
        from_x = (x - shift + NX) % NX
        for j in range(NZ):
            from_z = (z + (j % 2) * (1 - 2 * (z % 2)) - 2 * (j // 2) + NZ) % NZ
            from_chip = from_x * NZ + from_z
            ahead = (chip - from_chip) * PAIR - core * SLOTS
            seen = (slot < counts[2 * from_chip + core]) & (slot <= lane + ahead)
            bias[j * SLOTS : (j + 1) * SLOTS, :] = jnp.where(seen, 0.0, MASKED)


def lane_groups(ref):
    lanes = ref.shape[1]
    return [slice(a, min(a + GROUP, lanes)) for a in range(0, lanes, GROUP)]


def scores_of(keys, qt, bias):
    raw = dot(keys, qt)
    heads = raw.shape[1] // PAIR
    return raw * SCALE2 + jnp.concatenate([bias] * heads, axis=1)


def forward_kernel(shift, last, bias, pairs, qt, *refs):
    if shift == 0:
        acc, stats = refs
        acc[...] = jnp.zeros_like(acc)
        row = lax.broadcasted_iota(jnp.int32, stats.shape, 0)
        stats[...] = jnp.where(row == 0, MASKED, 0.0)
    else:
        if last:
            dt, gt, *refs = refs
        acc_in, stats_in, acc, stats = refs
        acc[...] = acc_in[...]
        stats[...] = stats_in[...]

    @pl.when(here()[0] >= shift)
    def _():
        keys, values = pairs[:, :HEAD_SIZE], pairs[:, HEAD_SIZE:]
        for cols in lane_groups(qt):
            scores = scores_of(keys, qt[:, cols], bias[...])
            old = stats[0:1, cols]
            new = jnp.maximum(old, jnp.max(scores, axis=0, keepdims=True))
            decay = jnp.exp2(old - new)
            weights = jnp.exp2(scores - new)
            stats[0:1, cols] = new
            total = jnp.sum(weights, axis=0, keepdims=True)
            stats[1:2, cols] = stats[1:2, cols] * decay + total
            acc[:, cols] = acc[:, cols] * decay + dot_tn(values, weights.astype(BF16))

    if last:
        stats[2:3, :] = jnp.sum(acc[...] * dt[...].astype(F32), axis=0, keepdims=True)
        stats[3:4, :] = jnp.sum(acc[...] * gt[...].astype(F32), axis=0, keepdims=True)


def merge_stats(ours, theirs):
    top = jnp.maximum(ours[0:1, :], theirs[0:1, :])
    a = jnp.exp2(ours[0:1, :] - top)
    b = jnp.exp2(theirs[0:1, :] - top)
    total = ours[1:2, :] * a + theirs[1:2, :] * b
    return top, a, b, total


def backward_kernel(shift, bias, pairs, qt, qs, dt, ds, ours, theirs, *refs):
    if shift == 1:
        out, dq = refs
        dq[...] = jnp.zeros_like(dq)
    else:
        if shift == 2:
            part, part_other, *refs = refs
        dq_in, out, dq, *refs = refs
        if shift == 2:
            refs[0][...] = part[...] + part_other[...]
        dq[...] = dq_in[...]
    used = here()[0] >= shift

    @pl.when(used)
    def _():
        top, a, b, total = merge_stats(ours, theirs)
        level = top + jnp.log2(total)
        delta = (ours[2:3, :] * a + theirs[2:3, :] * b) / total
        keys, values = pairs[:, :HEAD_SIZE], pairs[:, HEAD_SIZE:]
        d_values = jnp.zeros(values.shape, F32)
        d_keys = jnp.zeros(keys.shape, F32)
        for cols in lane_groups(qt):
            probs = jnp.exp2(scores_of(keys, qt[:, cols], bias[...]) - level[:, cols])
            d_probs = dot(values, dt[:, cols])
            d_scores = (probs * (d_probs - delta[:, cols])).astype(BF16)
            d_values += dot(probs.astype(BF16), ds[cols, :])
            d_keys += dot(d_scores, qs[cols, :])
            dq[:, cols] += dot_tn(keys, d_scores)
        out[:, :HEAD_SIZE] = (d_keys * SCALE).astype(out.dtype)
        out[:, HEAD_SIZE:] = d_values.astype(out.dtype)

    @pl.when(jnp.logical_not(used))
    def _():
        out[...] = jnp.zeros_like(out)


def gate_part_kernel(ours, theirs, part):
    top, a, b, total = merge_stats(ours, theirs)
    dots = (ours[3:4, :] * a + theirs[3:4, :] * b) / total
    part[...] = sum(
        dots[:, h * PAIR : (h + 1) * PAIR] for h in range(dots.shape[1] // PAIR)
    )


def rows_kernel(
    hot, ours, theirs, acc_ours, acc_theirs, gate, dq_ours, dq_theirs, routed, d_queries, ready
):
    ready[...] = gate[...]
    top, a, b, total = merge_stats(ours, theirs)
    a, b = a / total, b / total
    first = here()[2] == 0
    factor = own_column(gate[...])
    for h in range(acc_ours.shape[1] // PAIR):
        cols = slice(h * PAIR, (h + 1) * PAIR)
        mixed = (acc_ours[:, cols] * a[:, cols] + acc_theirs[:, cols] * b[:, cols]).T
        rows = jnp.where(first, mixed[:SLOTS, :], mixed[SLOTS:, :]).astype(BF16).astype(F32)
        routed[:, cols] = dot(hot[...], (rows * factor).astype(BF16)).astype(BF16)
        both = ((dq_ours[:, cols] + dq_theirs[:, cols]) * SCALE).T
        rows = jnp.where(first, both[:SLOTS, :], both[SLOTS:, :]).astype(BF16)
        d_queries[:, cols] = dot(hot[...], rows).astype(BF16)


def add_kernel(a, b, out):
    out[...] = a[...] + b[...]


def router_kernel(live, d_gate, d_gate_other, gate, t_rows, out):
    value = gate[...]
    d_logit = (d_gate[...] + d_gate_other[...]) * value * (1.0 - value)
    d_logit = own_column(jnp.where(live[...] > 0.0, d_logit, 0.0))
    terms = t_rows[...].astype(F32) * d_logit
    sums = jnp.sum(terms, axis=0, keepdims=True)
    width = out.shape[1]
    out[...] = jnp.zeros_like(out)
    for r in range(sums.shape[1] // width):
        out[r : r + 1, :] = sums[:, r * width : (r + 1) * width]


def put_sum(ref, at, total):
    high = total.astype(BF16)
    ref[at : at + TILE, :] = jnp.concatenate(
        [high.astype(F32), total - high.astype(F32)], axis=0
    ).astype(BF16)


def get_sum(ref, at):
    both = ref[at : at + TILE, :].astype(F32)
    return both[: TILE // 2, :] + both[TILE // 2 :, :]


def sum_x_kernel(own, a, b, c, r0, r1, dq, keep, keep_sum, dq_out, *sends):
    dq_out[...] = dq[...]
    size = keep.shape[0]
    router = r0[...] + r1[...]
    keep_sum[...] = router
    for i in range(4):
        at = slice(i * size, (i + 1) * size)
        total = own[at, :] + a[at, :].astype(F32) + b[at, :].astype(F32) + c[at, :].astype(F32)
        if i == 0:
            keep[...] = total
        else:
            sends[i - 1][:size, :] = total.astype(BF16)
            put_sum(sends[i - 1], size, router)


def sum_z_kernel(own, own_sum, a, b, c, keep, keep_sum, send):
    size = keep.shape[0]
    full = own.shape[0]
    parts = [ref[:full, :].astype(F32) for ref in (a, b, c)]
    total = own[...] + parts[0] + parts[1] + parts[2]
    router = own_sum[...] + get_sum(a, full) + get_sum(b, full) + get_sum(c, full)
    keep_sum[...] = router
    keep[...] = total[:size, :]
    send[:size, :] = total[size:, :].astype(BF16)
    put_sum(send, size, router)


def last_kernel(hot, own, a, r0, r1, r2, out, router):
    rows = own[...] + a[:SLOTS, :].astype(F32)
    rows = jnp.concatenate([rows[:, :HEAD_SIZE], rows[:, HEAD_SIZE:]], axis=0).astype(BF16)
    out[...] = dot(hot[...], rows).astype(BF16)
    total = r0[...] + get_sum(a, SLOTS) + r1[...] + r2[...]
    width = total.shape[1]
    for r in range(router.shape[0] // width):
        router[pl.ds(r * width, width)] = total[r, :]


def on_device(tokens, router_weight, queries, keys_values, routed_grad, chosen, counts):
    count = tokens.shape[0]
    width = queries.shape[1]
    lanes = width // HEAD_SIZE * PAIR
    features = tokens.shape[1]
    pair_width = 2 * HEAD_SIZE

    own_rows = call(
        pick_pairs_kernel,
        shape((SLOTS, pair_width), BF16),
        chosen,
        keys_values.reshape(2 * count, HEAD_SIZE),
        us=0.6,
    )

    pair_row = shape((1, PAIR), F32)
    two = call(
        join_kernel, shape((2 * SLOTS, pair_width), BF16), own_rows, move(own_rows, flip_z)
    )
    live, hot, both_hot, *biases = call(
        masks_kernel,
        (
            pair_row,
            shape((count, SLOTS), BF16),
            shape((2 * count, PAIR), BF16),
            *[shape((CHUNK, PAIR), F32)] * NX,
        ),
        counts,
        chosen,
        specs=[SMEM, VMEM],
        after=(own_rows,),
        us=1.0,
    )
    neighbours = [move(two, by_z(k)) for k in (2, 4, 6)]
    qg_rows, t_rows, logit = call(
        pick_rows_kernel,
        (shape((SLOTS, 2 * width), BF16), shape((SLOTS, features), BF16), pair_row),
        chosen,
        queries,
        routed_grad,
        tokens,
        router_weight.reshape(1, features),
        after=(two, live),
        us=0.6,
    )
    turned, stacked = shape((HEAD_SIZE, lanes), BF16), shape((lanes, HEAD_SIZE), BF16)
    qt, qs, gt, logit = call(
        prepare_kernel,
        (turned, stacked, turned, pair_row),
        qg_rows,
        move(qg_rows, flip_core),
        logit,
        flip_tp(logit, 1),
        us=0.25,
    )
    chunk, logit = call(
        join_sum_kernel,
        (shape((CHUNK, pair_width), BF16), pair_row),
        logit,
        move(logit, flip_core),
        two,
        *neighbours,
    )
    chunks = [chunk] + [move(chunk, up_x(k)) for k in (1, 2, 3)]

    acc_shape, stats_shape = shape((HEAD_SIZE, lanes), F32), shape((8, lanes), F32)
    state = ()
    for k in range(NX):
        extra = ()
        if k == NX - 1:
            gate, dt, ds = call(
                gate_kernel,
                (pair_row, turned, stacked),
                live,
                logit,
                flip_tp(logit, 2),
                gt,
                after=(state[1],),
                us=0.7,
            )
            extra = (dt, gt)
        state = call(
            functools.partial(forward_kernel, k, k == NX - 1),
            (acc_shape, stats_shape),
            biases[k],
            chunks[k],
            qt,
            *extra,
            *state,
            us=2.2,
        )
    acc, stats = state
    stats_other = move(stats, flip_core)
    acc_other = move(acc, flip_core)

    sums = shape((TILE // 2, pair_width), F32)
    part = call(gate_part_kernel, pair_row, stats, stats_other)

    received, state = {}, ()
    for k in (1, 2, 3, 0):
        extra, more, after = (), (), ()
        if k == 2:
            extra, more = (part, flip_tp(part, 1)), (pair_row,)
        if k == 0:
            router = call(
                router_kernel,
                sums,
                live,
                part,
                flip_tp(part, 2),
                gate,
                t_rows,
                after=(received[1], *state),
                us=0.7,
            )
            after = (router, received[2], acc_other)
        grad, *state = call(
            functools.partial(backward_kernel, k),
            (shape((CHUNK, pair_width), F32 if k == 0 else BF16), acc_shape, *more),
            biases[k],
            chunks[k],
            qt,
            qs,
            dt,
            ds,
            stats,
            stats_other,
            *extra,
            *state,
            after=after,
            us=2.3,
        )
        if k == 2:
            part = state.pop()
        received[k] = grad if k == 0 else move(grad, down_x(k))
    dq = state[0]

    router = call(add_kernel, sums, router, move(router, flip_x(1)), after=(dq,))
    half = CHUNK // 4
    keep, keep_sum, dq, *sends = call(
        sum_x_kernel,
        (shape((half, pair_width), F32), sums, acc_shape)
        + (shape((half + TILE, pair_width), BF16),) * 3,
        *[received[k] for k in range(NX)],
        router,
        move(router, flip_x(2)),
        dq,
        us=0.12,
    )
    routed, d_queries, ready = call(
        rows_kernel,
        (shape((count, width), BF16), shape((count, width), BF16), pair_row),
        hot,
        stats,
        stats_other,
        acc,
        acc_other,
        gate,
        dq,
        move(dq, flip_core),
        us=4.0,
    )
    keep, keep_sum, send = call(
        sum_z_kernel,
        (
            shape((SLOTS, pair_width), F32),
            sums,
            shape((SLOTS + TILE, pair_width), BF16),
        ),
        keep,
        keep_sum,
        *[move(sends[i], by_z(-k)) for i, k in enumerate((2, 4, 6))],
        after=(ready,),
    )
    got = move(send, flip_z)
    pair_grads, router_grad = call(
        last_kernel,
        (shape((2 * count, HEAD_SIZE), BF16), shape((features,), F32)),
        both_hot,
        keep,
        got,
        keep_sum,
        move(keep_sum, flip_core),
        move(keep_sum, flip_both),
        us=1.4,
    )
    return routed, d_queries, pair_grads.reshape(keys_values.shape), router_grad


def solution(mesh):
    placed = (
        P("ctx", "tp"),
        P("tp"),
        P("ctx", "tp"),
        P("ctx", None, "tp"),
        P("ctx", "tp"),
        P("ctx", None),
        P(),
    )
    return jax.shard_map(
        on_device,
        mesh=mesh,
        in_specs=placed,
        out_specs=(P("ctx", "tp"), P("ctx", "tp"), P("ctx", None, "tp"), P("tp")),
        check_vma=False,
    )
```

time: 95.2 us -> 89.3 us (0.938)
  the two profiles are of different devices: /device:TPU:1 before, /device:TPU:2 now
where the time goes in v3:
time: 89.3 us; the launch traced here: 89 us
  starting transfers between devices  44.7 us (50%)
  waiting for transfers between devices  30.5 us (34%)
  Pallas kernels  11.2 us (13%)
  local copies, waits for them, and re-layouts  1.59 us (2%)
  between operations  0.99 us (1%)
    ppermute x23, starting transfers between devices, move(): return lax.ppermute(value, 'ctx', pairs)  36 us
    ppermute x23, waiting for transfers between devices, move(): return lax.ppermute(value, 'ctx', pairs)  28.5 us
    pallas_call x22, Pallas kernels, call(): pl.pallas_call(body, out_shape=outs, in_specs=[ANY] * skip + list(specs o...  11.2 us
    ppermute x4, starting transfers between devices, flip_tp(): return lax.ppermute(value, 'tp', [(i, i ^ bit) for i in range(4)])  8.75 us
    ppermute x4, waiting for transfers between devices, flip_tp(): return lax.ppermute(value, 'tp', [(i, i ^ bit) for i in range(4)])  2.08 us
  transfers between devices with their start and end apart: 27, of which 11 were waited for; matrix products, arithmetic and copies ran while one was open for 0% of the time, Pallas kernels for 10%

profile of v3, /device:TPU:2, one launch (start us, length us, event | category | flops | bytes accessed | tf_op | source)
XLA Modules:
  0.0 89.0 jit_solution(1866645292986479644)
XLA Ops:
  0.6 0.6 copy-done.5
  1.3 0.9 %copy-done.3 = bf16[256,2,128]{2,1,0:T(2,128)(2,1)S(1)} copy-done((bf16[256,2,128]{2,1,0:T(2,128)(2,1)S(1)}, bf16[256,2,128]{2,1,0:T(2,128)(2,1)}, u32[]{:S(2)}) %copy-start.3) | copy-done | bytes 131096
  2.2 0.3 shard_map.102.refs_0_
  2.5 2.0 %collective-permute-start = (bf16[64,256]{1,0:T(8,128)(2,1)S(1)}, bf16[64,256]{1,0:T(8,128)(2,1)S(1)}, u32[]{:S(2)}, u32[]{:S(2)}) collective-permute-start(bf16[64,256]{1,0:T(8,128)(2,1)S(1)} %shard_map.102.refs_0_), channel_id=1, source_target_pairs={{0,8},{4,12},{8,0},{12,4},{16,24},{20,28},{24,16},{28,20},{32,40},... | collective-permute-start | bytes 98312 | tf_op jit(solution)/shard_map/ppermute | solution.py:40
  4.6 0.8 shard_map.103
  5.4 1.1 %collective-permute-done.refs_1_ = bf16[64,256]{1,0:T(8,128)(2,1)S(1)} collective-permute-done((bf16[64,256]{1,0:T(8,128)(2,1)S(1)}, bf16[64,256]{1,0:T(8,128)(2,1)S(1)}, u32[]{:S(2)}, u32[]{:S(2)}) %collective-permute-start) | collective-permute-done | bytes 32800 | tf_op jit(solution)/shard_map/ppermute | solution.py:40
  6.6 0.5 shard_map.105
  7.2 6.4 %collective-permute-start.6 = (bf16[128,256]{1,0:T(8,128)(2,1)S(1)}, bf16[128,256]{1,0:T(8,128)(2,1)S(1)}, u32[]{:S(2)}, u32[]{:S(2)}) collective-permute-start(bf16[128,256]{1,0:T(8,128)(2,1)S(1)} %shard_map.104.refs_0_.refs_2_), channel_id=1, source_target_pairs={{0,48},{4,52},{8,56},{12,60},{16,0},{20,4},{24,8},{28,12},{32,16},... | collective-permute-start | bytes 196616 | tf_op jit(solution)/shard_map/ppermute | solution.py:40
  13.6 1.0 %collective-permute-start.5 = (bf16[128,256]{1,0:T(8,128)(2,1)S(1)}, bf16[128,256]{1,0:T(8,128)(2,1)S(1)}, u32[]{:S(2)}, u32[]{:S(2)}) collective-permute-start(bf16[128,256]{1,0:T(8,128)(2,1)S(1)} %shard_map.104.refs_0_.refs_2_), channel_id=1, source_target_pairs={{0,32},{4,36},{8,40},{12,44},{16,48},{20,52},{24,56},{28,60},{32,0... | collective-permute-start | bytes 196616 | tf_op jit(solution)/shard_map/ppermute | solution.py:40
  14.6 2.8 %collective-permute-start.4 = (bf16[128,256]{1,0:T(8,128)(2,1)S(1)}, bf16[128,256]{1,0:T(8,128)(2,1)S(1)}, u32[]{:S(2)}, u32[]{:S(2)}) collective-permute-start(bf16[128,256]{1,0:T(8,128)(2,1)S(1)} %shard_map.104.refs_0_.refs_2_), channel_id=1, source_target_pairs={{0,16},{4,20},{8,24},{12,28},{16,32},{20,36},{24,40},{28,44},{32,4... | collective-permute-start | bytes 196616 | tf_op jit(solution)/shard_map/ppermute | solution.py:40
  17.4 1.6 %collective-permute-start.2 = (f32[1,128]{1,0:T(1,128)S(1)}, f32[1,128]{1,0:T(1,128)S(1)}, u32[]{:S(2)}, u32[]{:S(2)}) collective-permute-start(f32[1,128]{1,0:T(1,128)S(1)} %get-tuple-element.58.refs_2_), channel_id=1, source_target_pairs={{0,1},{1,0},{2,3},{3,2},{4,5},{5,4},{6,7},{7,6},{8,9},{9,8},{10,11... | collective-permute-start | bytes 1544 | tf_op jit(solution)/shard_map/ppermute | solution.py:72
  19.0 2.0 %collective-permute-done.2.refs_3_ = f32[1,128]{1,0:T(1,128)S(1)} collective-permute-done((f32[1,128]{1,0:T(1,128)S(1)}, f32[1,128]{1,0:T(1,128)S(1)}, u32[]{:S(2)}, u32[]{:S(2)}) %collective-permute-start.2) | collective-permute-done | bytes 544 | tf_op jit(solution)/shard_map/ppermute | solution.py:72
  20.9 0.2 shard_map.106
  21.2 0.1 collective-permute-start.3
  21.3 2.4 %collective-permute-done.5.refs_4_ = bf16[128,256]{1,0:T(8,128)(2,1)S(1)} collective-permute-done((bf16[128,256]{1,0:T(8,128)(2,1)S(1)}, bf16[128,256]{1,0:T(8,128)(2,1)S(1)}, u32[]{:S(2)}, u32[]{:S(2)}) %collective-permute-start.5) | collective-permute-done | bytes 65568 | tf_op jit(solution)/shard_map/ppermute | solution.py:40
  23.7 3.4 %collective-permute-start.9 = (bf16[512,256]{1,0:T(8,128)(2,1)S(1)}, bf16[512,256]{1,0:T(8,128)(2,1)S(1)}, u32[]{:S(2)}, u32[]{:S(2)}) collective-permute-start(bf16[512,256]{1,0:T(8,128)(2,1)S(1)} %get-tuple-element.60.refs_1_.refs_4_), channel_id=1, source_target_pairs={{0,64},{4,68},{8,72},{12,76},{16,80},{20,84},{24,88},{28,92},{32,9... | collective-permute-start | bytes 786440 | tf_op jit(solution)/shard_map/ppermute | solution.py:40
  27.1 1.9 %collective-permute-start.8 = (bf16[512,256]{1,0:T(8,128)(2,1)S(1)}, bf16[512,256]{1,0:T(8,128)(2,1)S(1)}, u32[]{:S(2)}, u32[]{:S(2)}) collective-permute-start(bf16[512,256]{1,0:T(8,128)(2,1)S(1)} %get-tuple-element.60.refs_1_.refs_4_), channel_id=1, source_target_pairs={{0,128},{4,132},{8,136},{12,140},{16,144},{20,148},{24,152},{28,15... | collective-permute-start | bytes 786440 | tf_op jit(solution)/shard_map/ppermute | solution.py:40
  29.1 0.7 collective-permute-start.7
  29.8 3.3 %collective-permute-start.10 = (f32[1,128]{1,0:T(1,128)S(1)}, f32[1,128]{1,0:T(1,128)S(1)}, u32[]{:S(2)}, u32[]{:S(2)}) collective-permute-start(f32[1,128]{1,0:T(1,128)S(1)} %get-tuple-element.70.refs_2_), channel_id=1, source_target_pairs={{0,2},{1,3},{2,0},{3,1},{4,6},{5,7},{6,4},{7,5},{8,10},{9,11},{10,... | collective-permute-start | bytes 1544 | tf_op jit(solution)/shard_map/ppermute | solution.py:72
  33.1 1.6 %shard_map.108 = (f32[128,896]{1,0:T(8,128)S(1)}, f32[8,896]{1,0:T(8,128)S(1)}) custom-call(f32[512,128]{1,0:T(8,128)S(1)} %get-tuple-element.64.refs_0_.refs_3_, bf16[512,256]{1,0:T(8,128)(2,1)S(1)} %get-tuple-element.60.refs_1_.refs_4_, bf16[128,896]{1,0:T(8,128)(2,1)S(1)} %get-tuple-element.61.refs_2_.refs_5_), custom_call_target="tpu_custom_call" | custom-call | flops 2537700096 | bytes 8118000 | tf_op jit(solution)/shard_map/pallas_call | solution.py:86
  34.7 1.6 %shard_map.109 = (f32[128,896]{1,0:T(8,128)S(1)}, f32[8,896]{1,0:T(8,128)S(1)}) custom-call(f32[512,128]{1,0:T(8,128)S(1)} %get-tuple-element.63.refs_0_, bf16[512,256]{1,0:T(8,128)(2,1)S(1)} %collective-permute-done.9.refs_1_, bf16[128,896]{1,0:T(8,128)(2,1)S(1)} %get-tuple-element.61.refs_2_.refs_5_, f32[128,896]{1,0:T(8,128)S(1)} %get-tuple-element.65.refs_3_, ...), custom_call_target="tpu_custom_call" | custom-call | flops 2537700096 | bytes 8118000 | tf_op jit(solution)/shard_map/pallas_call | solution.py:86
  36.3 0.2 shard_map.111
  36.5 0.2 shard_map.112
  36.8 0.5 collective-permute-start.12
  37.3 0.7 collective-permute-done.11.refs_7_.refs_1_.refs_10_.refs_2_
  38.0 0.9 %collective-permute-start.14 = (f32[1,128]{1,0:T(1,128)S(1)}, f32[1,128]{1,0:T(1,128)S(1)}, u32[]{:S(2)}, u32[]{:S(2)}) collective-permute-start(f32[1,128]{1,0:T(1,128)S(1)} %shard_map.114.refs_8_), channel_id=1, source_target_pairs={{0,1},{1,0},{2,3},{3,2},{4,5},{5,4},{6,7},{7,6},{8,9},{9,8},{10,11... | collective-permute-start | bytes 1544 | tf_op jit(solution)/shard_map/ppermute | solution.py:72
  38.9 1.5 %shard_map.113 = (bf16[512,256]{1,0:T(8,128)(2,1)S(1)}, f32[128,896]{1,0:T(8,128)S(1)}) custom-call(f32[512,128]{1,0:T(8,128)S(1)} %get-tuple-element.63.refs_0_, bf16[512,256]{1,0:T(8,128)(2,1)S(1)} %collective-permute-done.9.refs_1_, bf16[128,896]{1,0:T(8,128)(2,1)S(1)} %get-tuple-element.61.refs_2_.refs_5_, ...), custom_call_target="tpu_custom_call" | custom-call | flops 2653050112 | bytes 8487000 | tf_op jit(solution)/shard_map/pallas_call | solution.py:86
  40.4 5.5 %collective-permute-start.13 = (bf16[512,256]{1,0:T(8,128)(2,1)S(1)}, bf16[512,256]{1,0:T(8,128)(2,1)S(1)}, u32[]{:S(2)}, u32[]{:S(2)}) collective-permute-start(bf16[512,256]{1,0:T(8,128)(2,1)S(1)} %get-tuple-element.79), channel_id=1, source_target_pairs={{64,0},{68,4},{72,8},{76,12},{80,16},{84,20},{88,24},{92,28},{96,3... | collective-permute-start | bytes 786440 | tf_op jit(solution)/shard_map/ppermute | solution.py:40
  46.0 3.0 %collective-permute-start.15 = (f32[1,128]{1,0:T(1,128)S(1)}, f32[1,128]{1,0:T(1,128)S(1)}, u32[]{:S(2)}, u32[]{:S(2)}) collective-permute-start(f32[1,128]{1,0:T(1,128)S(1)} %get-tuple-element.83.refs_3_), channel_id=1, source_target_pairs={{0,2},{1,3},{2,0},{3,1},{4,6},{5,7},{6,4},{7,5},{8,10},{9,11},{10,... | collective-permute-start | bytes 1544 | tf_op jit(solution)/shard_map/ppermute | solution.py:72
  48.9 1.3 %collective-permute-start.16 = (bf16[512,256]{1,0:T(8,128)(2,1)S(1)}, bf16[512,256]{1,0:T(8,128)(2,1)S(1)}, u32[]{:S(2)}, u32[]{:S(2)}) collective-permute-start(bf16[512,256]{1,0:T(8,128)(2,1)S(1)} %get-tuple-element.85), channel_id=1, source_target_pairs={{128,0},{132,4},{136,8},{140,12},{144,16},{148,20},{152,24},{156,2... | collective-permute-start | bytes 786440 | tf_op jit(solution)/shard_map/ppermute | solution.py:40
  50.3 0.7 collective-permute-start.17
  51.0 0.1 collective-permute-done.15.refs_4_
  51.1 3.4 %collective-permute-done.13.refs_0_.refs_1_ = bf16[512,256]{1,0:T(8,128)(2,1)S(1)} collective-permute-done((bf16[512,256]{1,0:T(8,128)(2,1)S(1)}, bf16[512,256]{1,0:T(8,128)(2,1)S(1)}, u32[]{:S(2)}, u32[]{:S(2)}) %collective-permute-start.13) | collective-permute-done | bytes 262176 | tf_op jit(solution)/shard_map/ppermute | solution.py:40
  54.5 0.1 shard_map.117.refs_0_.refs_1_
  54.8 8.1 %collective-permute-done.16.refs_1_.refs_2_ = bf16[512,256]{1,0:T(8,128)(2,1)S(1)} collective-permute-done((bf16[512,256]{1,0:T(8,128)(2,1)S(1)}, bf16[512,256]{1,0:T(8,128)(2,1)S(1)}, u32[]{:S(2)}, u32[]{:S(2)}) %collective-permute-start.16) | collective-permute-done | bytes 262176 | tf_op jit(solution)/shard_map/ppermute | solution.py:40
  62.8 1.5 %shard_map.118 = (f32[512,256]{1,0:T(8,128)S(1)}, f32[128,896]{1,0:T(8,128)S(1)}) custom-call(f32[8,256]{1,0:T(8,128)S(1)} %shard_map.117.refs_0_.refs_1_, bf16[512,256]{1,0:T(8,128)(2,1)S(1)} %collective-permute-done.16.refs_1_.refs_2_, f32[128,896]{1,0:T(8,128)S(1)} %collective-permute-done.12.refs_2_.refs_4_, ...), custom_call_target="tpu_custom_call" | custom-call | flops 2653050112 | bytes 8487000 | tf_op jit(solution)/shard_map/pallas_call | solution.py:86
  64.4 5.1 %collective-permute-done.19.refs_5_ = f32[8,256]{1,0:T(8,128)S(1)} collective-permute-done((f32[8,256]{1,0:T(8,128)S(1)}, f32[8,256]{1,0:T(8,128)S(1)}, u32[]{:S(2)}, u32[]{:S(2)}) %collective-permute-start.19) | collective-permute-done | bytes 8224 | tf_op jit(solution)/shard_map/ppermute | solution.py:40
  69.6 0.1 shard_map.120
  69.8 1.7 %collective-permute-start.21 = (bf16[144,256]{1,0:T(8,128)(2,1)S(1)}, bf16[144,256]{1,0:T(8,128)(2,1)S(1)}, u32[]{:S(2)}, u32[]{:S(2)}) collective-permute-start(bf16[144,256]{1,0:T(8,128)(2,1)S(1)} %get-tuple-element.96), channel_id=1, source_target_pairs={{0,48},{4,52},{8,56},{12,60},{16,0},{20,4},{24,8},{28,12},{32,16},... | collective-permute-start | bytes 221192 | tf_op jit(solution)/shard_map/ppermute | solution.py:40
  71.5 4.6 %collective-permute-start.22 = (bf16[144,256]{1,0:T(8,128)(2,1)S(1)}, bf16[144,256]{1,0:T(8,128)(2,1)S(1)}, u32[]{:S(2)}, u32[]{:S(2)}) collective-permute-start(bf16[144,256]{1,0:T(8,128)(2,1)S(1)} %get-tuple-element.97), channel_id=1, source_target_pairs={{0,32},{4,36},{8,40},{12,44},{16,48},{20,52},{24,56},{28,60},{32,0... | collective-permute-start | bytes 221192 | tf_op jit(solution)/shard_map/ppermute | solution.py:40
  76.1 0.3 collective-permute-start.23
  76.4 1.5 %shard_map.121 = (bf16[256,896]{1,0:T(8,128)(2,1)}, bf16[256,896]{1,0:T(8,128)(2,1)}, f32[1,128]{1,0:T(1,128)S(1)}) custom-call(bf16[256,64]{1,0:T(8,128)(2,1)S(1)} %get-tuple-element.54.refs_0_, f32[8,896]{1,0:T(8,128)S(1)} %get-tuple-element.74.refs_6_.refs_0_.refs_9_.refs_1_, f32[8,896]{1,0:T(8,128)S(1)} %collective-permute-done.11.refs_7_.refs_1_.refs_10_.refs_2_, ...), custom_call_target="tpu_custom_call" | custom-call | flops 4614000128 | bytes 14760000 | tf_op jit(solution)/shard_map/pallas_call | solution.py:86
  77.9 4.0 %collective-permute-done.22.refs_4_ = bf16[144,256]{1,0:T(8,128)(2,1)S(1)} collective-permute-done((bf16[144,256]{1,0:T(8,128)(2,1)S(1)}, bf16[144,256]{1,0:T(8,128)(2,1)S(1)}, u32[]{:S(2)}, u32[]{:S(2)}) %collective-permute-start.22) | collective-permute-done | bytes 73760 | tf_op jit(solution)/shard_map/ppermute | solution.py:40
  81.9 0.7 collective-permute-done.23.refs_5_
  82.7 2.4 %collective-permute-start.24 = (bf16[80,256]{1,0:T(8,128)(2,1)S(1)}, bf16[80,256]{1,0:T(8,128)(2,1)S(1)}, u32[]{:S(2)}, u32[]{:S(2)}) collective-permute-start(bf16[80,256]{1,0:T(8,128)(2,1)S(1)} %get-tuple-element.100), channel_id=1, source_target_pairs={{0,8},{4,12},{8,0},{12,4},{16,24},{20,28},{24,16},{28,20},{32,40},... | collective-permute-start | bytes 122888 | tf_op jit(solution)/shard_map/ppermute | solution.py:40
  85.1 0.2 collective-permute-start.25
  85.3 2.9 %collective-permute-done.26.refs_5_ = f32[8,256]{1,0:T(8,128)S(1)} collective-permute-done((f32[8,256]{1,0:T(8,128)S(1)}, f32[8,256]{1,0:T(8,128)S(1)}, u32[]{:S(2)}, u32[]{:S(2)}) %collective-permute-start.26) | collective-permute-done | bytes 8224 | tf_op jit(solution)/shard_map/ppermute | solution.py:40
  88.2 0.8 shard_map.123
  (43 shorter events, 0.8 us)
Async XLA Ops:
  0.6 0.7 copy-start.5
  1.3 0.9 %copy-start.3 = (bf16[256,2,128]{2,1,0:T(2,128)(2,1)S(1)}, bf16[256,2,128]{2,1,0:T(2,128)(2,1)}, u32[]{:S(2)}) copy-start(bf16[256,2,128]{2,1,0:T(2,128)(2,1)} %param.10) | copy-start | bytes 393220
  2.2 2.4 %copy-start.4 = (s32[64]{0:T(128)S(1)}, s32[64]{0:T(128)}, u32[]{:S(2)}) copy-start(s32[64]{0:T(128)} %refs_1_.1) | copy-start | bytes 772
  2.5 2.9 %copy-start.6 = (bf16[1792]{0:T(1024)(128)(2,1)S(1)}, bf16[1792]{0:T(1024)(128)(2,1)}, u32[]{:S(2)}) copy-start(bf16[1792]{0:T(1024)(128)(2,1)} %param.8) | copy-start | bytes 10756
  2.5 4.0 %copy-start = (bf16[256,1792]{1,0:T(8,128)(2,1)S(1)}, bf16[256,1792]{1,0:T(8,128)(2,1)}, u32[]{:S(2)}) copy-start(bf16[256,1792]{1,0:T(8,128)(2,1)} %refs_5_.1) | copy-start | bytes 2752516
  2.5 4.0 %copy-start.1 = (bf16[256,896]{1,0:T(8,128)(2,1)S(1)}, bf16[256,896]{1,0:T(8,128)(2,1)}, u32[]{:S(2)}) copy-start(bf16[256,896]{1,0:T(8,128)(2,1)} %refs_3_.1) | copy-start | bytes 1376260
  2.5 4.0 %copy-start.2 = (bf16[256,896]{1,0:T(8,128)(2,1)S(1)}, bf16[256,896]{1,0:T(8,128)(2,1)}, u32[]{:S(2)}) copy-start(bf16[256,896]{1,0:T(8,128)(2,1)} %refs_4_.1) | copy-start | bytes 1376260
  2.5 4.0 %collective-permute-start = (bf16[64,256]{1,0:T(8,128)(2,1)S(1)}, bf16[64,256]{1,0:T(8,128)(2,1)S(1)}, u32[]{:S(2)}, u32[]{:S(2)}) collective-permute-start(bf16[64,256]{1,0:T(8,128)(2,1)S(1)} %shard_map.102.refs_0_), channel_id=1, source_target_pairs={{0,8},{4,12},{8,0},{12,4},{16,24},{20,28},{24,16},{28,20},{32,40},... | collective-permute-start | bytes 98312 | tf_op jit(solution)/shard_map/ppermute | solution.py:40
  7.1 13.8 %collective-permute-start.1 = (bf16[64,1792]{1,0:T(8,128)(2,1)S(1)}, bf16[64,1792]{1,0:T(8,128)(2,1)S(1)}, u32[]{:S(2)}, u32[]{:S(2)}) collective-permute-start(bf16[64,1792]{1,0:T(8,128)(2,1)S(1)} %get-tuple-element.57.refs_0_), channel_id=1, source_target_pairs={{0,4},{4,0},{8,12},{12,8},{16,20},{20,16},{24,28},{28,24},{32,36},... | collective-permute-start | bytes 688136 | tf_op jit(solution)/shard_map/ppermute | solution.py:40
  7.2 14.1 %collective-permute-start.6 = (bf16[128,256]{1,0:T(8,128)(2,1)S(1)}, bf16[128,256]{1,0:T(8,128)(2,1)S(1)}, u32[]{:S(2)}, u32[]{:S(2)}) collective-permute-start(bf16[128,256]{1,0:T(8,128)(2,1)S(1)} %shard_map.104.refs_0_.refs_2_), channel_id=1, source_target_pairs={{0,48},{4,52},{8,56},{12,60},{16,0},{20,4},{24,8},{28,12},{32,16},... | collective-permute-start | bytes 196616 | tf_op jit(solution)/shard_map/ppermute | solution.py:40
  13.6 10.1 %collective-permute-start.5 = (bf16[128,256]{1,0:T(8,128)(2,1)S(1)}, bf16[128,256]{1,0:T(8,128)(2,1)S(1)}, u32[]{:S(2)}, u32[]{:S(2)}) collective-permute-start(bf16[128,256]{1,0:T(8,128)(2,1)S(1)} %shard_map.104.refs_0_.refs_2_), channel_id=1, source_target_pairs={{0,32},{4,36},{8,40},{12,44},{16,48},{20,52},{24,56},{28,60},{32,0... | collective-permute-start | bytes 196616 | tf_op jit(solution)/shard_map/ppermute | solution.py:40
  14.6 9.1 %collective-permute-start.4 = (bf16[128,256]{1,0:T(8,128)(2,1)S(1)}, bf16[128,256]{1,0:T(8,128)(2,1)S(1)}, u32[]{:S(2)}, u32[]{:S(2)}) collective-permute-start(bf16[128,256]{1,0:T(8,128)(2,1)S(1)} %shard_map.104.refs_0_.refs_2_), channel_id=1, source_target_pairs={{0,16},{4,20},{8,24},{12,28},{16,32},{20,36},{24,40},{28,44},{32,4... | collective-permute-start | bytes 196616 | tf_op jit(solution)/shard_map/ppermute | solution.py:40
  17.4 3.5 %collective-permute-start.2 = (f32[1,128]{1,0:T(1,128)S(1)}, f32[1,128]{1,0:T(1,128)S(1)}, u32[]{:S(2)}, u32[]{:S(2)}) collective-permute-start(f32[1,128]{1,0:T(1,128)S(1)} %get-tuple-element.58.refs_2_), channel_id=1, source_target_pairs={{0,1},{1,0},{2,3},{3,2},{4,5},{5,4},{6,7},{7,6},{8,9},{9,8},{10,11... | collective-permute-start | bytes 1544 | tf_op jit(solution)/shard_map/ppermute | solution.py:72
  21.2 2.5 %collective-permute-start.3 = (f32[1,128]{1,0:T(1,128)S(1)}, f32[1,128]{1,0:T(1,128)S(1)}, u32[]{:S(2)}, u32[]{:S(2)}) collective-permute-start(f32[1,128]{1,0:T(1,128)S(1)} %get-tuple-element.59.refs_0_), channel_id=1, source_target_pairs={{0,4},{4,0},{8,12},{12,8},{16,20},{20,16},{24,28},{28,24},{32,36},... | collective-permute-start | bytes 1544 | tf_op jit(solution)/shard_map/ppermute | solution.py:40
  23.7 10.9 %collective-permute-start.9 = (bf16[512,256]{1,0:T(8,128)(2,1)S(1)}, bf16[512,256]{1,0:T(8,128)(2,1)S(1)}, u32[]{:S(2)}, u32[]{:S(2)}) collective-permute-start(bf16[512,256]{1,0:T(8,128)(2,1)S(1)} %get-tuple-element.60.refs_1_.refs_4_), channel_id=1, source_target_pairs={{0,64},{4,68},{8,72},{12,76},{16,80},{20,84},{24,88},{28,92},{32,9... | collective-permute-start | bytes 786440 | tf_op jit(solution)/shard_map/ppermute | solution.py:40
  27.1 9.1 %collective-permute-start.8 = (bf16[512,256]{1,0:T(8,128)(2,1)S(1)}, bf16[512,256]{1,0:T(8,128)(2,1)S(1)}, u32[]{:S(2)}, u32[]{:S(2)}) collective-permute-start(bf16[512,256]{1,0:T(8,128)(2,1)S(1)} %get-tuple-element.60.refs_1_.refs_4_), channel_id=1, source_target_pairs={{0,128},{4,132},{8,136},{12,140},{16,144},{20,148},{24,152},{28,15... | collective-permute-start | bytes 786440 | tf_op jit(solution)/shard_map/ppermute | solution.py:40
  29.1 7.4 %collective-permute-start.7 = (bf16[512,256]{1,0:T(8,128)(2,1)S(1)}, bf16[512,256]{1,0:T(8,128)(2,1)S(1)}, u32[]{:S(2)}, u32[]{:S(2)}) collective-permute-start(bf16[512,256]{1,0:T(8,128)(2,1)S(1)} %get-tuple-element.60.refs_1_.refs_4_), channel_id=1, source_target_pairs={{0,192},{4,196},{8,200},{12,204},{16,208},{20,212},{24,216},{28,22... | collective-permute-start | bytes 786440 | tf_op jit(solution)/shard_map/ppermute | solution.py:40
  29.8 6.6 %collective-permute-start.10 = (f32[1,128]{1,0:T(1,128)S(1)}, f32[1,128]{1,0:T(1,128)S(1)}, u32[]{:S(2)}, u32[]{:S(2)}) collective-permute-start(f32[1,128]{1,0:T(1,128)S(1)} %get-tuple-element.70.refs_2_), channel_id=1, source_target_pairs={{0,2},{1,3},{2,0},{3,1},{4,6},{5,7},{6,4},{7,5},{8,10},{9,11},{10,... | collective-permute-start | bytes 1544 | tf_op jit(solution)/shard_map/ppermute | solution.py:72
  36.7 1.3 %collective-permute-start.11 = (f32[8,896]{1,0:T(8,128)S(1)}, f32[8,896]{1,0:T(8,128)S(1)}, u32[]{:S(2)}, u32[]{:S(2)}) collective-permute-start(f32[8,896]{1,0:T(8,128)S(1)} %get-tuple-element.74.refs_6_.refs_0_.refs_9_.refs_1_), channel_id=1, source_target_pairs={{0,4},{4,0},{8,12},{12,8},{16,20},{20,16},{24,28},{28,24},{32,36},... | collective-permute-start | bytes 86024 | tf_op jit(solution)/shard_map/ppermute | solution.py:40
  36.8 26.0 %collective-permute-start.12 = (f32[128,896]{1,0:T(8,128)S(1)}, f32[128,896]{1,0:T(8,128)S(1)}, u32[]{:S(2)}, u32[]{:S(2)}) collective-permute-start(f32[128,896]{1,0:T(8,128)S(1)} %get-tuple-element.75.refs_3_), channel_id=1, source_target_pairs={{0,4},{4,0},{8,12},{12,8},{16,20},{20,16},{24,28},{28,24},{32,36},... | collective-permute-start | bytes 1376264 | tf_op jit(solution)/shard_map/ppermute | solution.py:40
  38.0 7.9 %collective-permute-start.14 = (f32[1,128]{1,0:T(1,128)S(1)}, f32[1,128]{1,0:T(1,128)S(1)}, u32[]{:S(2)}, u32[]{:S(2)}) collective-permute-start(f32[1,128]{1,0:T(1,128)S(1)} %shard_map.114.refs_8_), channel_id=1, source_target_pairs={{0,1},{1,0},{2,3},{3,2},{4,5},{5,4},{6,7},{7,6},{8,9},{9,8},{10,11... | collective-permute-start | bytes 1544 | tf_op jit(solution)/shard_map/ppermute | solution.py:72
  40.4 14.1 %collective-permute-start.13 = (bf16[512,256]{1,0:T(8,128)(2,1)S(1)}, bf16[512,256]{1,0:T(8,128)(2,1)S(1)}, u32[]{:S(2)}, u32[]{:S(2)}) collective-permute-start(bf16[512,256]{1,0:T(8,128)(2,1)S(1)} %get-tuple-element.79), channel_id=1, source_target_pairs={{64,0},{68,4},{72,8},{76,12},{80,16},{84,20},{88,24},{92,28},{96,3... | collective-permute-start | bytes 786440 | tf_op jit(solution)/shard_map/ppermute | solution.py:40
  46.0 5.1 %collective-permute-start.15 = (f32[1,128]{1,0:T(1,128)S(1)}, f32[1,128]{1,0:T(1,128)S(1)}, u32[]{:S(2)}, u32[]{:S(2)}) collective-permute-start(f32[1,128]{1,0:T(1,128)S(1)} %get-tuple-element.83.refs_3_), channel_id=1, source_target_pairs={{0,2},{1,3},{2,0},{3,1},{4,6},{5,7},{6,4},{7,5},{8,10},{9,11},{10,... | collective-permute-start | bytes 1544 | tf_op jit(solution)/shard_map/ppermute | solution.py:72
  48.9 13.9 %collective-permute-start.16 = (bf16[512,256]{1,0:T(8,128)(2,1)S(1)}, bf16[512,256]{1,0:T(8,128)(2,1)S(1)}, u32[]{:S(2)}, u32[]{:S(2)}) collective-permute-start(bf16[512,256]{1,0:T(8,128)(2,1)S(1)} %get-tuple-element.85), channel_id=1, source_target_pairs={{128,0},{132,4},{136,8},{140,12},{144,16},{148,20},{152,24},{156,2... | collective-permute-start | bytes 786440 | tf_op jit(solution)/shard_map/ppermute | solution.py:40
  50.3 14.1 %collective-permute-start.17 = (bf16[512,256]{1,0:T(8,128)(2,1)S(1)}, bf16[512,256]{1,0:T(8,128)(2,1)S(1)}, u32[]{:S(2)}, u32[]{:S(2)}) collective-permute-start(bf16[512,256]{1,0:T(8,128)(2,1)S(1)} %get-tuple-element.87), channel_id=1, source_target_pairs={{192,0},{196,4},{200,8},{204,12},{208,16},{212,20},{216,24},{220,2... | collective-permute-start | bytes 786440 | tf_op jit(solution)/shard_map/ppermute | solution.py:40
  54.7 9.6 %collective-permute-start.18 = (f32[8,256]{1,0:T(8,128)S(1)}, f32[8,256]{1,0:T(8,128)S(1)}, u32[]{:S(2)}, u32[]{:S(2)}) collective-permute-start(f32[8,256]{1,0:T(8,128)S(1)} %shard_map.117.refs_0_.refs_1_), channel_id=1, source_target_pairs={{0,64},{4,68},{8,72},{12,76},{16,80},{20,84},{24,88},{28,92},{32,9... | collective-permute-start | bytes 24584 | tf_op jit(solution)/shard_map/ppermute | solution.py:40
  64.3 5.2 %collective-permute-start.19 = (f32[8,256]{1,0:T(8,128)S(1)}, f32[8,256]{1,0:T(8,128)S(1)}, u32[]{:S(2)}, u32[]{:S(2)}) collective-permute-start(f32[8,256]{1,0:T(8,128)S(1)} %shard_map.119.refs_4_), channel_id=1, source_target_pairs={{0,128},{4,132},{8,136},{12,140},{16,144},{20,148},{24,152},{28,15... | collective-permute-start | bytes 24584 | tf_op jit(solution)/shard_map/ppermute | solution.py:40
  69.7 6.7 %collective-permute-start.20 = (f32[128,896]{1,0:T(8,128)S(1)}, f32[128,896]{1,0:T(8,128)S(1)}, u32[]{:S(2)}, u32[]{:S(2)}) collective-permute-start(f32[128,896]{1,0:T(8,128)S(1)} %get-tuple-element.89.refs_6_), channel_id=1, source_target_pairs={{0,4},{4,0},{8,12},{12,8},{16,20},{20,16},{24,28},{28,24},{32,36},... | collective-permute-start | bytes 1376264 | tf_op jit(solution)/shard_map/ppermute | solution.py:40
  69.8 8.1 %collective-permute-start.21 = (bf16[144,256]{1,0:T(8,128)(2,1)S(1)}, bf16[144,256]{1,0:T(8,128)(2,1)S(1)}, u32[]{:S(2)}, u32[]{:S(2)}) collective-permute-start(bf16[144,256]{1,0:T(8,128)(2,1)S(1)} %get-tuple-element.96), channel_id=1, source_target_pairs={{0,48},{4,52},{8,56},{12,60},{16,0},{20,4},{24,8},{28,12},{32,16},... | collective-permute-start | bytes 221192 | tf_op jit(solution)/shard_map/ppermute | solution.py:40
  71.5 10.4 %collective-permute-start.22 = (bf16[144,256]{1,0:T(8,128)(2,1)S(1)}, bf16[144,256]{1,0:T(8,128)(2,1)S(1)}, u32[]{:S(2)}, u32[]{:S(2)}) collective-permute-start(bf16[144,256]{1,0:T(8,128)(2,1)S(1)} %get-tuple-element.97), channel_id=1, source_target_pairs={{0,32},{4,36},{8,40},{12,44},{16,48},{20,52},{24,56},{28,60},{32,0... | collective-permute-start | bytes 221192 | tf_op jit(solution)/shard_map/ppermute | solution.py:40
  76.1 6.5 %collective-permute-start.23 = (bf16[144,256]{1,0:T(8,128)(2,1)S(1)}, bf16[144,256]{1,0:T(8,128)(2,1)S(1)}, u32[]{:S(2)}, u32[]{:S(2)}) collective-permute-start(bf16[144,256]{1,0:T(8,128)(2,1)S(1)} %get-tuple-element.98), channel_id=1, source_target_pairs={{0,16},{4,20},{8,24},{12,28},{16,32},{20,36},{24,40},{28,44},{32,4... | collective-permute-start | bytes 221192 | tf_op jit(solution)/shard_map/ppermute | solution.py:40
  82.7 5.5 %collective-permute-start.24 = (bf16[80,256]{1,0:T(8,128)(2,1)S(1)}, bf16[80,256]{1,0:T(8,128)(2,1)S(1)}, u32[]{:S(2)}, u32[]{:S(2)}) collective-permute-start(bf16[80,256]{1,0:T(8,128)(2,1)S(1)} %get-tuple-element.100), channel_id=1, source_target_pairs={{0,8},{4,12},{8,0},{12,4},{16,24},{20,28},{24,16},{28,20},{32,40},... | collective-permute-start | bytes 122888 | tf_op jit(solution)/shard_map/ppermute | solution.py:40
  85.1 3.1 %collective-permute-start.26 = (f32[8,256]{1,0:T(8,128)S(1)}, f32[8,256]{1,0:T(8,128)S(1)}, u32[]{:S(2)}, u32[]{:S(2)}) collective-permute-start(f32[8,256]{1,0:T(8,128)S(1)} %get-tuple-element.101.refs_3_), channel_id=1, source_target_pairs={{0,12},{4,8},{8,4},{12,0},{16,28},{20,24},{24,20},{28,16},{32,44},... | collective-permute-start | bytes 24584 | tf_op jit(solution)/shard_map/ppermute | solution.py:40
  85.1 3.1 %collective-permute-start.25 = (f32[8,256]{1,0:T(8,128)S(1)}, f32[8,256]{1,0:T(8,128)S(1)}, u32[]{:S(2)}, u32[]{:S(2)}) collective-permute-start(f32[8,256]{1,0:T(8,128)S(1)} %get-tuple-element.101.refs_3_), channel_id=1, source_target_pairs={{0,4},{4,0},{8,12},{12,8},{16,20},{20,16},{24,28},{28,24},{32,36},... | collective-permute-start | bytes 24584 | tf_op jit(solution)/shard_map/ppermute | solution.py:40

commit v4 on v3

--- a/solution.py
+++ b/solution.py
@@ -40,12 +40,16 @@
     return lax.ppermute(value, "ctx", pairs)
 
 
-def up_x(k):
-    return lambda x, z, c: (x + k, z, c) if x + k < NX else None
-
-
-def down_x(k):
-    return lambda x, z, c: (x - k, z, c) if x >= k else None
+def by_x(k):
+    return lambda x, z, c: ((x + k) % NX, z, c)
+
+
+def down_x(least):
+    return lambda x, z, c: (x - 1, z, c) if x >= least else None
+
+
+def last_to_first(x, z, c):
+    return (0, z, c) if x == NX - 1 else None
 
 
 def flip_x(bit):
@@ -166,8 +170,7 @@
     logit[...] = jnp.sum(jnp.where(mine, column, 0.0), axis=0, keepdims=True)
 
 
-def prepare_kernel(own, other, logit, logit_other, qt, qs, gt, logit_sum):
-    logit_sum[...] = logit[...] + logit_other[...]
+def prepare_kernel(own, other, qt, qs, gt):
     first = here()[2] == 0
     lanes = qt.shape[1]
     for h in range(own.shape[1] // HEAD_SIZE):
@@ -284,15 +287,15 @@
     return top, a, b, total
 
 
-def backward_kernel(shift, bias, pairs, qt, qs, dt, ds, ours, theirs, *refs):
-    if shift == 1:
+def backward_kernel(shift, place, bias, pairs, qt, qs, dt, ds, ours, theirs, *refs):
+    if place == 0:
         out, dq = refs
         dq[...] = jnp.zeros_like(dq)
     else:
-        if shift == 2:
+        if place == 1:
             part, part_other, *refs = refs
         dq_in, out, dq, *refs = refs
-        if shift == 2:
+        if place == 1:
             refs[0][...] = part[...] + part_other[...]
         dq[...] = dq_in[...]
     used = here()[0] >= shift
@@ -346,6 +349,10 @@
         d_queries[:, cols] = dot(hot[...], rows).astype(BF16)
 
 
+def merge_kernel(grads, received, out):
+    out[...] = (grads[...] + received[...].astype(F32)).astype(BF16)
+
+
 def add_kernel(a, b, out):
     out[...] = a[...] + b[...]
 
@@ -374,14 +381,14 @@
     return both[: TILE // 2, :] + both[TILE // 2 :, :]
 
 
-def sum_x_kernel(own, a, b, c, r0, r1, dq, keep, keep_sum, dq_out, *sends):
+def sum_x_kernel(own, a, b, r0, r1, dq, keep, keep_sum, dq_out, *sends):
     dq_out[...] = dq[...]
     size = keep.shape[0]
     router = r0[...] + r1[...]
     keep_sum[...] = router
     for i in range(4):
         at = slice(i * size, (i + 1) * size)
-        total = own[at, :] + a[at, :].astype(F32) + b[at, :].astype(F32) + c[at, :].astype(F32)
+        total = own[at, :] + a[at, :].astype(F32) + b[at, :].astype(F32)
         if i == 0:
             keep[...] = total
         else:
@@ -457,15 +464,14 @@
         us=0.6,
     )
     turned, stacked = shape((HEAD_SIZE, lanes), BF16), shape((lanes, HEAD_SIZE), BF16)
-    qt, qs, gt, logit = call(
+    qt, qs, gt = call(
         prepare_kernel,
-        (turned, stacked, turned, pair_row),
+        (turned, stacked, turned),
         qg_rows,
         move(qg_rows, flip_core),
-        logit,
-        flip_tp(logit, 1),
         us=0.25,
     )
+    logit = call(add_kernel, pair_row, logit, flip_tp(logit, 1))
     chunk, logit = call(
         join_sum_kernel,
         (shape((CHUNK, pair_width), BF16), pair_row),
@@ -474,7 +480,7 @@
         two,
         *neighbours,
     )
-    chunks = [chunk] + [move(chunk, up_x(k)) for k in (1, 2, 3)]
+    chunks = [chunk] + [move(chunk, by_x(k)) for k in (1, 2, 3)]
 
     acc_shape, stats_shape = shape((HEAD_SIZE, lanes), F32), shape((8, lanes), F32)
     state = ()
@@ -509,27 +515,16 @@
     sums = shape((TILE // 2, pair_width), F32)
     part = call(gate_part_kernel, pair_row, stats, stats_other)
 
-    received, state = {}, ()
-    for k in (1, 2, 3, 0):
+    state, order = (), (2, 3, 1, 0)
+    for k in order:
         extra, more, after = (), (), ()
-        if k == 2:
+        if k == order[1]:
             extra, more = (part, flip_tp(part, 1)), (pair_row,)
         if k == 0:
-            router = call(
-                router_kernel,
-                sums,
-                live,
-                part,
-                flip_tp(part, 2),
-                gate,
-                t_rows,
-                after=(received[1], *state),
-                us=0.7,
-            )
-            after = (router, received[2], acc_other)
+            after = (router, acc_other, far)
         grad, *state = call(
-            functools.partial(backward_kernel, k),
-            (shape((CHUNK, pair_width), F32 if k == 0 else BF16), acc_shape, *more),
+            functools.partial(backward_kernel, k, order.index(k)),
+            (shape((CHUNK, pair_width), F32 if k < 2 else BF16), acc_shape, *more),
             biases[k],
             chunks[k],
             qt,
@@ -544,17 +539,35 @@
             us=2.3,
         )
         if k == 2:
+            handed = move(grad, down_x(2))
+        if k == 3:
             part = state.pop()
-        received[k] = grad if k == 0 else move(grad, down_x(k))
+            far = move(grad, last_to_first)
+        if k == 1:
+            near = call(merge_kernel, shape((CHUNK, pair_width), BF16), grad, handed, us=0.15)
+            router = call(
+                router_kernel,
+                sums,
+                live,
+                part,
+                flip_tp(part, 2),
+                gate,
+                t_rows,
+                after=(near,),
+                us=0.15,
+            )
+            near = move(near, down_x(1))
+            router = call(add_kernel, sums, router, move(router, flip_x(1)))
     dq = state[0]
 
-    router = call(add_kernel, sums, router, move(router, flip_x(1)), after=(dq,))
     half = CHUNK // 4
     keep, keep_sum, dq, *sends = call(
         sum_x_kernel,
         (shape((half, pair_width), F32), sums, acc_shape)
         + (shape((half + TILE, pair_width), BF16),) * 3,
-        *[received[k] for k in range(NX)],
+        grad,
+        near,
+        far,
         router,
         move(router, flip_x(2)),
         dq,

time: 89.3 us -> 84.8 us (0.950)
  waiting for transfers between devices: 30.5 us -> 25 us
  starting transfers between devices: 44.7 us -> 45.7 us
    ppermute x23, waiting for transfers between devices: 28.5 us -> 22.5 us  [move(): return lax.ppermute(value, 'ctx', pairs)]
    ppermute x4, starting transfers between devices: 8.75 us -> 9.72 us  [flip_tp(): return lax.ppermute(value, 'tp', [(i, i ^ bit) for i in range(4)])]
    pallas_call x22 -> x24, Pallas kernels: 11.2 us -> 11.4 us  [call(): pl.pallas_call(body, out_shape=outs, in_specs=[ANY] * skip + list(specs o...]
  transfers between devices with their start and end apart: 27 -> 27, of which waited for: 11 -> 13; matrix products, arithmetic and copies ran while one was open for 0% -> 0% of each run, Pallas kernels for 10% -> 11%
where the time goes in v4:
time: 84.8 us; the launch traced here: 84.6 us
  starting transfers between devices  45.7 us (54%)
  waiting for transfers between devices  25 us (29%)
  Pallas kernels  11.4 us (13%)
  local copies, waits for them, and re-layouts  1.59 us (2%)
  between operations  0.91 us (1%)
    ppermute x23, starting transfers between devices, move(): return lax.ppermute(value, 'ctx', pairs)  36 us
    ppermute x23, waiting for transfers between devices, move(): return lax.ppermute(value, 'ctx', pairs)  22.5 us
    pallas_call x24, Pallas kernels, call(): pl.pallas_call(body, out_shape=outs, in_specs=[ANY] * skip + list(specs o...  11.4 us
    ppermute x4, starting transfers between devices, flip_tp(): return lax.ppermute(value, 'tp', [(i, i ^ bit) for i in range(4)])  9.72 us
    ppermute x4, waiting for transfers between devices, flip_tp(): return lax.ppermute(value, 'tp', [(i, i ^ bit) for i in range(4)])  2.58 us
  transfers between devices with their start and end apart: 27, of which 13 were waited for; matrix products, arithmetic and copies ran while one was open for 0% of the time, Pallas kernels for 11%

profile of v4, /device:TPU:2, one launch (start us, length us, event | category | flops | bytes accessed | tf_op | source)
XLA Modules:
  0.0 84.6 jit_solution(12319301281260471275)
XLA Ops:
  0.6 0.6 copy-done.5
  1.3 0.9 %copy-done.3 = bf16[256,2,128]{2,1,0:T(2,128)(2,1)S(1)} copy-done((bf16[256,2,128]{2,1,0:T(2,128)(2,1)S(1)}, bf16[256,2,128]{2,1,0:T(2,128)(2,1)}, u32[]{:S(2)}) %copy-start.3) | copy-done | bytes 131096
  2.2 0.3 shard_map.102.refs_0_
  2.5 2.0 %collective-permute-start = (bf16[64,256]{1,0:T(8,128)(2,1)S(1)}, bf16[64,256]{1,0:T(8,128)(2,1)S(1)}, u32[]{:S(2)}, u32[]{:S(2)}) collective-permute-start(bf16[64,256]{1,0:T(8,128)(2,1)S(1)} %shard_map.102.refs_0_), channel_id=1, source_target_pairs={{0,8},{4,12},{8,0},{12,4},{16,24},{20,28},{24,16},{28,20},{32,40},... | collective-permute-start | bytes 98312 | tf_op jit(solution)/shard_map/ppermute | solution.py:40
  4.6 0.8 shard_map.103
  5.4 1.1 %collective-permute-done.refs_1_ = bf16[64,256]{1,0:T(8,128)(2,1)S(1)} collective-permute-done((bf16[64,256]{1,0:T(8,128)(2,1)S(1)}, bf16[64,256]{1,0:T(8,128)(2,1)S(1)}, u32[]{:S(2)}, u32[]{:S(2)}) %collective-permute-start) | collective-permute-done | bytes 32800 | tf_op jit(solution)/shard_map/ppermute | solution.py:40
  6.6 0.5 shard_map.105
  7.2 6.4 %collective-permute-start.5 = (bf16[128,256]{1,0:T(8,128)(2,1)S(1)}, bf16[128,256]{1,0:T(8,128)(2,1)S(1)}, u32[]{:S(2)}, u32[]{:S(2)}) collective-permute-start(bf16[128,256]{1,0:T(8,128)(2,1)S(1)} %shard_map.104.refs_0_.refs_2_), channel_id=1, source_target_pairs={{0,48},{4,52},{8,56},{12,60},{16,0},{20,4},{24,8},{28,12},{32,16},... | collective-permute-start | bytes 196616 | tf_op jit(solution)/shard_map/ppermute | solution.py:40
  13.6 1.0 %collective-permute-start.4 = (bf16[128,256]{1,0:T(8,128)(2,1)S(1)}, bf16[128,256]{1,0:T(8,128)(2,1)S(1)}, u32[]{:S(2)}, u32[]{:S(2)}) collective-permute-start(bf16[128,256]{1,0:T(8,128)(2,1)S(1)} %shard_map.104.refs_0_.refs_2_), channel_id=1, source_target_pairs={{0,32},{4,36},{8,40},{12,44},{16,48},{20,52},{24,56},{28,60},{32,0... | collective-permute-start | bytes 196616 | tf_op jit(solution)/shard_map/ppermute | solution.py:40
  14.6 2.8 %collective-permute-start.3 = (bf16[128,256]{1,0:T(8,128)(2,1)S(1)}, bf16[128,256]{1,0:T(8,128)(2,1)S(1)}, u32[]{:S(2)}, u32[]{:S(2)}) collective-permute-start(bf16[128,256]{1,0:T(8,128)(2,1)S(1)} %shard_map.104.refs_0_.refs_2_), channel_id=1, source_target_pairs={{0,16},{4,20},{8,24},{12,28},{16,32},{20,36},{24,40},{28,44},{32,4... | collective-permute-start | bytes 196616 | tf_op jit(solution)/shard_map/ppermute | solution.py:40
  17.4 1.6 %collective-permute-start.1 = (f32[1,128]{1,0:T(1,128)S(1)}, f32[1,128]{1,0:T(1,128)S(1)}, u32[]{:S(2)}, u32[]{:S(2)}) collective-permute-start(f32[1,128]{1,0:T(1,128)S(1)} %get-tuple-element.56.refs_0_), channel_id=1, source_target_pairs={{0,1},{1,0},{2,3},{3,2},{4,5},{5,4},{6,7},{7,6},{8,9},{9,8},{10,11... | collective-permute-start | bytes 1544 | tf_op jit(solution)/shard_map/ppermute | solution.py:76
  19.0 2.0 %collective-permute-done.1.refs_1_ = f32[1,128]{1,0:T(1,128)S(1)} collective-permute-done((f32[1,128]{1,0:T(1,128)S(1)}, f32[1,128]{1,0:T(1,128)S(1)}, u32[]{:S(2)}, u32[]{:S(2)}) %collective-permute-start.1) | collective-permute-done | bytes 544 | tf_op jit(solution)/shard_map/ppermute | solution.py:76
  20.9 1.1 %collective-permute-done.2.refs_1_ = f32[1,128]{1,0:T(1,128)S(1)} collective-permute-done((f32[1,128]{1,0:T(1,128)S(1)}, f32[1,128]{1,0:T(1,128)S(1)}, u32[]{:S(2)}, u32[]{:S(2)}) %collective-permute-start.2) | collective-permute-done | bytes 544 | tf_op jit(solution)/shard_map/ppermute | solution.py:40
  22.1 1.6 %collective-permute-done.4.refs_4_ = bf16[128,256]{1,0:T(8,128)(2,1)S(1)} collective-permute-done((bf16[128,256]{1,0:T(8,128)(2,1)S(1)}, bf16[128,256]{1,0:T(8,128)(2,1)S(1)}, u32[]{:S(2)}, u32[]{:S(2)}) %collective-permute-start.4) | collective-permute-done | bytes 65568 | tf_op jit(solution)/shard_map/ppermute | solution.py:40
  23.7 1.6 %collective-permute-start.9 = (bf16[512,256]{1,0:T(8,128)(2,1)S(1)}, bf16[512,256]{1,0:T(8,128)(2,1)S(1)}, u32[]{:S(2)}, u32[]{:S(2)}) collective-permute-start(bf16[512,256]{1,0:T(8,128)(2,1)S(1)} %get-tuple-element.57.refs_1_.refs_4_), channel_id=1, source_target_pairs={{0,64},{4,68},{8,72},{12,76},{16,80},{20,84},{24,88},{28,92},{32,9... | collective-permute-start | bytes 786440 | tf_op jit(solution)/shard_map/ppermute | solution.py:40
  25.3 1.3 %collective-permute-start.8 = (bf16[512,256]{1,0:T(8,128)(2,1)S(1)}, bf16[512,256]{1,0:T(8,128)(2,1)S(1)}, u32[]{:S(2)}, u32[]{:S(2)}) collective-permute-start(bf16[512,256]{1,0:T(8,128)(2,1)S(1)} %get-tuple-element.57.refs_1_.refs_4_), channel_id=1, source_target_pairs={{0,128},{4,132},{8,136},{12,140},{16,144},{20,148},{24,152},{28,15... | collective-permute-start | bytes 786440 | tf_op jit(solution)/shard_map/ppermute | solution.py:40
  26.6 2.0 %collective-permute-start.6 = (bf16[512,256]{1,0:T(8,128)(2,1)S(1)}, bf16[512,256]{1,0:T(8,128)(2,1)S(1)}, u32[]{:S(2)}, u32[]{:S(2)}) collective-permute-start(bf16[512,256]{1,0:T(8,128)(2,1)S(1)} %get-tuple-element.57.refs_1_.refs_4_), channel_id=1, source_target_pairs={{0,192},{4,196},{8,200},{12,204},{16,208},{20,212},{24,216},{28,22... | collective-permute-start | bytes 786440 | tf_op jit(solution)/shard_map/ppermute | solution.py:40
  28.6 3.2 %collective-permute-start.10 = (f32[1,128]{1,0:T(1,128)S(1)}, f32[1,128]{1,0:T(1,128)S(1)}, u32[]{:S(2)}, u32[]{:S(2)}) collective-permute-start(f32[1,128]{1,0:T(1,128)S(1)} %get-tuple-element.68.refs_2_), channel_id=1, source_target_pairs={{0,2},{1,3},{2,0},{3,1},{4,6},{5,7},{6,4},{7,5},{8,10},{9,11},{10,... | collective-permute-start | bytes 1544 | tf_op jit(solution)/shard_map/ppermute | solution.py:76
  31.8 0.2 shard_map.108
  32.0 1.6 %shard_map.109 = (f32[128,896]{1,0:T(8,128)S(1)}, f32[8,896]{1,0:T(8,128)S(1)}) custom-call(f32[512,128]{1,0:T(8,128)S(1)} %get-tuple-element.62.refs_0_.refs_3_, bf16[512,256]{1,0:T(8,128)(2,1)S(1)} %get-tuple-element.57.refs_1_.refs_4_, bf16[128,896]{1,0:T(8,128)(2,1)S(1)} %get-tuple-element.59.refs_2_.refs_5_), custom_call_target="tpu_custom_call" | custom-call | flops 2537700096 | bytes 8118000 | tf_op jit(solution)/shard_map/pallas_call | solution.py:90
  33.6 1.6 %shard_map.110 = (f32[128,896]{1,0:T(8,128)S(1)}, f32[8,896]{1,0:T(8,128)S(1)}) custom-call(f32[512,128]{1,0:T(8,128)S(1)} %get-tuple-element.61.refs_0_, bf16[512,256]{1,0:T(8,128)(2,1)S(1)} %collective-permute-done.9.refs_1_, bf16[128,896]{1,0:T(8,128)(2,1)S(1)} %get-tuple-element.59.refs_2_.refs_5_, f32[128,896]{1,0:T(8,128)S(1)} %get-tuple-element.63.refs_3_, ...), custom_call_target="tpu_custom_call" | custom-call | flops 2537700096 | bytes 8118000 | tf_op jit(solution)/shard_map/pallas_call | solution.py:90
  35.2 0.8 collective-permute-done.8.refs_1_
  36.3 2.0 %collective-permute-done.6.refs_1_ = bf16[512,256]{1,0:T(8,128)(2,1)S(1)} collective-permute-done((bf16[512,256]{1,0:T(8,128)(2,1)S(1)}, bf16[512,256]{1,0:T(8,128)(2,1)S(1)}, u32[]{:S(2)}, u32[]{:S(2)}) %collective-permute-start.6) | collective-permute-done | bytes 262176 | tf_op jit(solution)/shard_map/ppermute | solution.py:40
  38.3 0.4 shard_map.113
  38.7 0.5 collective-permute-start.12
  39.2 0.7 collective-permute-done.11.refs_1_.refs_7_.refs_10_.refs_2_
  39.9 1.7 %collective-permute-start.13 = (f32[1,128]{1,0:T(1,128)S(1)}, f32[1,128]{1,0:T(1,128)S(1)}, u32[]{:S(2)}, u32[]{:S(2)}) collective-permute-start(f32[1,128]{1,0:T(1,128)S(1)} %shard_map.114.refs_8_), channel_id=1, source_target_pairs={{0,1},{1,0},{2,3},{3,2},{4,5},{5,4},{6,7},{7,6},{8,9},{9,8},{10,11... | collective-permute-start | bytes 1544 | tf_op jit(solution)/shard_map/ppermute | solution.py:76
  41.6 1.3 %collective-permute-start.14 = (bf16[512,256]{1,0:T(8,128)(2,1)S(1)}, bf16[512,256]{1,0:T(8,128)(2,1)S(1)}, u32[]{:S(2)}, u32[]{:S(2)}) collective-permute-start(bf16[512,256]{1,0:T(8,128)(2,1)S(1)} %get-tuple-element.80), channel_id=1, source_target_pairs={{128,64},{132,68},{136,72},{140,76},{144,80},{148,84},{152,88},{15... | collective-permute-start | bytes 786440 | tf_op jit(solution)/shard_map/ppermute | solution.py:40
  42.9 0.6 collective-permute-done.13.refs_9_
  43.6 3.3 %collective-permute-start.15 = (f32[1,128]{1,0:T(1,128)S(1)}, f32[1,128]{1,0:T(1,128)S(1)}, u32[]{:S(2)}, u32[]{:S(2)}) collective-permute-start(f32[1,128]{1,0:T(1,128)S(1)} %get-tuple-element.81.refs_2_), channel_id=1, source_target_pairs={{0,2},{1,3},{2,0},{3,1},{4,6},{5,7},{6,4},{7,5},{8,10},{9,11},{10,... | collective-permute-start | bytes 1544 | tf_op jit(solution)/shard_map/ppermute | solution.py:76
  46.9 0.7 collective-permute-start.17
  47.6 1.5 %shard_map.117 = (f32[512,256]{1,0:T(8,128)S(1)}, f32[128,896]{1,0:T(8,128)S(1)}) custom-call(f32[512,128]{1,0:T(8,128)S(1)} %get-tuple-element.61.refs_0_, bf16[512,256]{1,0:T(8,128)(2,1)S(1)} %collective-permute-done.9.refs_1_, bf16[128,896]{1,0:T(8,128)(2,1)S(1)} %get-tuple-element.59.refs_2_.refs_5_, ...), custom_call_target="tpu_custom_call" | custom-call | flops 2653050112 | bytes 8487000 | tf_op jit(solution)/shard_map/pallas_call | solution.py:90
  49.0 3.6 %collective-permute-done.14.refs_1_ = bf16[512,256]{1,0:T(8,128)(2,1)S(1)} collective-permute-done((bf16[512,256]{1,0:T(8,128)(2,1)S(1)}, bf16[512,256]{1,0:T(8,128)(2,1)S(1)}, u32[]{:S(2)}, u32[]{:S(2)}) %collective-permute-start.14) | collective-permute-done | bytes 262176 | tf_op jit(solution)/shard_map/ppermute | solution.py:40
  52.7 0.2 shard_map.119.refs_0_
  52.9 3.9 %collective-permute-start.18 = (bf16[512,256]{1,0:T(8,128)(2,1)S(1)}, bf16[512,256]{1,0:T(8,128)(2,1)S(1)}, u32[]{:S(2)}, u32[]{:S(2)}) collective-permute-start(bf16[512,256]{1,0:T(8,128)(2,1)S(1)} %shard_map.118.refs_0_), channel_id=1, source_target_pairs={{64,0},{68,4},{72,8},{76,12},{80,16},{84,20},{88,24},{92,28},{96,3... | collective-permute-start | bytes 786440 | tf_op jit(solution)/shard_map/ppermute | solution.py:40
  56.9 2.5 %collective-permute-start.19 = (f32[8,256]{1,0:T(8,128)S(1)}, f32[8,256]{1,0:T(8,128)S(1)}, u32[]{:S(2)}, u32[]{:S(2)}) collective-permute-start(f32[8,256]{1,0:T(8,128)S(1)} %shard_map.120.refs_0_.refs_3_), channel_id=1, source_target_pairs={{0,128},{4,132},{8,136},{12,140},{16,144},{20,148},{24,152},{28,15... | collective-permute-start | bytes 24584 | tf_op jit(solution)/shard_map/ppermute | solution.py:40
  59.4 1.5 %shard_map.121 = (f32[512,256]{1,0:T(8,128)S(1)}, f32[128,896]{1,0:T(8,128)S(1)}) custom-call(f32[8,256]{1,0:T(8,128)S(1)} %shard_map.120.refs_0_.refs_3_, f32[128,896]{1,0:T(8,128)S(1)} %collective-permute-done.12.refs_1_.refs_4_, bf16[512,256]{1,0:T(8,128)(2,1)S(1)} %collective-permute-done.17.refs_2_, f32[512,128]{1,0:T(8,128)S(1)} %get-tuple-element.62.refs_0_.refs_3_, ...), custom_call_target="tpu_custom_call" | custom-call | flops 2653050112 | bytes 8487000 | tf_op jit(solution)/shard_map/pallas_call | solution.py:90
  60.9 4.0 %collective-permute-done.19.refs_4_ = f32[8,256]{1,0:T(8,128)S(1)} collective-permute-done((f32[8,256]{1,0:T(8,128)S(1)}, f32[8,256]{1,0:T(8,128)S(1)}, u32[]{:S(2)}, u32[]{:S(2)}) %collective-permute-start.19) | collective-permute-done | bytes 8224 | tf_op jit(solution)/shard_map/ppermute | solution.py:40
  65.1 2.0 %collective-permute-start.21 = (bf16[144,256]{1,0:T(8,128)(2,1)S(1)}, bf16[144,256]{1,0:T(8,128)(2,1)S(1)}, u32[]{:S(2)}, u32[]{:S(2)}) collective-permute-start(bf16[144,256]{1,0:T(8,128)(2,1)S(1)} %get-tuple-element.94), channel_id=1, source_target_pairs={{0,48},{4,52},{8,56},{12,60},{16,0},{20,4},{24,8},{28,12},{32,16},... | collective-permute-start | bytes 221192 | tf_op jit(solution)/shard_map/ppermute | solution.py:40
  67.2 4.3 %collective-permute-start.22 = (bf16[144,256]{1,0:T(8,128)(2,1)S(1)}, bf16[144,256]{1,0:T(8,128)(2,1)S(1)}, u32[]{:S(2)}, u32[]{:S(2)}) collective-permute-start(bf16[144,256]{1,0:T(8,128)(2,1)S(1)} %get-tuple-element.95), channel_id=1, source_target_pairs={{0,32},{4,36},{8,40},{12,44},{16,48},{20,52},{24,56},{28,60},{32,0... | collective-permute-start | bytes 221192 | tf_op jit(solution)/shard_map/ppermute | solution.py:40
  71.5 0.6 collective-permute-start.23
  72.1 1.5 %shard_map.123 = (bf16[256,896]{1,0:T(8,128)(2,1)}, bf16[256,896]{1,0:T(8,128)(2,1)}, f32[1,128]{1,0:T(1,128)S(1)}) custom-call(bf16[256,64]{1,0:T(8,128)(2,1)S(1)} %get-tuple-element.53.refs_0_, f32[8,896]{1,0:T(8,128)S(1)} %get-tuple-element.72.refs_0_.refs_6_.refs_9_.refs_1_, f32[8,896]{1,0:T(8,128)S(1)} %collective-permute-done.11.refs_1_.refs_7_.refs_10_.refs_2_, ...), custom_call_target="tpu_custom_call" | custom-call | flops 4614000128 | bytes 14760000 | tf_op jit(solution)/shard_map/pallas_call | solution.py:90
  73.5 4.3 %collective-permute-done.22.refs_4_ = bf16[144,256]{1,0:T(8,128)(2,1)S(1)} collective-permute-done((bf16[144,256]{1,0:T(8,128)(2,1)S(1)}, bf16[144,256]{1,0:T(8,128)(2,1)S(1)}, u32[]{:S(2)}, u32[]{:S(2)}) %collective-permute-start.22) | collective-permute-done | bytes 73760 | tf_op jit(solution)/shard_map/ppermute | solution.py:40
  77.9 0.2 collective-permute-done.23.refs_5_
  78.1 2.5 %collective-permute-start.24 = (bf16[80,256]{1,0:T(8,128)(2,1)S(1)}, bf16[80,256]{1,0:T(8,128)(2,1)S(1)}, u32[]{:S(2)}, u32[]{:S(2)}) collective-permute-start(bf16[80,256]{1,0:T(8,128)(2,1)S(1)} %get-tuple-element.98), channel_id=1, source_target_pairs={{0,8},{4,12},{8,0},{12,4},{16,24},{20,28},{24,16},{28,20},{32,40},... | collective-permute-start | bytes 122888 | tf_op jit(solution)/shard_map/ppermute | solution.py:40
  80.7 0.2 collective-permute-start.25
  80.9 2.9 %collective-permute-done.26.refs_5_ = f32[8,256]{1,0:T(8,128)S(1)} collective-permute-done((f32[8,256]{1,0:T(8,128)S(1)}, f32[8,256]{1,0:T(8,128)S(1)}, u32[]{:S(2)}, u32[]{:S(2)}) %collective-permute-start.26) | collective-permute-done | bytes 8224 | tf_op jit(solution)/shard_map/ppermute | solution.py:40
  83.8 0.8 shard_map.125
  (45 shorter events, 1.0 us)
Async XLA Ops:
  0.6 0.7 copy-start.5
  1.3 0.9 %copy-start.3 = (bf16[256,2,128]{2,1,0:T(2,128)(2,1)S(1)}, bf16[256,2,128]{2,1,0:T(2,128)(2,1)}, u32[]{:S(2)}) copy-start(bf16[256,2,128]{2,1,0:T(2,128)(2,1)} %param.10) | copy-start | bytes 393220
  2.2 2.4 %copy-start.4 = (s32[64]{0:T(128)S(1)}, s32[64]{0:T(128)}, u32[]{:S(2)}) copy-start(s32[64]{0:T(128)} %refs_1_.1) | copy-start | bytes 772
  2.5 2.9 %copy-start.6 = (bf16[1792]{0:T(1024)(128)(2,1)S(1)}, bf16[1792]{0:T(1024)(128)(2,1)}, u32[]{:S(2)}) copy-start(bf16[1792]{0:T(1024)(128)(2,1)} %param.8) | copy-start | bytes 10756
  2.5 4.0 %copy-start = (bf16[256,1792]{1,0:T(8,128)(2,1)S(1)}, bf16[256,1792]{1,0:T(8,128)(2,1)}, u32[]{:S(2)}) copy-start(bf16[256,1792]{1,0:T(8,128)(2,1)} %refs_5_.1) | copy-start | bytes 2752516
  2.5 4.0 %copy-start.1 = (bf16[256,896]{1,0:T(8,128)(2,1)S(1)}, bf16[256,896]{1,0:T(8,128)(2,1)}, u32[]{:S(2)}) copy-start(bf16[256,896]{1,0:T(8,128)(2,1)} %refs_3_.1) | copy-start | bytes 1376260
  2.5 4.0 %copy-start.2 = (bf16[256,896]{1,0:T(8,128)(2,1)S(1)}, bf16[256,896]{1,0:T(8,128)(2,1)}, u32[]{:S(2)}) copy-start(bf16[256,896]{1,0:T(8,128)(2,1)} %refs_4_.1) | copy-start | bytes 1376260
  2.5 4.0 %collective-permute-start = (bf16[64,256]{1,0:T(8,128)(2,1)S(1)}, bf16[64,256]{1,0:T(8,128)(2,1)S(1)}, u32[]{:S(2)}, u32[]{:S(2)}) collective-permute-start(bf16[64,256]{1,0:T(8,128)(2,1)S(1)} %shard_map.102.refs_0_), channel_id=1, source_target_pairs={{0,8},{4,12},{8,0},{12,4},{16,24},{20,28},{24,16},{28,20},{32,40},... | collective-permute-start | bytes 98312 | tf_op jit(solution)/shard_map/ppermute | solution.py:40
  7.1 24.7 %collective-permute-start.7 = (bf16[64,1792]{1,0:T(8,128)(2,1)S(1)}, bf16[64,1792]{1,0:T(8,128)(2,1)S(1)}, u32[]{:S(2)}, u32[]{:S(2)}) collective-permute-start(bf16[64,1792]{1,0:T(8,128)(2,1)S(1)} %get-tuple-element.58.refs_0_), channel_id=1, source_target_pairs={{0,4},{4,0},{8,12},{12,8},{16,20},{20,16},{24,28},{28,24},{32,36},... | collective-permute-start | bytes 688136 | tf_op jit(solution)/shard_map/ppermute | solution.py:40
  7.2 14.9 %collective-permute-start.5 = (bf16[128,256]{1,0:T(8,128)(2,1)S(1)}, bf16[128,256]{1,0:T(8,128)(2,1)S(1)}, u32[]{:S(2)}, u32[]{:S(2)}) collective-permute-start(bf16[128,256]{1,0:T(8,128)(2,1)S(1)} %shard_map.104.refs_0_.refs_2_), channel_id=1, source_target_pairs={{0,48},{4,52},{8,56},{12,60},{16,0},{20,4},{24,8},{28,12},{32,16},... | collective-permute-start | bytes 196616 | tf_op jit(solution)/shard_map/ppermute | solution.py:40
  13.6 10.1 %collective-permute-start.4 = (bf16[128,256]{1,0:T(8,128)(2,1)S(1)}, bf16[128,256]{1,0:T(8,128)(2,1)S(1)}, u32[]{:S(2)}, u32[]{:S(2)}) collective-permute-start(bf16[128,256]{1,0:T(8,128)(2,1)S(1)} %shard_map.104.refs_0_.refs_2_), channel_id=1, source_target_pairs={{0,32},{4,36},{8,40},{12,44},{16,48},{20,52},{24,56},{28,60},{32,0... | collective-permute-start | bytes 196616 | tf_op jit(solution)/shard_map/ppermute | solution.py:40
  14.6 9.1 %collective-permute-start.3 = (bf16[128,256]{1,0:T(8,128)(2,1)S(1)}, bf16[128,256]{1,0:T(8,128)(2,1)S(1)}, u32[]{:S(2)}, u32[]{:S(2)}) collective-permute-start(bf16[128,256]{1,0:T(8,128)(2,1)S(1)} %shard_map.104.refs_0_.refs_2_), channel_id=1, source_target_pairs={{0,16},{4,20},{8,24},{12,28},{16,32},{20,36},{24,40},{28,44},{32,4... | collective-permute-start | bytes 196616 | tf_op jit(solution)/shard_map/ppermute | solution.py:40
  17.4 3.5 %collective-permute-start.1 = (f32[1,128]{1,0:T(1,128)S(1)}, f32[1,128]{1,0:T(1,128)S(1)}, u32[]{:S(2)}, u32[]{:S(2)}) collective-permute-start(f32[1,128]{1,0:T(1,128)S(1)} %get-tuple-element.56.refs_0_), channel_id=1, source_target_pairs={{0,1},{1,0},{2,3},{3,2},{4,5},{5,4},{6,7},{7,6},{8,9},{9,8},{10,11... | collective-permute-start | bytes 1544 | tf_op jit(solution)/shard_map/ppermute | solution.py:76
  20.9 1.1 %collective-permute-start.2 = (f32[1,128]{1,0:T(1,128)S(1)}, f32[1,128]{1,0:T(1,128)S(1)}, u32[]{:S(2)}, u32[]{:S(2)}) collective-permute-start(f32[1,128]{1,0:T(1,128)S(1)} %shard_map.106.refs_0_), channel_id=1, source_target_pairs={{0,4},{4,0},{8,12},{12,8},{16,20},{20,16},{24,28},{28,24},{32,36},... | collective-permute-start | bytes 1544 | tf_op jit(solution)/shard_map/ppermute | solution.py:40
  23.7 9.9 %collective-permute-start.9 = (bf16[512,256]{1,0:T(8,128)(2,1)S(1)}, bf16[512,256]{1,0:T(8,128)(2,1)S(1)}, u32[]{:S(2)}, u32[]{:S(2)}) collective-permute-start(bf16[512,256]{1,0:T(8,128)(2,1)S(1)} %get-tuple-element.57.refs_1_.refs_4_), channel_id=1, source_target_pairs={{0,64},{4,68},{8,72},{12,76},{16,80},{20,84},{24,88},{28,92},{32,9... | collective-permute-start | bytes 786440 | tf_op jit(solution)/shard_map/ppermute | solution.py:40
  25.3 10.8 %collective-permute-start.8 = (bf16[512,256]{1,0:T(8,128)(2,1)S(1)}, bf16[512,256]{1,0:T(8,128)(2,1)S(1)}, u32[]{:S(2)}, u32[]{:S(2)}) collective-permute-start(bf16[512,256]{1,0:T(8,128)(2,1)S(1)} %get-tuple-element.57.refs_1_.refs_4_), channel_id=1, source_target_pairs={{0,128},{4,132},{8,136},{12,140},{16,144},{20,148},{24,152},{28,15... | collective-permute-start | bytes 786440 | tf_op jit(solution)/shard_map/ppermute | solution.py:40
  26.6 11.7 %collective-permute-start.6 = (bf16[512,256]{1,0:T(8,128)(2,1)S(1)}, bf16[512,256]{1,0:T(8,128)(2,1)S(1)}, u32[]{:S(2)}, u32[]{:S(2)}) collective-permute-start(bf16[512,256]{1,0:T(8,128)(2,1)S(1)} %get-tuple-element.57.refs_1_.refs_4_), channel_id=1, source_target_pairs={{0,192},{4,196},{8,200},{12,204},{16,208},{20,212},{24,216},{28,22... | collective-permute-start | bytes 786440 | tf_op jit(solution)/shard_map/ppermute | solution.py:40
  28.6 7.5 %collective-permute-start.10 = (f32[1,128]{1,0:T(1,128)S(1)}, f32[1,128]{1,0:T(1,128)S(1)}, u32[]{:S(2)}, u32[]{:S(2)}) collective-permute-start(f32[1,128]{1,0:T(1,128)S(1)} %get-tuple-element.68.refs_2_), channel_id=1, source_target_pairs={{0,2},{1,3},{2,0},{3,1},{4,6},{5,7},{6,4},{7,5},{8,10},{9,11},{10,... | collective-permute-start | bytes 1544 | tf_op jit(solution)/shard_map/ppermute | solution.py:76
  38.6 1.3 %collective-permute-start.11 = (f32[8,896]{1,0:T(8,128)S(1)}, f32[8,896]{1,0:T(8,128)S(1)}, u32[]{:S(2)}, u32[]{:S(2)}) collective-permute-start(f32[8,896]{1,0:T(8,128)S(1)} %get-tuple-element.72.refs_0_.refs_6_.refs_9_.refs_1_), channel_id=1, source_target_pairs={{0,4},{4,0},{8,12},{12,8},{16,20},{20,16},{24,28},{28,24},{32,36},... | collective-permute-start | bytes 86024 | tf_op jit(solution)/shard_map/ppermute | solution.py:40
  38.7 20.7 %collective-permute-start.12 = (f32[128,896]{1,0:T(8,128)S(1)}, f32[128,896]{1,0:T(8,128)S(1)}, u32[]{:S(2)}, u32[]{:S(2)}) collective-permute-start(f32[128,896]{1,0:T(8,128)S(1)} %get-tuple-element.73.refs_3_), channel_id=1, source_target_pairs={{0,4},{4,0},{8,12},{12,8},{16,20},{20,16},{24,28},{28,24},{32,36},... | collective-permute-start | bytes 1376264 | tf_op jit(solution)/shard_map/ppermute | solution.py:40
  39.9 3.6 %collective-permute-start.13 = (f32[1,128]{1,0:T(1,128)S(1)}, f32[1,128]{1,0:T(1,128)S(1)}, u32[]{:S(2)}, u32[]{:S(2)}) collective-permute-start(f32[1,128]{1,0:T(1,128)S(1)} %shard_map.114.refs_8_), channel_id=1, source_target_pairs={{0,1},{1,0},{2,3},{3,2},{4,5},{5,4},{6,7},{7,6},{8,9},{9,8},{10,11... | collective-permute-start | bytes 1544 | tf_op jit(solution)/shard_map/ppermute | solution.py:76
  41.6 11.0 %collective-permute-start.14 = (bf16[512,256]{1,0:T(8,128)(2,1)S(1)}, bf16[512,256]{1,0:T(8,128)(2,1)S(1)}, u32[]{:S(2)}, u32[]{:S(2)}) collective-permute-start(bf16[512,256]{1,0:T(8,128)(2,1)S(1)} %get-tuple-element.80), channel_id=1, source_target_pairs={{128,64},{132,68},{136,72},{140,76},{144,80},{148,84},{152,88},{15... | collective-permute-start | bytes 786440 | tf_op jit(solution)/shard_map/ppermute | solution.py:40
  43.6 9.1 %collective-permute-start.15 = (f32[1,128]{1,0:T(1,128)S(1)}, f32[1,128]{1,0:T(1,128)S(1)}, u32[]{:S(2)}, u32[]{:S(2)}) collective-permute-start(f32[1,128]{1,0:T(1,128)S(1)} %get-tuple-element.81.refs_2_), channel_id=1, source_target_pairs={{0,2},{1,3},{2,0},{3,1},{4,6},{5,7},{6,4},{7,5},{8,10},{9,11},{10,... | collective-permute-start | bytes 1544 | tf_op jit(solution)/shard_map/ppermute | solution.py:76
  46.9 12.5 %collective-permute-start.17 = (bf16[512,256]{1,0:T(8,128)(2,1)S(1)}, bf16[512,256]{1,0:T(8,128)(2,1)S(1)}, u32[]{:S(2)}, u32[]{:S(2)}) collective-permute-start(bf16[512,256]{1,0:T(8,128)(2,1)S(1)} %get-tuple-element.83), channel_id=1, source_target_pairs={{192,0},{196,4},{200,8},{204,12},{208,16},{212,20},{216,24},{220,2... | collective-permute-start | bytes 786440 | tf_op jit(solution)/shard_map/ppermute | solution.py:40
  52.8 4.0 %collective-permute-start.16 = (f32[8,256]{1,0:T(8,128)S(1)}, f32[8,256]{1,0:T(8,128)S(1)}, u32[]{:S(2)}, u32[]{:S(2)}) collective-permute-start(f32[8,256]{1,0:T(8,128)S(1)} %shard_map.119.refs_0_), channel_id=1, source_target_pairs={{0,64},{4,68},{8,72},{12,76},{16,80},{20,84},{24,88},{28,92},{32,9... | collective-permute-start | bytes 24584 | tf_op jit(solution)/shard_map/ppermute | solution.py:40
  52.9 12.0 %collective-permute-start.18 = (bf16[512,256]{1,0:T(8,128)(2,1)S(1)}, bf16[512,256]{1,0:T(8,128)(2,1)S(1)}, u32[]{:S(2)}, u32[]{:S(2)}) collective-permute-start(bf16[512,256]{1,0:T(8,128)(2,1)S(1)} %shard_map.118.refs_0_), channel_id=1, source_target_pairs={{64,0},{68,4},{72,8},{76,12},{80,16},{84,20},{88,24},{92,28},{96,3... | collective-permute-start | bytes 786440 | tf_op jit(solution)/shard_map/ppermute | solution.py:40
  56.9 8.1 %collective-permute-start.19 = (f32[8,256]{1,0:T(8,128)S(1)}, f32[8,256]{1,0:T(8,128)S(1)}, u32[]{:S(2)}, u32[]{:S(2)}) collective-permute-start(f32[8,256]{1,0:T(8,128)S(1)} %shard_map.120.refs_0_.refs_3_), channel_id=1, source_target_pairs={{0,128},{4,132},{8,136},{12,140},{16,144},{20,148},{24,152},{28,15... | collective-permute-start | bytes 24584 | tf_op jit(solution)/shard_map/ppermute | solution.py:40
  65.0 7.0 %collective-permute-start.20 = (f32[128,896]{1,0:T(8,128)S(1)}, f32[128,896]{1,0:T(8,128)S(1)}, u32[]{:S(2)}, u32[]{:S(2)}) collective-permute-start(f32[128,896]{1,0:T(8,128)S(1)} %get-tuple-element.87.refs_6_), channel_id=1, source_target_pairs={{0,4},{4,0},{8,12},{12,8},{16,20},{20,16},{24,28},{28,24},{32,36},... | collective-permute-start | bytes 1376264 | tf_op jit(solution)/shard_map/ppermute | solution.py:40
  65.1 8.4 %collective-permute-start.21 = (bf16[144,256]{1,0:T(8,128)(2,1)S(1)}, bf16[144,256]{1,0:T(8,128)(2,1)S(1)}, u32[]{:S(2)}, u32[]{:S(2)}) collective-permute-start(bf16[144,256]{1,0:T(8,128)(2,1)S(1)} %get-tuple-element.94), channel_id=1, source_target_pairs={{0,48},{4,52},{8,56},{12,60},{16,0},{20,4},{24,8},{28,12},{32,16},... | collective-permute-start | bytes 221192 | tf_op jit(solution)/shard_map/ppermute | solution.py:40
  67.2 10.7 %collective-permute-start.22 = (bf16[144,256]{1,0:T(8,128)(2,1)S(1)}, bf16[144,256]{1,0:T(8,128)(2,1)S(1)}, u32[]{:S(2)}, u32[]{:S(2)}) collective-permute-start(bf16[144,256]{1,0:T(8,128)(2,1)S(1)} %get-tuple-element.95), channel_id=1, source_target_pairs={{0,32},{4,36},{8,40},{12,44},{16,48},{20,52},{24,56},{28,60},{32,0... | collective-permute-start | bytes 221192 | tf_op jit(solution)/shard_map/ppermute | solution.py:40
  71.5 6.6 %collective-permute-start.23 = (bf16[144,256]{1,0:T(8,128)(2,1)S(1)}, bf16[144,256]{1,0:T(8,128)(2,1)S(1)}, u32[]{:S(2)}, u32[]{:S(2)}) collective-permute-start(bf16[144,256]{1,0:T(8,128)(2,1)S(1)} %get-tuple-element.96), channel_id=1, source_target_pairs={{0,16},{4,20},{8,24},{12,28},{16,32},{20,36},{24,40},{28,44},{32,4... | collective-permute-start | bytes 221192 | tf_op jit(solution)/shard_map/ppermute | solution.py:40
  78.1 5.6 %collective-permute-start.24 = (bf16[80,256]{1,0:T(8,128)(2,1)S(1)}, bf16[80,256]{1,0:T(8,128)(2,1)S(1)}, u32[]{:S(2)}, u32[]{:S(2)}) collective-permute-start(bf16[80,256]{1,0:T(8,128)(2,1)S(1)} %get-tuple-element.98), channel_id=1, source_target_pairs={{0,8},{4,12},{8,0},{12,4},{16,24},{20,28},{24,16},{28,20},{32,40},... | collective-permute-start | bytes 122888 | tf_op jit(solution)/shard_map/ppermute | solution.py:40
  80.7 3.1 %collective-permute-start.26 = (f32[8,256]{1,0:T(8,128)S(1)}, f32[8,256]{1,0:T(8,128)S(1)}, u32[]{:S(2)}, u32[]{:S(2)}) collective-permute-start(f32[8,256]{1,0:T(8,128)S(1)} %get-tuple-element.99.refs_3_), channel_id=1, source_target_pairs={{0,12},{4,8},{8,4},{12,0},{16,28},{20,24},{24,20},{28,16},{32,44},... | collective-permute-start | bytes 24584 | tf_op jit(solution)/shard_map/ppermute | solution.py:40
  80.7 3.1 %collective-permute-start.25 = (f32[8,256]{1,0:T(8,128)S(1)}, f32[8,256]{1,0:T(8,128)S(1)}, u32[]{:S(2)}, u32[]{:S(2)}) collective-permute-start(f32[8,256]{1,0:T(8,128)S(1)} %get-tuple-element.99.refs_3_), channel_id=1, source_target_pairs={{0,4},{4,0},{8,12},{12,8},{16,20},{20,16},{24,28},{28,24},{32,36},... | collective-permute-start | bytes 24584 | tf_op jit(solution)/shard_map/ppermute | solution.py:40

commit v5 on v4

--- a/solution.py
+++ b/solution.py
@@ -381,38 +381,39 @@
     return both[: TILE // 2, :] + both[TILE // 2 :, :]
 
 
-def sum_x_kernel(own, a, b, r0, r1, dq, keep, keep_sum, dq_out, *sends):
+def sum_x_kernel(own, a, b, r0, r1, keep, router, send):
+    size = keep.shape[0]
+    router[...] = r0[...] + r1[...]
+    for i in range(CHUNK // SLOTS):
+        at = slice(i * SLOTS, (i + 1) * SLOTS)
+        to = slice(i // 2 * SLOTS, (i // 2 + 1) * SLOTS)
+        total = own[at, :] + a[at, :].astype(F32) + b[at, :].astype(F32)
+        if i % 2 == 0:
+            keep[to, :] = total
+        else:
+            send[to, :] = total.astype(BF16)
+    put_sum(send, size, router[...])
+
+
+def sum_z_kernel(own, a, r0, r1, r2, dq, keep, router, dq_out, *sends):
     dq_out[...] = dq[...]
     size = keep.shape[0]
-    router = r0[...] + r1[...]
-    keep_sum[...] = router
-    for i in range(4):
-        at = slice(i * size, (i + 1) * size)
-        total = own[at, :] + a[at, :].astype(F32) + b[at, :].astype(F32)
-        if i == 0:
-            keep[...] = total
-        else:
-            sends[i - 1][:size, :] = total.astype(BF16)
-            put_sum(sends[i - 1], size, router)
-
-
-def sum_z_kernel(own, own_sum, a, b, c, keep, keep_sum, send):
-    size = keep.shape[0]
     full = own.shape[0]
-    parts = [ref[:full, :].astype(F32) for ref in (a, b, c)]
-    total = own[...] + parts[0] + parts[1] + parts[2]
-    router = own_sum[...] + get_sum(a, full) + get_sum(b, full) + get_sum(c, full)
-    keep_sum[...] = router
+    total = own[...] + a[:full, :].astype(F32)
+    router[...] = r0[...] + get_sum(a, full) + r1[...] + r2[...]
     keep[...] = total[:size, :]
-    send[:size, :] = total[size:, :].astype(BF16)
-    put_sum(send, size, router)
-
-
-def last_kernel(hot, own, a, r0, r1, r2, out, router):
-    rows = own[...] + a[:SLOTS, :].astype(F32)
+    for i, send in enumerate(sends, 1):
+        send[:size, :] = total[i * size : (i + 1) * size, :].astype(BF16)
+        put_sum(send, size, router[...])
+
+
+def last_kernel(hot, own, r0, a, b, c, out, router):
+    rows, total = own[...], r0[...]
+    for part in (a, b, c):
+        rows = rows + part[:SLOTS, :].astype(F32)
+        total = total + get_sum(part, SLOTS)
     rows = jnp.concatenate([rows[:, :HEAD_SIZE], rows[:, HEAD_SIZE:]], axis=0).astype(BF16)
     out[...] = dot(hot[...], rows).astype(BF16)
-    total = r0[...] + get_sum(a, SLOTS) + r1[...] + r2[...]
     width = total.shape[1]
     for r in range(router.shape[0] // width):
         router[pl.ds(r * width, width)] = total[r, :]
@@ -506,7 +507,7 @@
             qt,
             *extra,
             *state,
-            us=2.2,
+            us=0.3,
         )
     acc, stats = state
     stats_other = move(stats, flip_core)
@@ -560,18 +561,31 @@
             router = call(add_kernel, sums, router, move(router, flip_x(1)))
     dq = state[0]
 
-    half = CHUNK // 4
-    keep, keep_sum, dq, *sends = call(
+    half = CHUNK // 2
+    keep, router, send = call(
         sum_x_kernel,
-        (shape((half, pair_width), F32), sums, acc_shape)
-        + (shape((half + TILE, pair_width), BF16),) * 3,
+        (
+            shape((half, pair_width), F32),
+            sums,
+            shape((half + TILE, pair_width), BF16),
+        ),
         grad,
         near,
         far,
         router,
         move(router, flip_x(2)),
+        us=0.12,
+    )
+    keep, router, dq, *sends = call(
+        sum_z_kernel,
+        (shape((SLOTS, pair_width), F32), sums, acc_shape)
+        + (shape((SLOTS + TILE, pair_width), BF16),) * 3,
+        keep,
+        move(send, flip_z),
+        router,
+        move(router, flip_core),
+        move(router, flip_both),
         dq,
-        us=0.12,
     )
     routed, d_queries, ready = call(
         rows_kernel,
@@ -584,30 +598,16 @@
         gate,
         dq,
         move(dq, flip_core),
-        us=4.0,
-    )
-    keep, keep_sum, send = call(
-        sum_z_kernel,
-        (
-            shape((SLOTS, pair_width), F32),
-            sums,
-            shape((SLOTS + TILE, pair_width), BF16),
-        ),
-        keep,
-        keep_sum,
-        *[move(sends[i], by_z(-k)) for i, k in enumerate((2, 4, 6))],
-        after=(ready,),
-    )
-    got = move(send, flip_z)
+        us=0.1,
+    )
     pair_grads, router_grad = call(
         last_kernel,
         (shape((2 * count, HEAD_SIZE), BF16), shape((features,), F32)),
         both_hot,
         keep,
-        got,
-        keep_sum,
-        move(keep_sum, flip_core),
-        move(keep_sum, flip_both),
+        router,
+        *[move(sends[i], by_z(-k)) for i, k in enumerate((2, 4, 6))],
+        after=(ready,),
         us=1.4,
     )
     return routed, d_queries, pair_grads.reshape(keys_values.shape), router_grad

time: 84.8 us -> 84 us (level)
  starting transfers between devices: 45.7 us -> 44.6 us
    ppermute x23, starting transfers between devices: 36 us -> 34.8 us  [move(): return lax.ppermute(value, 'ctx', pairs)]
  transfers between devices with their start and end apart: 27 -> 27, of which waited for: 13 -> 13; matrix products, arithmetic and copies ran while one was open for 0% -> 0% of each run, Pallas kernels for 11% -> 12%
where the time goes in v5:
time: 84 us; the launch traced here: 83.8 us
  starting transfers between devices  44.6 us (53%)
  waiting for transfers between devices  25.3 us (30%)
  Pallas kernels  11.4 us (14%)
  local copies, waits for them, and re-layouts  1.59 us (2%)
  between operations  0.89 us (1%)
    ppermute x23, starting transfers between devices, move(): return lax.ppermute(value, 'ctx', pairs)  34.8 us
    ppermute x23, waiting for transfers between devices, move(): return lax.ppermute(value, 'ctx', pairs)  22.7 us
    pallas_call x24, Pallas kernels, call(): pl.pallas_call(body, out_shape=outs, in_specs=[ANY] * skip + list(specs o...  11.4 us
    ppermute x4, starting transfers between devices, flip_tp(): return lax.ppermute(value, 'tp', [(i, i ^ bit) for i in range(4)])  9.8 us
    ppermute x4, waiting for transfers between devices, flip_tp(): return lax.ppermute(value, 'tp', [(i, i ^ bit) for i in range(4)])  2.58 us
  transfers between devices with their start and end apart: 27, of which 13 were waited for; matrix products, arithmetic and copies ran while one was open for 0% of the time, Pallas kernels for 12%

profile of v5, /device:TPU:2, one launch (start us, length us, event | category | flops | bytes accessed | tf_op | source)
XLA Modules:
  0.0 83.8 jit_solution(2615628170383917947)
XLA Ops:
  0.6 0.6 copy-done.5
  1.3 0.9 %copy-done.3 = bf16[256,2,128]{2,1,0:T(2,128)(2,1)S(1)} copy-done((bf16[256,2,128]{2,1,0:T(2,128)(2,1)S(1)}, bf16[256,2,128]{2,1,0:T(2,128)(2,1)}, u32[]{:S(2)}) %copy-start.3) | copy-done | bytes 131096
  2.2 0.3 shard_map.102.refs_0_
  2.5 2.0 %collective-permute-start = (bf16[64,256]{1,0:T(8,128)(2,1)S(1)}, bf16[64,256]{1,0:T(8,128)(2,1)S(1)}, u32[]{:S(2)}, u32[]{:S(2)}) collective-permute-start(bf16[64,256]{1,0:T(8,128)(2,1)S(1)} %shard_map.102.refs_0_), channel_id=1, source_target_pairs={{0,8},{4,12},{8,0},{12,4},{16,24},{20,28},{24,16},{28,20},{32,40},... | collective-permute-start | bytes 98312 | tf_op jit(solution)/shard_map/ppermute | solution.py:40
  4.6 0.8 %shard_map.103 = (f32[1,128]{1,0:T(1,128)S(1)}, bf16[256,64]{1,0:T(8,128)(2,1)S(1)}, bf16[512,128]{1,0:T(8,128)(2,1)S(1)}, f32[512,128]{1,0:T(8,128)S(1)}, f32[5...) custom-call(bf16[64,256]{1,0:T(8,128)(2,1)S(1)} %shard_map.102.refs_0_, s32[64]{0:T(128)S(1)} %copy-done.4, ...), custom_call_target="tpu_custom_call" | custom-call | flops 1153500032 | bytes 3690000 | tf_op jit(solution)/shard_map/pallas_call | solution.py:90
  5.4 1.1 %collective-permute-done.refs_1_ = bf16[64,256]{1,0:T(8,128)(2,1)S(1)} collective-permute-done((bf16[64,256]{1,0:T(8,128)(2,1)S(1)}, bf16[64,256]{1,0:T(8,128)(2,1)S(1)}, u32[]{:S(2)}, u32[]{:S(2)}) %collective-permute-start) | collective-permute-done | bytes 32800 | tf_op jit(solution)/shard_map/ppermute | solution.py:40
  6.6 6.3 %collective-permute-start.5 = (bf16[128,256]{1,0:T(8,128)(2,1)S(1)}, bf16[128,256]{1,0:T(8,128)(2,1)S(1)}, u32[]{:S(2)}, u32[]{:S(2)}) collective-permute-start(bf16[128,256]{1,0:T(8,128)(2,1)S(1)} %shard_map.104.refs_0_.refs_2_), channel_id=1, source_target_pairs={{0,48},{4,52},{8,56},{12,60},{16,0},{20,4},{24,8},{28,12},{32,16},... | collective-permute-start | bytes 196616 | tf_op jit(solution)/shard_map/ppermute | solution.py:40
  12.9 1.0 %collective-permute-start.4 = (bf16[128,256]{1,0:T(8,128)(2,1)S(1)}, bf16[128,256]{1,0:T(8,128)(2,1)S(1)}, u32[]{:S(2)}, u32[]{:S(2)}) collective-permute-start(bf16[128,256]{1,0:T(8,128)(2,1)S(1)} %shard_map.104.refs_0_.refs_2_), channel_id=1, source_target_pairs={{0,32},{4,36},{8,40},{12,44},{16,48},{20,52},{24,56},{28,60},{32,0... | collective-permute-start | bytes 196616 | tf_op jit(solution)/shard_map/ppermute | solution.py:40
  13.8 2.8 %collective-permute-start.3 = (bf16[128,256]{1,0:T(8,128)(2,1)S(1)}, bf16[128,256]{1,0:T(8,128)(2,1)S(1)}, u32[]{:S(2)}, u32[]{:S(2)}) collective-permute-start(bf16[128,256]{1,0:T(8,128)(2,1)S(1)} %shard_map.104.refs_0_.refs_2_), channel_id=1, source_target_pairs={{0,16},{4,20},{8,24},{12,28},{16,32},{20,36},{24,40},{28,44},{32,4... | collective-permute-start | bytes 196616 | tf_op jit(solution)/shard_map/ppermute | solution.py:40
  16.7 0.5 shard_map.105
  17.3 1.7 %collective-permute-start.1 = (f32[1,128]{1,0:T(1,128)S(1)}, f32[1,128]{1,0:T(1,128)S(1)}, u32[]{:S(2)}, u32[]{:S(2)}) collective-permute-start(f32[1,128]{1,0:T(1,128)S(1)} %get-tuple-element.56.refs_0_), channel_id=1, source_target_pairs={{0,1},{1,0},{2,3},{3,2},{4,5},{5,4},{6,7},{7,6},{8,9},{9,8},{10,11... | collective-permute-start | bytes 1544 | tf_op jit(solution)/shard_map/ppermute | solution.py:76
  19.0 2.0 %collective-permute-done.1.refs_1_ = f32[1,128]{1,0:T(1,128)S(1)} collective-permute-done((f32[1,128]{1,0:T(1,128)S(1)}, f32[1,128]{1,0:T(1,128)S(1)}, u32[]{:S(2)}, u32[]{:S(2)}) %collective-permute-start.1) | collective-permute-done | bytes 544 | tf_op jit(solution)/shard_map/ppermute | solution.py:76
  20.9 1.1 %collective-permute-done.2.refs_1_ = f32[1,128]{1,0:T(1,128)S(1)} collective-permute-done((f32[1,128]{1,0:T(1,128)S(1)}, f32[1,128]{1,0:T(1,128)S(1)}, u32[]{:S(2)}, u32[]{:S(2)}) %collective-permute-start.2) | collective-permute-done | bytes 544 | tf_op jit(solution)/shard_map/ppermute | solution.py:40
  22.1 1.6 %collective-permute-start.9 = (bf16[512,256]{1,0:T(8,128)(2,1)S(1)}, bf16[512,256]{1,0:T(8,128)(2,1)S(1)}, u32[]{:S(2)}, u32[]{:S(2)}) collective-permute-start(bf16[512,256]{1,0:T(8,128)(2,1)S(1)} %get-tuple-element.57.refs_1_.refs_4_), channel_id=1, source_target_pairs={{0,64},{4,68},{8,72},{12,76},{16,80},{20,84},{24,88},{28,92},{32,9... | collective-permute-start | bytes 786440 | tf_op jit(solution)/shard_map/ppermute | solution.py:40
  23.7 1.1 %collective-permute-start.8 = (bf16[512,256]{1,0:T(8,128)(2,1)S(1)}, bf16[512,256]{1,0:T(8,128)(2,1)S(1)}, u32[]{:S(2)}, u32[]{:S(2)}) collective-permute-start(bf16[512,256]{1,0:T(8,128)(2,1)S(1)} %get-tuple-element.57.refs_1_.refs_4_), channel_id=1, source_target_pairs={{0,128},{4,132},{8,136},{12,140},{16,144},{20,148},{24,152},{28,15... | collective-permute-start | bytes 786440 | tf_op jit(solution)/shard_map/ppermute | solution.py:40
  24.8 2.2 %collective-permute-start.6 = (bf16[512,256]{1,0:T(8,128)(2,1)S(1)}, bf16[512,256]{1,0:T(8,128)(2,1)S(1)}, u32[]{:S(2)}, u32[]{:S(2)}) collective-permute-start(bf16[512,256]{1,0:T(8,128)(2,1)S(1)} %get-tuple-element.57.refs_1_.refs_4_), channel_id=1, source_target_pairs={{0,192},{4,196},{8,200},{12,204},{16,208},{20,212},{24,216},{28,22... | collective-permute-start | bytes 786440 | tf_op jit(solution)/shard_map/ppermute | solution.py:40
  26.9 3.2 %collective-permute-start.10 = (f32[1,128]{1,0:T(1,128)S(1)}, f32[1,128]{1,0:T(1,128)S(1)}, u32[]{:S(2)}, u32[]{:S(2)}) collective-permute-start(f32[1,128]{1,0:T(1,128)S(1)} %get-tuple-element.68.refs_2_), channel_id=1, source_target_pairs={{0,2},{1,3},{2,0},{3,1},{4,6},{5,7},{6,4},{7,5},{8,10},{9,11},{10,... | collective-permute-start | bytes 1544 | tf_op jit(solution)/shard_map/ppermute | solution.py:76
  30.1 0.2 shard_map.108
  30.4 1.6 %shard_map.109 = (f32[128,896]{1,0:T(8,128)S(1)}, f32[8,896]{1,0:T(8,128)S(1)}) custom-call(f32[512,128]{1,0:T(8,128)S(1)} %get-tuple-element.62.refs_0_.refs_3_, bf16[512,256]{1,0:T(8,128)(2,1)S(1)} %get-tuple-element.57.refs_1_.refs_4_, bf16[128,896]{1,0:T(8,128)(2,1)S(1)} %get-tuple-element.59.refs_2_.refs_5_), custom_call_target="tpu_custom_call" | custom-call | flops 346049984 | bytes 1107000 | tf_op jit(solution)/shard_map/pallas_call | solution.py:90
  32.0 1.6 %shard_map.110 = (f32[128,896]{1,0:T(8,128)S(1)}, f32[8,896]{1,0:T(8,128)S(1)}) custom-call(f32[512,128]{1,0:T(8,128)S(1)} %get-tuple-element.61.refs_0_, bf16[512,256]{1,0:T(8,128)(2,1)S(1)} %collective-permute-done.9.refs_1_, bf16[128,896]{1,0:T(8,128)(2,1)S(1)} %get-tuple-element.59.refs_2_.refs_5_, f32[128,896]{1,0:T(8,128)S(1)} %get-tuple-element.63.refs_3_, ...), custom_call_target="tpu_custom_call" | custom-call | flops 346049984 | bytes 1107000 | tf_op jit(solution)/shard_map/pallas_call | solution.py:90
  33.6 0.8 collective-permute-done.8.refs_1_
  34.6 3.7 %collective-permute-done.6.refs_1_ = bf16[512,256]{1,0:T(8,128)(2,1)S(1)} collective-permute-done((bf16[512,256]{1,0:T(8,128)(2,1)S(1)}, bf16[512,256]{1,0:T(8,128)(2,1)S(1)}, u32[]{:S(2)}, u32[]{:S(2)}) %collective-permute-start.6) | collective-permute-done | bytes 262176 | tf_op jit(solution)/shard_map/ppermute | solution.py:40
  38.3 0.4 shard_map.113
  38.7 0.5 collective-permute-start.12
  39.2 0.7 collective-permute-done.11.refs_1_.refs_7_.refs_10_.refs_2_
  39.9 1.7 %collective-permute-start.13 = (f32[1,128]{1,0:T(1,128)S(1)}, f32[1,128]{1,0:T(1,128)S(1)}, u32[]{:S(2)}, u32[]{:S(2)}) collective-permute-start(f32[1,128]{1,0:T(1,128)S(1)} %shard_map.114.refs_8_), channel_id=1, source_target_pairs={{0,1},{1,0},{2,3},{3,2},{4,5},{5,4},{6,7},{7,6},{8,9},{9,8},{10,11... | collective-permute-start | bytes 1544 | tf_op jit(solution)/shard_map/ppermute | solution.py:76
  41.6 1.3 %collective-permute-start.14 = (bf16[512,256]{1,0:T(8,128)(2,1)S(1)}, bf16[512,256]{1,0:T(8,128)(2,1)S(1)}, u32[]{:S(2)}, u32[]{:S(2)}) collective-permute-start(bf16[512,256]{1,0:T(8,128)(2,1)S(1)} %get-tuple-element.80), channel_id=1, source_target_pairs={{128,64},{132,68},{136,72},{140,76},{144,80},{148,84},{152,88},{15... | collective-permute-start | bytes 786440 | tf_op jit(solution)/shard_map/ppermute | solution.py:40
  42.9 0.6 collective-permute-done.13.refs_9_
  43.6 3.3 %collective-permute-start.15 = (f32[1,128]{1,0:T(1,128)S(1)}, f32[1,128]{1,0:T(1,128)S(1)}, u32[]{:S(2)}, u32[]{:S(2)}) collective-permute-start(f32[1,128]{1,0:T(1,128)S(1)} %get-tuple-element.81.refs_2_), channel_id=1, source_target_pairs={{0,2},{1,3},{2,0},{3,1},{4,6},{5,7},{6,4},{7,5},{8,10},{9,11},{10,... | collective-permute-start | bytes 1544 | tf_op jit(solution)/shard_map/ppermute | solution.py:76
  46.9 0.7 collective-permute-start.17
  47.6 1.5 %shard_map.117 = (f32[512,256]{1,0:T(8,128)S(1)}, f32[128,896]{1,0:T(8,128)S(1)}) custom-call(f32[512,128]{1,0:T(8,128)S(1)} %get-tuple-element.61.refs_0_, bf16[512,256]{1,0:T(8,128)(2,1)S(1)} %collective-permute-done.9.refs_1_, bf16[128,896]{1,0:T(8,128)(2,1)S(1)} %get-tuple-element.59.refs_2_.refs_5_, ...), custom_call_target="tpu_custom_call" | custom-call | flops 2653050112 | bytes 8487000 | tf_op jit(solution)/shard_map/pallas_call | solution.py:90
  49.0 3.6 %collective-permute-done.14.refs_1_ = bf16[512,256]{1,0:T(8,128)(2,1)S(1)} collective-permute-done((bf16[512,256]{1,0:T(8,128)(2,1)S(1)}, bf16[512,256]{1,0:T(8,128)(2,1)S(1)}, u32[]{:S(2)}, u32[]{:S(2)}) %collective-permute-start.14) | collective-permute-done | bytes 262176 | tf_op jit(solution)/shard_map/ppermute | solution.py:40
  52.7 0.2 shard_map.119.refs_0_
  52.9 3.9 %collective-permute-start.18 = (bf16[512,256]{1,0:T(8,128)(2,1)S(1)}, bf16[512,256]{1,0:T(8,128)(2,1)S(1)}, u32[]{:S(2)}, u32[]{:S(2)}) collective-permute-start(bf16[512,256]{1,0:T(8,128)(2,1)S(1)} %shard_map.118.refs_0_), channel_id=1, source_target_pairs={{64,0},{68,4},{72,8},{76,12},{80,16},{84,20},{88,24},{92,28},{96,3... | collective-permute-start | bytes 786440 | tf_op jit(solution)/shard_map/ppermute | solution.py:40
  56.9 2.5 %collective-permute-start.19 = (f32[8,256]{1,0:T(8,128)S(1)}, f32[8,256]{1,0:T(8,128)S(1)}, u32[]{:S(2)}, u32[]{:S(2)}) collective-permute-start(f32[8,256]{1,0:T(8,128)S(1)} %shard_map.120.refs_0_.refs_3_), channel_id=1, source_target_pairs={{0,128},{4,132},{8,136},{12,140},{16,144},{20,148},{24,152},{28,15... | collective-permute-start | bytes 24584 | tf_op jit(solution)/shard_map/ppermute | solution.py:40
  59.4 1.5 %shard_map.121 = (f32[512,256]{1,0:T(8,128)S(1)}, f32[128,896]{1,0:T(8,128)S(1)}) custom-call(f32[8,256]{1,0:T(8,128)S(1)} %shard_map.120.refs_0_.refs_3_, f32[128,896]{1,0:T(8,128)S(1)} %collective-permute-done.12.refs_1_.refs_4_, bf16[512,256]{1,0:T(8,128)(2,1)S(1)} %collective-permute-done.17.refs_2_, f32[512,128]{1,0:T(8,128)S(1)} %get-tuple-element.62.refs_0_.refs_3_, ...), custom_call_target="tpu_custom_call" | custom-call | flops 2653050112 | bytes 8487000 | tf_op jit(solution)/shard_map/pallas_call | solution.py:90
  60.9 4.1 %collective-permute-done.19.refs_4_ = f32[8,256]{1,0:T(8,128)S(1)} collective-permute-done((f32[8,256]{1,0:T(8,128)S(1)}, f32[8,256]{1,0:T(8,128)S(1)}, u32[]{:S(2)}, u32[]{:S(2)}) %collective-permute-start.19) | collective-permute-done | bytes 8224 | tf_op jit(solution)/shard_map/ppermute | solution.py:40
  65.0 1.1 %collective-permute-start.20 = (bf16[272,256]{1,0:T(8,128)(2,1)S(1)}, bf16[272,256]{1,0:T(8,128)(2,1)S(1)}, u32[]{:S(2)}, u32[]{:S(2)}) collective-permute-start(bf16[272,256]{1,0:T(8,128)(2,1)S(1)} %get-tuple-element.87), channel_id=1, source_target_pairs={{0,8},{4,12},{8,0},{12,4},{16,24},{20,28},{24,16},{28,20},{32,40},... | collective-permute-start | bytes 417800 | tf_op jit(solution)/shard_map/ppermute | solution.py:40
  66.1 1.1 %collective-permute-start.21 = (f32[8,256]{1,0:T(8,128)S(1)}, f32[8,256]{1,0:T(8,128)S(1)}, u32[]{:S(2)}, u32[]{:S(2)}) collective-permute-start(f32[8,256]{1,0:T(8,128)S(1)} %get-tuple-element.88.refs_2_), channel_id=1, source_target_pairs={{0,4},{4,0},{8,12},{12,8},{16,20},{20,16},{24,28},{28,24},{32,36},... | collective-permute-start | bytes 24584 | tf_op jit(solution)/shard_map/ppermute | solution.py:40
  67.2 2.0 %collective-permute-done.22.refs_4_ = f32[8,256]{1,0:T(8,128)S(1)} collective-permute-done((f32[8,256]{1,0:T(8,128)S(1)}, f32[8,256]{1,0:T(8,128)S(1)}, u32[]{:S(2)}, u32[]{:S(2)}) %collective-permute-start.22) | collective-permute-done | bytes 8224 | tf_op jit(solution)/shard_map/ppermute | solution.py:40
  69.2 1.0 %collective-permute-done.20.refs_1_ = bf16[272,256]{1,0:T(8,128)(2,1)S(1)} collective-permute-done((bf16[272,256]{1,0:T(8,128)(2,1)S(1)}, bf16[272,256]{1,0:T(8,128)(2,1)S(1)}, u32[]{:S(2)}, u32[]{:S(2)}) %collective-permute-start.20) | collective-permute-done | bytes 139296 | tf_op jit(solution)/shard_map/ppermute | solution.py:40
  70.3 0.2 collective-permute-start.23
  70.5 1.3 %collective-permute-start.24 = (bf16[80,256]{1,0:T(8,128)(2,1)S(1)}, bf16[80,256]{1,0:T(8,128)(2,1)S(1)}, u32[]{:S(2)}, u32[]{:S(2)}) collective-permute-start(bf16[80,256]{1,0:T(8,128)(2,1)S(1)} %get-tuple-element.97), channel_id=1, source_target_pairs={{0,48},{4,52},{8,56},{12,60},{16,0},{20,4},{24,8},{28,12},{32,16},... | collective-permute-start | bytes 122888 | tf_op jit(solution)/shard_map/ppermute | solution.py:40
  71.8 4.9 %collective-permute-start.25 = (bf16[80,256]{1,0:T(8,128)(2,1)S(1)}, bf16[80,256]{1,0:T(8,128)(2,1)S(1)}, u32[]{:S(2)}, u32[]{:S(2)}) collective-permute-start(bf16[80,256]{1,0:T(8,128)(2,1)S(1)} %get-tuple-element.98), channel_id=1, source_target_pairs={{0,32},{4,36},{8,40},{12,44},{16,48},{20,52},{24,56},{28,60},{32,0... | collective-permute-start | bytes 122888 | tf_op jit(solution)/shard_map/ppermute | solution.py:40
  76.8 1.5 %shard_map.124 = (bf16[256,896]{1,0:T(8,128)(2,1)}, bf16[256,896]{1,0:T(8,128)(2,1)}, f32[1,128]{1,0:T(1,128)S(1)}) custom-call(bf16[256,64]{1,0:T(8,128)(2,1)S(1)} %get-tuple-element.53.refs_0_, f32[8,896]{1,0:T(8,128)S(1)} %get-tuple-element.72.refs_0_.refs_6_.refs_9_.refs_1_, f32[8,896]{1,0:T(8,128)S(1)} %collective-permute-done.11.refs_1_.refs_7_.refs_10_.refs_2_, ...), custom_call_target="tpu_custom_call" | custom-call | flops 115350000 | bytes 369000 | tf_op jit(solution)/shard_map/pallas_call | solution.py:90
  78.3 2.7 %collective-permute-done.25.refs_5_ = bf16[80,256]{1,0:T(8,128)(2,1)S(1)} collective-permute-done((bf16[80,256]{1,0:T(8,128)(2,1)S(1)}, bf16[80,256]{1,0:T(8,128)(2,1)S(1)}, u32[]{:S(2)}, u32[]{:S(2)}) %collective-permute-start.25) | collective-permute-done | bytes 40992 | tf_op jit(solution)/shard_map/ppermute | solution.py:40
  81.0 2.0 %collective-permute-done.26.refs_6_ = bf16[80,256]{1,0:T(8,128)(2,1)S(1)} collective-permute-done((bf16[80,256]{1,0:T(8,128)(2,1)S(1)}, bf16[80,256]{1,0:T(8,128)(2,1)S(1)}, u32[]{:S(2)}, u32[]{:S(2)}) %collective-permute-start.26) | collective-permute-done | bytes 40992 | tf_op jit(solution)/shard_map/ppermute | solution.py:40
  83.0 0.8 %shard_map.125 = (bf16[512,128]{1,0:T(8,128)(2,1)}, f32[1792]{0:T(1024)}) custom-call(f32[1,128]{1,0:T(1,128)S(1)} %get-tuple-element.93.refs_0_, bf16[512,128]{1,0:T(8,128)(2,1)S(1)} %get-tuple-element.94.refs_1_, f32[64,256]{1,0:T(8,128)S(1)} %get-tuple-element.95.refs_2_, f32[8,256]{1,0:T(8,128)S(1)} %get-tuple-element.96.refs_3_, ...), custom_call_target="tpu_custom_call" | custom-call | flops 1614899968 | bytes 5166000 | tf_op jit(solution)/shard_map/pallas_call | solution.py:90
  (45 shorter events, 0.9 us)
Async XLA Ops:
  0.6 0.7 copy-start.5
  1.3 0.9 %copy-start.3 = (bf16[256,2,128]{2,1,0:T(2,128)(2,1)S(1)}, bf16[256,2,128]{2,1,0:T(2,128)(2,1)}, u32[]{:S(2)}) copy-start(bf16[256,2,128]{2,1,0:T(2,128)(2,1)} %param.10) | copy-start | bytes 393220
  2.2 2.4 %copy-start.4 = (s32[64]{0:T(128)S(1)}, s32[64]{0:T(128)}, u32[]{:S(2)}) copy-start(s32[64]{0:T(128)} %refs_1_.1) | copy-start | bytes 772
  2.5 2.9 %copy-start.6 = (bf16[1792]{0:T(1024)(128)(2,1)S(1)}, bf16[1792]{0:T(1024)(128)(2,1)}, u32[]{:S(2)}) copy-start(bf16[1792]{0:T(1024)(128)(2,1)} %param.8) | copy-start | bytes 10756
  2.5 14.2 %copy-start = (bf16[256,1792]{1,0:T(8,128)(2,1)S(1)}, bf16[256,1792]{1,0:T(8,128)(2,1)}, u32[]{:S(2)}) copy-start(bf16[256,1792]{1,0:T(8,128)(2,1)} %refs_5_.1) | copy-start | bytes 2752516
  2.5 14.1 %copy-start.1 = (bf16[256,896]{1,0:T(8,128)(2,1)S(1)}, bf16[256,896]{1,0:T(8,128)(2,1)}, u32[]{:S(2)}) copy-start(bf16[256,896]{1,0:T(8,128)(2,1)} %refs_3_.1) | copy-start | bytes 1376260
  2.5 14.1 %copy-start.2 = (bf16[256,896]{1,0:T(8,128)(2,1)S(1)}, bf16[256,896]{1,0:T(8,128)(2,1)}, u32[]{:S(2)}) copy-start(bf16[256,896]{1,0:T(8,128)(2,1)} %refs_4_.1) | copy-start | bytes 1376260
  2.5 4.0 %collective-permute-start = (bf16[64,256]{1,0:T(8,128)(2,1)S(1)}, bf16[64,256]{1,0:T(8,128)(2,1)S(1)}, u32[]{:S(2)}, u32[]{:S(2)}) collective-permute-start(bf16[64,256]{1,0:T(8,128)(2,1)S(1)} %shard_map.102.refs_0_), channel_id=1, source_target_pairs={{0,8},{4,12},{8,0},{12,4},{16,24},{20,28},{24,16},{28,20},{32,40},... | collective-permute-start | bytes 98312 | tf_op jit(solution)/shard_map/ppermute | solution.py:40
  6.6 15.5 %collective-permute-start.5 = (bf16[128,256]{1,0:T(8,128)(2,1)S(1)}, bf16[128,256]{1,0:T(8,128)(2,1)S(1)}, u32[]{:S(2)}, u32[]{:S(2)}) collective-permute-start(bf16[128,256]{1,0:T(8,128)(2,1)S(1)} %shard_map.104.refs_0_.refs_2_), channel_id=1, source_target_pairs={{0,48},{4,52},{8,56},{12,60},{16,0},{20,4},{24,8},{28,12},{32,16},... | collective-permute-start | bytes 196616 | tf_op jit(solution)/shard_map/ppermute | solution.py:40
  12.9 9.2 %collective-permute-start.4 = (bf16[128,256]{1,0:T(8,128)(2,1)S(1)}, bf16[128,256]{1,0:T(8,128)(2,1)S(1)}, u32[]{:S(2)}, u32[]{:S(2)}) collective-permute-start(bf16[128,256]{1,0:T(8,128)(2,1)S(1)} %shard_map.104.refs_0_.refs_2_), channel_id=1, source_target_pairs={{0,32},{4,36},{8,40},{12,44},{16,48},{20,52},{24,56},{28,60},{32,0... | collective-permute-start | bytes 196616 | tf_op jit(solution)/shard_map/ppermute | solution.py:40
  13.8 8.2 %collective-permute-start.3 = (bf16[128,256]{1,0:T(8,128)(2,1)S(1)}, bf16[128,256]{1,0:T(8,128)(2,1)S(1)}, u32[]{:S(2)}, u32[]{:S(2)}) collective-permute-start(bf16[128,256]{1,0:T(8,128)(2,1)S(1)} %shard_map.104.refs_0_.refs_2_), channel_id=1, source_target_pairs={{0,16},{4,20},{8,24},{12,28},{16,32},{20,36},{24,40},{28,44},{32,4... | collective-permute-start | bytes 196616 | tf_op jit(solution)/shard_map/ppermute | solution.py:40
  17.2 12.9 %collective-permute-start.7 = (bf16[64,1792]{1,0:T(8,128)(2,1)S(1)}, bf16[64,1792]{1,0:T(8,128)(2,1)S(1)}, u32[]{:S(2)}, u32[]{:S(2)}) collective-permute-start(bf16[64,1792]{1,0:T(8,128)(2,1)S(1)} %get-tuple-element.58.refs_0_), channel_id=1, source_target_pairs={{0,4},{4,0},{8,12},{12,8},{16,20},{20,16},{24,28},{28,24},{32,36},... | collective-permute-start | bytes 688136 | tf_op jit(solution)/shard_map/ppermute | solution.py:40
  17.3 3.6 %collective-permute-start.1 = (f32[1,128]{1,0:T(1,128)S(1)}, f32[1,128]{1,0:T(1,128)S(1)}, u32[]{:S(2)}, u32[]{:S(2)}) collective-permute-start(f32[1,128]{1,0:T(1,128)S(1)} %get-tuple-element.56.refs_0_), channel_id=1, source_target_pairs={{0,1},{1,0},{2,3},{3,2},{4,5},{5,4},{6,7},{7,6},{8,9},{9,8},{10,11... | collective-permute-start | bytes 1544 | tf_op jit(solution)/shard_map/ppermute | solution.py:76
  20.9 1.1 %collective-permute-start.2 = (f32[1,128]{1,0:T(1,128)S(1)}, f32[1,128]{1,0:T(1,128)S(1)}, u32[]{:S(2)}, u32[]{:S(2)}) collective-permute-start(f32[1,128]{1,0:T(1,128)S(1)} %shard_map.106.refs_0_), channel_id=1, source_target_pairs={{0,4},{4,0},{8,12},{12,8},{16,20},{20,16},{24,28},{28,24},{32,36},... | collective-permute-start | bytes 1544 | tf_op jit(solution)/shard_map/ppermute | solution.py:40
  22.1 9.9 %collective-permute-start.9 = (bf16[512,256]{1,0:T(8,128)(2,1)S(1)}, bf16[512,256]{1,0:T(8,128)(2,1)S(1)}, u32[]{:S(2)}, u32[]{:S(2)}) collective-permute-start(bf16[512,256]{1,0:T(8,128)(2,1)S(1)} %get-tuple-element.57.refs_1_.refs_4_), channel_id=1, source_target_pairs={{0,64},{4,68},{8,72},{12,76},{16,80},{20,84},{24,88},{28,92},{32,9... | collective-permute-start | bytes 786440 | tf_op jit(solution)/shard_map/ppermute | solution.py:40
  23.7 10.7 %collective-permute-start.8 = (bf16[512,256]{1,0:T(8,128)(2,1)S(1)}, bf16[512,256]{1,0:T(8,128)(2,1)S(1)}, u32[]{:S(2)}, u32[]{:S(2)}) collective-permute-start(bf16[512,256]{1,0:T(8,128)(2,1)S(1)} %get-tuple-element.57.refs_1_.refs_4_), channel_id=1, source_target_pairs={{0,128},{4,132},{8,136},{12,140},{16,144},{20,148},{24,152},{28,15... | collective-permute-start | bytes 786440 | tf_op jit(solution)/shard_map/ppermute | solution.py:40
  24.8 13.5 %collective-permute-start.6 = (bf16[512,256]{1,0:T(8,128)(2,1)S(1)}, bf16[512,256]{1,0:T(8,128)(2,1)S(1)}, u32[]{:S(2)}, u32[]{:S(2)}) collective-permute-start(bf16[512,256]{1,0:T(8,128)(2,1)S(1)} %get-tuple-element.57.refs_1_.refs_4_), channel_id=1, source_target_pairs={{0,192},{4,196},{8,200},{12,204},{16,208},{20,212},{24,216},{28,22... | collective-permute-start | bytes 786440 | tf_op jit(solution)/shard_map/ppermute | solution.py:40
  26.9 7.5 %collective-permute-start.10 = (f32[1,128]{1,0:T(1,128)S(1)}, f32[1,128]{1,0:T(1,128)S(1)}, u32[]{:S(2)}, u32[]{:S(2)}) collective-permute-start(f32[1,128]{1,0:T(1,128)S(1)} %get-tuple-element.68.refs_2_), channel_id=1, source_target_pairs={{0,2},{1,3},{2,0},{3,1},{4,6},{5,7},{6,4},{7,5},{8,10},{9,11},{10,... | collective-permute-start | bytes 1544 | tf_op jit(solution)/shard_map/ppermute | solution.py:76
  38.6 1.3 %collective-permute-start.11 = (f32[8,896]{1,0:T(8,128)S(1)}, f32[8,896]{1,0:T(8,128)S(1)}, u32[]{:S(2)}, u32[]{:S(2)}) collective-permute-start(f32[8,896]{1,0:T(8,128)S(1)} %get-tuple-element.72.refs_0_.refs_6_.refs_9_.refs_1_), channel_id=1, source_target_pairs={{0,4},{4,0},{8,12},{12,8},{16,20},{20,16},{24,28},{28,24},{32,36},... | collective-permute-start | bytes 86024 | tf_op jit(solution)/shard_map/ppermute | solution.py:40
  38.7 20.7 %collective-permute-start.12 = (f32[128,896]{1,0:T(8,128)S(1)}, f32[128,896]{1,0:T(8,128)S(1)}, u32[]{:S(2)}, u32[]{:S(2)}) collective-permute-start(f32[128,896]{1,0:T(8,128)S(1)} %get-tuple-element.73.refs_3_), channel_id=1, source_target_pairs={{0,4},{4,0},{8,12},{12,8},{16,20},{20,16},{24,28},{28,24},{32,36},... | collective-permute-start | bytes 1376264 | tf_op jit(solution)/shard_map/ppermute | solution.py:40
  39.9 3.6 %collective-permute-start.13 = (f32[1,128]{1,0:T(1,128)S(1)}, f32[1,128]{1,0:T(1,128)S(1)}, u32[]{:S(2)}, u32[]{:S(2)}) collective-permute-start(f32[1,128]{1,0:T(1,128)S(1)} %shard_map.114.refs_8_), channel_id=1, source_target_pairs={{0,1},{1,0},{2,3},{3,2},{4,5},{5,4},{6,7},{7,6},{8,9},{9,8},{10,11... | collective-permute-start | bytes 1544 | tf_op jit(solution)/shard_map/ppermute | solution.py:76
  41.6 11.0 %collective-permute-start.14 = (bf16[512,256]{1,0:T(8,128)(2,1)S(1)}, bf16[512,256]{1,0:T(8,128)(2,1)S(1)}, u32[]{:S(2)}, u32[]{:S(2)}) collective-permute-start(bf16[512,256]{1,0:T(8,128)(2,1)S(1)} %get-tuple-element.80), channel_id=1, source_target_pairs={{128,64},{132,68},{136,72},{140,76},{144,80},{148,84},{152,88},{15... | collective-permute-start | bytes 786440 | tf_op jit(solution)/shard_map/ppermute | solution.py:40
  43.6 9.1 %collective-permute-start.15 = (f32[1,128]{1,0:T(1,128)S(1)}, f32[1,128]{1,0:T(1,128)S(1)}, u32[]{:S(2)}, u32[]{:S(2)}) collective-permute-start(f32[1,128]{1,0:T(1,128)S(1)} %get-tuple-element.81.refs_2_), channel_id=1, source_target_pairs={{0,2},{1,3},{2,0},{3,1},{4,6},{5,7},{6,4},{7,5},{8,10},{9,11},{10,... | collective-permute-start | bytes 1544 | tf_op jit(solution)/shard_map/ppermute | solution.py:76
  46.9 12.5 %collective-permute-start.17 = (bf16[512,256]{1,0:T(8,128)(2,1)S(1)}, bf16[512,256]{1,0:T(8,128)(2,1)S(1)}, u32[]{:S(2)}, u32[]{:S(2)}) collective-permute-start(bf16[512,256]{1,0:T(8,128)(2,1)S(1)} %get-tuple-element.83), channel_id=1, source_target_pairs={{192,0},{196,4},{200,8},{204,12},{208,16},{212,20},{216,24},{220,2... | collective-permute-start | bytes 786440 | tf_op jit(solution)/shard_map/ppermute | solution.py:40
  52.8 4.0 %collective-permute-start.16 = (f32[8,256]{1,0:T(8,128)S(1)}, f32[8,256]{1,0:T(8,128)S(1)}, u32[]{:S(2)}, u32[]{:S(2)}) collective-permute-start(f32[8,256]{1,0:T(8,128)S(1)} %shard_map.119.refs_0_), channel_id=1, source_target_pairs={{0,64},{4,68},{8,72},{12,76},{16,80},{20,84},{24,88},{28,92},{32,9... | collective-permute-start | bytes 24584 | tf_op jit(solution)/shard_map/ppermute | solution.py:40
  52.9 12.0 %collective-permute-start.18 = (bf16[512,256]{1,0:T(8,128)(2,1)S(1)}, bf16[512,256]{1,0:T(8,128)(2,1)S(1)}, u32[]{:S(2)}, u32[]{:S(2)}) collective-permute-start(bf16[512,256]{1,0:T(8,128)(2,1)S(1)} %shard_map.118.refs_0_), channel_id=1, source_target_pairs={{64,0},{68,4},{72,8},{76,12},{80,16},{84,20},{88,24},{92,28},{96,3... | collective-permute-start | bytes 786440 | tf_op jit(solution)/shard_map/ppermute | solution.py:40
  56.9 8.0 %collective-permute-start.19 = (f32[8,256]{1,0:T(8,128)S(1)}, f32[8,256]{1,0:T(8,128)S(1)}, u32[]{:S(2)}, u32[]{:S(2)}) collective-permute-start(f32[8,256]{1,0:T(8,128)S(1)} %shard_map.120.refs_0_.refs_3_), channel_id=1, source_target_pairs={{0,128},{4,132},{8,136},{12,140},{16,144},{20,148},{24,152},{28,15... | collective-permute-start | bytes 24584 | tf_op jit(solution)/shard_map/ppermute | solution.py:40
  65.0 5.2 %collective-permute-start.20 = (bf16[272,256]{1,0:T(8,128)(2,1)S(1)}, bf16[272,256]{1,0:T(8,128)(2,1)S(1)}, u32[]{:S(2)}, u32[]{:S(2)}) collective-permute-start(bf16[272,256]{1,0:T(8,128)(2,1)S(1)} %get-tuple-element.87), channel_id=1, source_target_pairs={{0,8},{4,12},{8,0},{12,4},{16,24},{20,28},{24,16},{28,20},{32,40},... | collective-permute-start | bytes 417800 | tf_op jit(solution)/shard_map/ppermute | solution.py:40
  66.1 3.1 %collective-permute-start.22 = (f32[8,256]{1,0:T(8,128)S(1)}, f32[8,256]{1,0:T(8,128)S(1)}, u32[]{:S(2)}, u32[]{:S(2)}) collective-permute-start(f32[8,256]{1,0:T(8,128)S(1)} %get-tuple-element.88.refs_2_), channel_id=1, source_target_pairs={{0,12},{4,8},{8,4},{12,0},{16,28},{20,24},{24,20},{28,16},{32,44},... | collective-permute-start | bytes 24584 | tf_op jit(solution)/shard_map/ppermute | solution.py:40
  66.1 3.1 %collective-permute-start.21 = (f32[8,256]{1,0:T(8,128)S(1)}, f32[8,256]{1,0:T(8,128)S(1)}, u32[]{:S(2)}, u32[]{:S(2)}) collective-permute-start(f32[8,256]{1,0:T(8,128)S(1)} %get-tuple-element.88.refs_2_), channel_id=1, source_target_pairs={{0,4},{4,0},{8,12},{12,8},{16,20},{20,16},{24,28},{28,24},{32,36},... | collective-permute-start | bytes 24584 | tf_op jit(solution)/shard_map/ppermute | solution.py:40
  70.3 6.5 %collective-permute-start.23 = (f32[128,896]{1,0:T(8,128)S(1)}, f32[128,896]{1,0:T(8,128)S(1)}, u32[]{:S(2)}, u32[]{:S(2)}) collective-permute-start(f32[128,896]{1,0:T(8,128)S(1)} %get-tuple-element.90.refs_6_), channel_id=1, source_target_pairs={{0,4},{4,0},{8,12},{12,8},{16,20},{20,16},{24,28},{28,24},{32,36},... | collective-permute-start | bytes 1376264 | tf_op jit(solution)/shard_map/ppermute | solution.py:40
  70.5 7.8 %collective-permute-start.24 = (bf16[80,256]{1,0:T(8,128)(2,1)S(1)}, bf16[80,256]{1,0:T(8,128)(2,1)S(1)}, u32[]{:S(2)}, u32[]{:S(2)}) collective-permute-start(bf16[80,256]{1,0:T(8,128)(2,1)S(1)} %get-tuple-element.97), channel_id=1, source_target_pairs={{0,48},{4,52},{8,56},{12,60},{16,0},{20,4},{24,8},{28,12},{32,16},... | collective-permute-start | bytes 122888 | tf_op jit(solution)/shard_map/ppermute | solution.py:40
  71.8 9.1 %collective-permute-start.25 = (bf16[80,256]{1,0:T(8,128)(2,1)S(1)}, bf16[80,256]{1,0:T(8,128)(2,1)S(1)}, u32[]{:S(2)}, u32[]{:S(2)}) collective-permute-start(bf16[80,256]{1,0:T(8,128)(2,1)S(1)} %get-tuple-element.98), channel_id=1, source_target_pairs={{0,32},{4,36},{8,40},{12,44},{16,48},{20,52},{24,56},{28,60},{32,0... | collective-permute-start | bytes 122888 | tf_op jit(solution)/shard_map/ppermute | solution.py:40
  76.8 6.2 %collective-permute-start.26 = (bf16[80,256]{1,0:T(8,128)(2,1)S(1)}, bf16[80,256]{1,0:T(8,128)(2,1)S(1)}, u32[]{:S(2)}, u32[]{:S(2)}) collective-permute-start(bf16[80,256]{1,0:T(8,128)(2,1)S(1)} %get-tuple-element.99), channel_id=1, source_target_pairs={{0,16},{4,20},{8,24},{12,28},{16,32},{20,36},{24,40},{28,44},{32,4... | collective-permute-start | bytes 122888 | tf_op jit(solution)/shard_map/ppermute | solution.py:40

commit v6 on v5

--- a/solution.py
+++ b/solution.py
@@ -236,9 +236,9 @@
             bias[j * SLOTS : (j + 1) * SLOTS, :] = jnp.where(seen, 0.0, MASKED)
 
 
-def lane_groups(ref):
+def lane_groups(ref, size=GROUP):
     lanes = ref.shape[1]
-    return [slice(a, min(a + GROUP, lanes)) for a in range(0, lanes, GROUP)]
+    return [slice(a, min(a + size, lanes)) for a in range(0, lanes, size)]
 
 
 def scores_of(keys, qt, bias):
@@ -263,7 +263,7 @@
     @pl.when(here()[0] >= shift)
     def _():
         keys, values = pairs[:, :HEAD_SIZE], pairs[:, HEAD_SIZE:]
-        for cols in lane_groups(qt):
+        for cols in lane_groups(qt, PAIR):
             scores = scores_of(keys, qt[:, cols], bias[...])
             old = stats[0:1, cols]
             new = jnp.maximum(old, jnp.max(scores, axis=0, keepdims=True))

time: 84 us -> 83.7 us (level)
  Pallas kernels: 11.4 us -> 10 us
  waiting for transfers between devices: 25.3 us -> 26.2 us
    pallas_call x24, Pallas kernels: 11.4 us -> 10 us  [call(): pl.pallas_call(body, out_shape=outs, in_specs=[ANY] * skip + list(specs o...]
    ppermute x23, waiting for transfers between devices: 22.7 us -> 23.7 us  [move(): return lax.ppermute(value, 'ctx', pairs)]
  transfers between devices with their start and end apart: 27 -> 27, of which waited for: 13 -> 13; matrix products, arithmetic and copies ran while one was open for 0% -> 0% of each run, Pallas kernels for 12% -> 10%
where the time goes in v6:
time: 83.7 us; the launch traced here: 83.5 us
  starting transfers between devices  44.8 us (54%)
  waiting for transfers between devices  26.2 us (31%)
  Pallas kernels  10 us (12%)
  local copies, waits for them, and re-layouts  1.59 us (2%)
  between operations  0.89 us (1%)
    ppermute x23, starting transfers between devices, move(): return lax.ppermute(value, 'ctx', pairs)  35 us
    ppermute x23, waiting for transfers between devices, move(): return lax.ppermute(value, 'ctx', pairs)  23.7 us
    pallas_call x24, Pallas kernels, call(): pl.pallas_call(body, out_shape=outs, in_specs=[ANY] * skip + list(specs o...  10 us
    ppermute x4, starting transfers between devices, flip_tp(): return lax.ppermute(value, 'tp', [(i, i ^ bit) for i in range(4)])  9.8 us
    ppermute x4, waiting for transfers between devices, flip_tp(): return lax.ppermute(value, 'tp', [(i, i ^ bit) for i in range(4)])  2.58 us
  transfers between devices with their start and end apart: 27, of which 13 were waited for; matrix products, arithmetic and copies ran while one was open for 0% of the time, Pallas kernels for 10%

profile of v6, /device:TPU:2, one launch (start us, length us, event | category | flops | bytes accessed | tf_op | source)
XLA Modules:
  0.0 83.5 jit_solution(15719365479398309180)
XLA Ops:
  0.6 0.6 copy-done.5
  1.3 0.9 %copy-done.3 = bf16[256,2,128]{2,1,0:T(2,128)(2,1)S(1)} copy-done((bf16[256,2,128]{2,1,0:T(2,128)(2,1)S(1)}, bf16[256,2,128]{2,1,0:T(2,128)(2,1)}, u32[]{:S(2)}) %copy-start.3) | copy-done | bytes 131096
  2.2 0.3 shard_map.102.refs_0_
  2.5 2.0 %collective-permute-start = (bf16[64,256]{1,0:T(8,128)(2,1)S(1)}, bf16[64,256]{1,0:T(8,128)(2,1)S(1)}, u32[]{:S(2)}, u32[]{:S(2)}) collective-permute-start(bf16[64,256]{1,0:T(8,128)(2,1)S(1)} %shard_map.102.refs_0_), channel_id=1, source_target_pairs={{0,8},{4,12},{8,0},{12,4},{16,24},{20,28},{24,16},{28,20},{32,40},... | collective-permute-start | bytes 98312 | tf_op jit(solution)/shard_map/ppermute | solution.py:40
  4.6 0.8 %shard_map.103 = (f32[1,128]{1,0:T(1,128)S(1)}, bf16[256,64]{1,0:T(8,128)(2,1)S(1)}, bf16[512,128]{1,0:T(8,128)(2,1)S(1)}, f32[512,128]{1,0:T(8,128)S(1)}, f32[5...) custom-call(bf16[64,256]{1,0:T(8,128)(2,1)S(1)} %shard_map.102.refs_0_, s32[64]{0:T(128)S(1)} %copy-done.4, ...), custom_call_target="tpu_custom_call" | custom-call | flops 1153500032 | bytes 3690000 | tf_op jit(solution)/shard_map/pallas_call | solution.py:90
  5.4 1.1 %collective-permute-done.refs_1_ = bf16[64,256]{1,0:T(8,128)(2,1)S(1)} collective-permute-done((bf16[64,256]{1,0:T(8,128)(2,1)S(1)}, bf16[64,256]{1,0:T(8,128)(2,1)S(1)}, u32[]{:S(2)}, u32[]{:S(2)}) %collective-permute-start) | collective-permute-done | bytes 32800 | tf_op jit(solution)/shard_map/ppermute | solution.py:40
  6.6 6.3 %collective-permute-start.5 = (bf16[128,256]{1,0:T(8,128)(2,1)S(1)}, bf16[128,256]{1,0:T(8,128)(2,1)S(1)}, u32[]{:S(2)}, u32[]{:S(2)}) collective-permute-start(bf16[128,256]{1,0:T(8,128)(2,1)S(1)} %shard_map.104.refs_0_.refs_2_), channel_id=1, source_target_pairs={{0,48},{4,52},{8,56},{12,60},{16,0},{20,4},{24,8},{28,12},{32,16},... | collective-permute-start | bytes 196616 | tf_op jit(solution)/shard_map/ppermute | solution.py:40
  12.9 1.0 %collective-permute-start.4 = (bf16[128,256]{1,0:T(8,128)(2,1)S(1)}, bf16[128,256]{1,0:T(8,128)(2,1)S(1)}, u32[]{:S(2)}, u32[]{:S(2)}) collective-permute-start(bf16[128,256]{1,0:T(8,128)(2,1)S(1)} %shard_map.104.refs_0_.refs_2_), channel_id=1, source_target_pairs={{0,32},{4,36},{8,40},{12,44},{16,48},{20,52},{24,56},{28,60},{32,0... | collective-permute-start | bytes 196616 | tf_op jit(solution)/shard_map/ppermute | solution.py:40
  13.8 2.8 %collective-permute-start.3 = (bf16[128,256]{1,0:T(8,128)(2,1)S(1)}, bf16[128,256]{1,0:T(8,128)(2,1)S(1)}, u32[]{:S(2)}, u32[]{:S(2)}) collective-permute-start(bf16[128,256]{1,0:T(8,128)(2,1)S(1)} %shard_map.104.refs_0_.refs_2_), channel_id=1, source_target_pairs={{0,16},{4,20},{8,24},{12,28},{16,32},{20,36},{24,40},{28,44},{32,4... | collective-permute-start | bytes 196616 | tf_op jit(solution)/shard_map/ppermute | solution.py:40
  16.7 0.5 shard_map.105
  17.3 1.7 %collective-permute-start.1 = (f32[1,128]{1,0:T(1,128)S(1)}, f32[1,128]{1,0:T(1,128)S(1)}, u32[]{:S(2)}, u32[]{:S(2)}) collective-permute-start(f32[1,128]{1,0:T(1,128)S(1)} %get-tuple-element.56.refs_0_), channel_id=1, source_target_pairs={{0,1},{1,0},{2,3},{3,2},{4,5},{5,4},{6,7},{7,6},{8,9},{9,8},{10,11... | collective-permute-start | bytes 1544 | tf_op jit(solution)/shard_map/ppermute | solution.py:76
  19.0 2.0 %collective-permute-done.1.refs_1_ = f32[1,128]{1,0:T(1,128)S(1)} collective-permute-done((f32[1,128]{1,0:T(1,128)S(1)}, f32[1,128]{1,0:T(1,128)S(1)}, u32[]{:S(2)}, u32[]{:S(2)}) %collective-permute-start.1) | collective-permute-done | bytes 544 | tf_op jit(solution)/shard_map/ppermute | solution.py:76
  20.9 1.1 %collective-permute-done.2.refs_1_ = f32[1,128]{1,0:T(1,128)S(1)} collective-permute-done((f32[1,128]{1,0:T(1,128)S(1)}, f32[1,128]{1,0:T(1,128)S(1)}, u32[]{:S(2)}, u32[]{:S(2)}) %collective-permute-start.2) | collective-permute-done | bytes 544 | tf_op jit(solution)/shard_map/ppermute | solution.py:40
  22.1 1.6 %collective-permute-start.9 = (bf16[512,256]{1,0:T(8,128)(2,1)S(1)}, bf16[512,256]{1,0:T(8,128)(2,1)S(1)}, u32[]{:S(2)}, u32[]{:S(2)}) collective-permute-start(bf16[512,256]{1,0:T(8,128)(2,1)S(1)} %get-tuple-element.57.refs_1_.refs_4_), channel_id=1, source_target_pairs={{0,64},{4,68},{8,72},{12,76},{16,80},{20,84},{24,88},{28,92},{32,9... | collective-permute-start | bytes 786440 | tf_op jit(solution)/shard_map/ppermute | solution.py:40
  23.7 1.1 %collective-permute-start.8 = (bf16[512,256]{1,0:T(8,128)(2,1)S(1)}, bf16[512,256]{1,0:T(8,128)(2,1)S(1)}, u32[]{:S(2)}, u32[]{:S(2)}) collective-permute-start(bf16[512,256]{1,0:T(8,128)(2,1)S(1)} %get-tuple-element.57.refs_1_.refs_4_), channel_id=1, source_target_pairs={{0,128},{4,132},{8,136},{12,140},{16,144},{20,148},{24,152},{28,15... | collective-permute-start | bytes 786440 | tf_op jit(solution)/shard_map/ppermute | solution.py:40
  24.8 2.2 %collective-permute-start.6 = (bf16[512,256]{1,0:T(8,128)(2,1)S(1)}, bf16[512,256]{1,0:T(8,128)(2,1)S(1)}, u32[]{:S(2)}, u32[]{:S(2)}) collective-permute-start(bf16[512,256]{1,0:T(8,128)(2,1)S(1)} %get-tuple-element.57.refs_1_.refs_4_), channel_id=1, source_target_pairs={{0,192},{4,196},{8,200},{12,204},{16,208},{20,212},{24,216},{28,22... | collective-permute-start | bytes 786440 | tf_op jit(solution)/shard_map/ppermute | solution.py:40
  26.9 3.2 %collective-permute-start.10 = (f32[1,128]{1,0:T(1,128)S(1)}, f32[1,128]{1,0:T(1,128)S(1)}, u32[]{:S(2)}, u32[]{:S(2)}) collective-permute-start(f32[1,128]{1,0:T(1,128)S(1)} %get-tuple-element.68.refs_2_), channel_id=1, source_target_pairs={{0,2},{1,3},{2,0},{3,1},{4,6},{5,7},{6,4},{7,5},{8,10},{9,11},{10,... | collective-permute-start | bytes 1544 | tf_op jit(solution)/shard_map/ppermute | solution.py:76
  30.1 0.2 shard_map.108
  30.4 1.0 %shard_map.109 = (f32[128,896]{1,0:T(8,128)S(1)}, f32[8,896]{1,0:T(8,128)S(1)}) custom-call(f32[512,128]{1,0:T(8,128)S(1)} %get-tuple-element.62.refs_0_.refs_3_, bf16[512,256]{1,0:T(8,128)(2,1)S(1)} %get-tuple-element.57.refs_1_.refs_4_, bf16[128,896]{1,0:T(8,128)(2,1)S(1)} %get-tuple-element.59.refs_2_.refs_5_), custom_call_target="tpu_custom_call" | custom-call | flops 346049984 | bytes 1107000 | tf_op jit(solution)/shard_map/pallas_call | solution.py:90
  31.4 1.0 %shard_map.110 = (f32[128,896]{1,0:T(8,128)S(1)}, f32[8,896]{1,0:T(8,128)S(1)}) custom-call(f32[512,128]{1,0:T(8,128)S(1)} %get-tuple-element.61.refs_0_, bf16[512,256]{1,0:T(8,128)(2,1)S(1)} %collective-permute-done.9.refs_1_, bf16[128,896]{1,0:T(8,128)(2,1)S(1)} %get-tuple-element.59.refs_2_.refs_5_, f32[128,896]{1,0:T(8,128)S(1)} %get-tuple-element.63.refs_3_, ...), custom_call_target="tpu_custom_call" | custom-call | flops 346049984 | bytes 1107000 | tf_op jit(solution)/shard_map/pallas_call | solution.py:90
  32.4 2.0 %collective-permute-done.8.refs_1_ = bf16[512,256]{1,0:T(8,128)(2,1)S(1)} collective-permute-done((bf16[512,256]{1,0:T(8,128)(2,1)S(1)}, bf16[512,256]{1,0:T(8,128)(2,1)S(1)}, u32[]{:S(2)}, u32[]{:S(2)}) %collective-permute-start.8) | collective-permute-done | bytes 262176 | tf_op jit(solution)/shard_map/ppermute | solution.py:40
  34.6 3.7 %collective-permute-done.6.refs_1_ = bf16[512,256]{1,0:T(8,128)(2,1)S(1)} collective-permute-done((bf16[512,256]{1,0:T(8,128)(2,1)S(1)}, bf16[512,256]{1,0:T(8,128)(2,1)S(1)}, u32[]{:S(2)}, u32[]{:S(2)}) %collective-permute-start.6) | collective-permute-done | bytes 262176 | tf_op jit(solution)/shard_map/ppermute | solution.py:40
  38.3 0.2 shard_map.113
  38.4 0.3 collective-permute-start.11
  38.7 0.5 collective-permute-start.12
  39.2 0.7 collective-permute-done.11.refs_1_.refs_7_.refs_10_.refs_2_
  39.9 1.7 %collective-permute-start.13 = (f32[1,128]{1,0:T(1,128)S(1)}, f32[1,128]{1,0:T(1,128)S(1)}, u32[]{:S(2)}, u32[]{:S(2)}) collective-permute-start(f32[1,128]{1,0:T(1,128)S(1)} %shard_map.114.refs_8_), channel_id=1, source_target_pairs={{0,1},{1,0},{2,3},{3,2},{4,5},{5,4},{6,7},{7,6},{8,9},{9,8},{10,11... | collective-permute-start | bytes 1544 | tf_op jit(solution)/shard_map/ppermute | solution.py:76
  41.6 1.3 %collective-permute-start.14 = (bf16[512,256]{1,0:T(8,128)(2,1)S(1)}, bf16[512,256]{1,0:T(8,128)(2,1)S(1)}, u32[]{:S(2)}, u32[]{:S(2)}) collective-permute-start(bf16[512,256]{1,0:T(8,128)(2,1)S(1)} %get-tuple-element.80), channel_id=1, source_target_pairs={{128,64},{132,68},{136,72},{140,76},{144,80},{148,84},{152,88},{15... | collective-permute-start | bytes 786440 | tf_op jit(solution)/shard_map/ppermute | solution.py:40
  42.9 0.6 collective-permute-done.13.refs_9_
  43.6 3.3 %collective-permute-start.15 = (f32[1,128]{1,0:T(1,128)S(1)}, f32[1,128]{1,0:T(1,128)S(1)}, u32[]{:S(2)}, u32[]{:S(2)}) collective-permute-start(f32[1,128]{1,0:T(1,128)S(1)} %get-tuple-element.81.refs_2_), channel_id=1, source_target_pairs={{0,2},{1,3},{2,0},{3,1},{4,6},{5,7},{6,4},{7,5},{8,10},{9,11},{10,... | collective-permute-start | bytes 1544 | tf_op jit(solution)/shard_map/ppermute | solution.py:76
  46.9 0.7 collective-permute-start.17
  47.6 1.5 %shard_map.117 = (f32[512,256]{1,0:T(8,128)S(1)}, f32[128,896]{1,0:T(8,128)S(1)}) custom-call(f32[512,128]{1,0:T(8,128)S(1)} %get-tuple-element.61.refs_0_, bf16[512,256]{1,0:T(8,128)(2,1)S(1)} %collective-permute-done.9.refs_1_, bf16[128,896]{1,0:T(8,128)(2,1)S(1)} %get-tuple-element.59.refs_2_.refs_5_, ...), custom_call_target="tpu_custom_call" | custom-call | flops 2653050112 | bytes 8487000 | tf_op jit(solution)/shard_map/pallas_call | solution.py:90
  49.0 3.6 %collective-permute-done.14.refs_1_ = bf16[512,256]{1,0:T(8,128)(2,1)S(1)} collective-permute-done((bf16[512,256]{1,0:T(8,128)(2,1)S(1)}, bf16[512,256]{1,0:T(8,128)(2,1)S(1)}, u32[]{:S(2)}, u32[]{:S(2)}) %collective-permute-start.14) | collective-permute-done | bytes 262176 | tf_op jit(solution)/shard_map/ppermute | solution.py:40
  52.9 3.9 %collective-permute-start.18 = (bf16[512,256]{1,0:T(8,128)(2,1)S(1)}, bf16[512,256]{1,0:T(8,128)(2,1)S(1)}, u32[]{:S(2)}, u32[]{:S(2)}) collective-permute-start(bf16[512,256]{1,0:T(8,128)(2,1)S(1)} %shard_map.118.refs_0_), channel_id=1, source_target_pairs={{64,0},{68,4},{72,8},{76,12},{80,16},{84,20},{88,24},{92,28},{96,3... | collective-permute-start | bytes 786440 | tf_op jit(solution)/shard_map/ppermute | solution.py:40
  56.9 2.5 %collective-permute-start.19 = (f32[8,256]{1,0:T(8,128)S(1)}, f32[8,256]{1,0:T(8,128)S(1)}, u32[]{:S(2)}, u32[]{:S(2)}) collective-permute-start(f32[8,256]{1,0:T(8,128)S(1)} %shard_map.120.refs_0_.refs_3_), channel_id=1, source_target_pairs={{0,128},{4,132},{8,136},{12,140},{16,144},{20,148},{24,152},{28,15... | collective-permute-start | bytes 24584 | tf_op jit(solution)/shard_map/ppermute | solution.py:40
  59.4 1.5 %shard_map.121 = (f32[512,256]{1,0:T(8,128)S(1)}, f32[128,896]{1,0:T(8,128)S(1)}) custom-call(f32[8,256]{1,0:T(8,128)S(1)} %shard_map.120.refs_0_.refs_3_, f32[128,896]{1,0:T(8,128)S(1)} %collective-permute-done.12.refs_1_.refs_4_, bf16[512,256]{1,0:T(8,128)(2,1)S(1)} %collective-permute-done.17.refs_2_, f32[512,128]{1,0:T(8,128)S(1)} %get-tuple-element.62.refs_0_.refs_3_, ...), custom_call_target="tpu_custom_call" | custom-call | flops 2653050112 | bytes 8487000 | tf_op jit(solution)/shard_map/pallas_call | solution.py:90
  60.9 3.8 %collective-permute-done.19.refs_4_ = f32[8,256]{1,0:T(8,128)S(1)} collective-permute-done((f32[8,256]{1,0:T(8,128)S(1)}, f32[8,256]{1,0:T(8,128)S(1)}, u32[]{:S(2)}, u32[]{:S(2)}) %collective-permute-start.19) | collective-permute-done | bytes 8224 | tf_op jit(solution)/shard_map/ppermute | solution.py:40
  64.7 1.1 %collective-permute-start.20 = (bf16[272,256]{1,0:T(8,128)(2,1)S(1)}, bf16[272,256]{1,0:T(8,128)(2,1)S(1)}, u32[]{:S(2)}, u32[]{:S(2)}) collective-permute-start(bf16[272,256]{1,0:T(8,128)(2,1)S(1)} %get-tuple-element.87), channel_id=1, source_target_pairs={{0,8},{4,12},{8,0},{12,4},{16,24},{20,28},{24,16},{28,20},{32,40},... | collective-permute-start | bytes 417800 | tf_op jit(solution)/shard_map/ppermute | solution.py:40
  65.8 1.1 %collective-permute-start.21 = (f32[8,256]{1,0:T(8,128)S(1)}, f32[8,256]{1,0:T(8,128)S(1)}, u32[]{:S(2)}, u32[]{:S(2)}) collective-permute-start(f32[8,256]{1,0:T(8,128)S(1)} %get-tuple-element.88.refs_2_), channel_id=1, source_target_pairs={{0,4},{4,0},{8,12},{12,8},{16,20},{20,16},{24,28},{28,24},{32,36},... | collective-permute-start | bytes 24584 | tf_op jit(solution)/shard_map/ppermute | solution.py:40
  67.0 2.0 %collective-permute-done.22.refs_4_ = f32[8,256]{1,0:T(8,128)S(1)} collective-permute-done((f32[8,256]{1,0:T(8,128)S(1)}, f32[8,256]{1,0:T(8,128)S(1)}, u32[]{:S(2)}, u32[]{:S(2)}) %collective-permute-start.22) | collective-permute-done | bytes 8224 | tf_op jit(solution)/shard_map/ppermute | solution.py:40
  68.9 1.0 %collective-permute-done.20.refs_1_ = bf16[272,256]{1,0:T(8,128)(2,1)S(1)} collective-permute-done((bf16[272,256]{1,0:T(8,128)(2,1)S(1)}, bf16[272,256]{1,0:T(8,128)(2,1)S(1)}, u32[]{:S(2)}, u32[]{:S(2)}) %collective-permute-start.20) | collective-permute-done | bytes 139296 | tf_op jit(solution)/shard_map/ppermute | solution.py:40
  70.0 0.2 collective-permute-start.23
  70.2 1.3 %collective-permute-start.24 = (bf16[80,256]{1,0:T(8,128)(2,1)S(1)}, bf16[80,256]{1,0:T(8,128)(2,1)S(1)}, u32[]{:S(2)}, u32[]{:S(2)}) collective-permute-start(bf16[80,256]{1,0:T(8,128)(2,1)S(1)} %get-tuple-element.97), channel_id=1, source_target_pairs={{0,48},{4,52},{8,56},{12,60},{16,0},{20,4},{24,8},{28,12},{32,16},... | collective-permute-start | bytes 122888 | tf_op jit(solution)/shard_map/ppermute | solution.py:40
  71.6 5.0 %collective-permute-start.25 = (bf16[80,256]{1,0:T(8,128)(2,1)S(1)}, bf16[80,256]{1,0:T(8,128)(2,1)S(1)}, u32[]{:S(2)}, u32[]{:S(2)}) collective-permute-start(bf16[80,256]{1,0:T(8,128)(2,1)S(1)} %get-tuple-element.98), channel_id=1, source_target_pairs={{0,32},{4,36},{8,40},{12,44},{16,48},{20,52},{24,56},{28,60},{32,0... | collective-permute-start | bytes 122888 | tf_op jit(solution)/shard_map/ppermute | solution.py:40
  76.5 1.5 %shard_map.124 = (bf16[256,896]{1,0:T(8,128)(2,1)}, bf16[256,896]{1,0:T(8,128)(2,1)}, f32[1,128]{1,0:T(1,128)S(1)}) custom-call(bf16[256,64]{1,0:T(8,128)(2,1)S(1)} %get-tuple-element.53.refs_0_, f32[8,896]{1,0:T(8,128)S(1)} %get-tuple-element.72.refs_0_.refs_6_.refs_9_.refs_1_, f32[8,896]{1,0:T(8,128)S(1)} %collective-permute-done.11.refs_1_.refs_7_.refs_10_.refs_2_, ...), custom_call_target="tpu_custom_call" | custom-call | flops 115350000 | bytes 369000 | tf_op jit(solution)/shard_map/pallas_call | solution.py:90
  78.0 2.7 %collective-permute-done.25.refs_5_ = bf16[80,256]{1,0:T(8,128)(2,1)S(1)} collective-permute-done((bf16[80,256]{1,0:T(8,128)(2,1)S(1)}, bf16[80,256]{1,0:T(8,128)(2,1)S(1)}, u32[]{:S(2)}, u32[]{:S(2)}) %collective-permute-start.25) | collective-permute-done | bytes 40992 | tf_op jit(solution)/shard_map/ppermute | solution.py:40
  80.7 2.0 %collective-permute-done.26.refs_6_ = bf16[80,256]{1,0:T(8,128)(2,1)S(1)} collective-permute-done((bf16[80,256]{1,0:T(8,128)(2,1)S(1)}, bf16[80,256]{1,0:T(8,128)(2,1)S(1)}, u32[]{:S(2)}, u32[]{:S(2)}) %collective-permute-start.26) | collective-permute-done | bytes 40992 | tf_op jit(solution)/shard_map/ppermute | solution.py:40
  82.7 0.8 %shard_map.125 = (bf16[512,128]{1,0:T(8,128)(2,1)}, f32[1792]{0:T(1024)}) custom-call(f32[1,128]{1,0:T(1,128)S(1)} %get-tuple-element.93.refs_0_, bf16[512,128]{1,0:T(8,128)(2,1)S(1)} %get-tuple-element.94.refs_1_, f32[64,256]{1,0:T(8,128)S(1)} %get-tuple-element.95.refs_2_, f32[8,256]{1,0:T(8,128)S(1)} %get-tuple-element.96.refs_3_, ...), custom_call_target="tpu_custom_call" | custom-call | flops 1614899968 | bytes 5166000 | tf_op jit(solution)/shard_map/pallas_call | solution.py:90
  (45 shorter events, 1.0 us)
Async XLA Ops:
  0.6 0.7 copy-start.5
  1.3 0.9 %copy-start.3 = (bf16[256,2,128]{2,1,0:T(2,128)(2,1)S(1)}, bf16[256,2,128]{2,1,0:T(2,128)(2,1)}, u32[]{:S(2)}) copy-start(bf16[256,2,128]{2,1,0:T(2,128)(2,1)} %param.10) | copy-start | bytes 393220
  2.2 2.4 %copy-start.4 = (s32[64]{0:T(128)S(1)}, s32[64]{0:T(128)}, u32[]{:S(2)}) copy-start(s32[64]{0:T(128)} %refs_1_.1) | copy-start | bytes 772
  2.5 2.9 %copy-start.6 = (bf16[1792]{0:T(1024)(128)(2,1)S(1)}, bf16[1792]{0:T(1024)(128)(2,1)}, u32[]{:S(2)}) copy-start(bf16[1792]{0:T(1024)(128)(2,1)} %param.8) | copy-start | bytes 10756
  2.5 14.2 %copy-start = (bf16[256,1792]{1,0:T(8,128)(2,1)S(1)}, bf16[256,1792]{1,0:T(8,128)(2,1)}, u32[]{:S(2)}) copy-start(bf16[256,1792]{1,0:T(8,128)(2,1)} %refs_5_.1) | copy-start | bytes 2752516
  2.5 14.1 %copy-start.1 = (bf16[256,896]{1,0:T(8,128)(2,1)S(1)}, bf16[256,896]{1,0:T(8,128)(2,1)}, u32[]{:S(2)}) copy-start(bf16[256,896]{1,0:T(8,128)(2,1)} %refs_3_.1) | copy-start | bytes 1376260
  2.5 14.1 %copy-start.2 = (bf16[256,896]{1,0:T(8,128)(2,1)S(1)}, bf16[256,896]{1,0:T(8,128)(2,1)}, u32[]{:S(2)}) copy-start(bf16[256,896]{1,0:T(8,128)(2,1)} %refs_4_.1) | copy-start | bytes 1376260
  2.5 4.0 %collective-permute-start = (bf16[64,256]{1,0:T(8,128)(2,1)S(1)}, bf16[64,256]{1,0:T(8,128)(2,1)S(1)}, u32[]{:S(2)}, u32[]{:S(2)}) collective-permute-start(bf16[64,256]{1,0:T(8,128)(2,1)S(1)} %shard_map.102.refs_0_), channel_id=1, source_target_pairs={{0,8},{4,12},{8,0},{12,4},{16,24},{20,28},{24,16},{28,20},{32,40},... | collective-permute-start | bytes 98312 | tf_op jit(solution)/shard_map/ppermute | solution.py:40
  6.6 15.5 %collective-permute-start.5 = (bf16[128,256]{1,0:T(8,128)(2,1)S(1)}, bf16[128,256]{1,0:T(8,128)(2,1)S(1)}, u32[]{:S(2)}, u32[]{:S(2)}) collective-permute-start(bf16[128,256]{1,0:T(8,128)(2,1)S(1)} %shard_map.104.refs_0_.refs_2_), channel_id=1, source_target_pairs={{0,48},{4,52},{8,56},{12,60},{16,0},{20,4},{24,8},{28,12},{32,16},... | collective-permute-start | bytes 196616 | tf_op jit(solution)/shard_map/ppermute | solution.py:40
  12.9 9.2 %collective-permute-start.4 = (bf16[128,256]{1,0:T(8,128)(2,1)S(1)}, bf16[128,256]{1,0:T(8,128)(2,1)S(1)}, u32[]{:S(2)}, u32[]{:S(2)}) collective-permute-start(bf16[128,256]{1,0:T(8,128)(2,1)S(1)} %shard_map.104.refs_0_.refs_2_), channel_id=1, source_target_pairs={{0,32},{4,36},{8,40},{12,44},{16,48},{20,52},{24,56},{28,60},{32,0... | collective-permute-start | bytes 196616 | tf_op jit(solution)/shard_map/ppermute | solution.py:40
  13.8 8.2 %collective-permute-start.3 = (bf16[128,256]{1,0:T(8,128)(2,1)S(1)}, bf16[128,256]{1,0:T(8,128)(2,1)S(1)}, u32[]{:S(2)}, u32[]{:S(2)}) collective-permute-start(bf16[128,256]{1,0:T(8,128)(2,1)S(1)} %shard_map.104.refs_0_.refs_2_), channel_id=1, source_target_pairs={{0,16},{4,20},{8,24},{12,28},{16,32},{20,36},{24,40},{28,44},{32,4... | collective-permute-start | bytes 196616 | tf_op jit(solution)/shard_map/ppermute | solution.py:40
  17.2 12.9 %collective-permute-start.7 = (bf16[64,1792]{1,0:T(8,128)(2,1)S(1)}, bf16[64,1792]{1,0:T(8,128)(2,1)S(1)}, u32[]{:S(2)}, u32[]{:S(2)}) collective-permute-start(bf16[64,1792]{1,0:T(8,128)(2,1)S(1)} %get-tuple-element.58.refs_0_), channel_id=1, source_target_pairs={{0,4},{4,0},{8,12},{12,8},{16,20},{20,16},{24,28},{28,24},{32,36},... | collective-permute-start | bytes 688136 | tf_op jit(solution)/shard_map/ppermute | solution.py:40
  17.3 3.6 %collective-permute-start.1 = (f32[1,128]{1,0:T(1,128)S(1)}, f32[1,128]{1,0:T(1,128)S(1)}, u32[]{:S(2)}, u32[]{:S(2)}) collective-permute-start(f32[1,128]{1,0:T(1,128)S(1)} %get-tuple-element.56.refs_0_), channel_id=1, source_target_pairs={{0,1},{1,0},{2,3},{3,2},{4,5},{5,4},{6,7},{7,6},{8,9},{9,8},{10,11... | collective-permute-start | bytes 1544 | tf_op jit(solution)/shard_map/ppermute | solution.py:76
  20.9 1.1 %collective-permute-start.2 = (f32[1,128]{1,0:T(1,128)S(1)}, f32[1,128]{1,0:T(1,128)S(1)}, u32[]{:S(2)}, u32[]{:S(2)}) collective-permute-start(f32[1,128]{1,0:T(1,128)S(1)} %shard_map.106.refs_0_), channel_id=1, source_target_pairs={{0,4},{4,0},{8,12},{12,8},{16,20},{20,16},{24,28},{28,24},{32,36},... | collective-permute-start | bytes 1544 | tf_op jit(solution)/shard_map/ppermute | solution.py:40
  22.1 9.3 %collective-permute-start.9 = (bf16[512,256]{1,0:T(8,128)(2,1)S(1)}, bf16[512,256]{1,0:T(8,128)(2,1)S(1)}, u32[]{:S(2)}, u32[]{:S(2)}) collective-permute-start(bf16[512,256]{1,0:T(8,128)(2,1)S(1)} %get-tuple-element.57.refs_1_.refs_4_), channel_id=1, source_target_pairs={{0,64},{4,68},{8,72},{12,76},{16,80},{20,84},{24,88},{28,92},{32,9... | collective-permute-start | bytes 786440 | tf_op jit(solution)/shard_map/ppermute | solution.py:40
  23.7 10.7 %collective-permute-start.8 = (bf16[512,256]{1,0:T(8,128)(2,1)S(1)}, bf16[512,256]{1,0:T(8,128)(2,1)S(1)}, u32[]{:S(2)}, u32[]{:S(2)}) collective-permute-start(bf16[512,256]{1,0:T(8,128)(2,1)S(1)} %get-tuple-element.57.refs_1_.refs_4_), channel_id=1, source_target_pairs={{0,128},{4,132},{8,136},{12,140},{16,144},{20,148},{24,152},{28,15... | collective-permute-start | bytes 786440 | tf_op jit(solution)/shard_map/ppermute | solution.py:40
  24.8 13.5 %collective-permute-start.6 = (bf16[512,256]{1,0:T(8,128)(2,1)S(1)}, bf16[512,256]{1,0:T(8,128)(2,1)S(1)}, u32[]{:S(2)}, u32[]{:S(2)}) collective-permute-start(bf16[512,256]{1,0:T(8,128)(2,1)S(1)} %get-tuple-element.57.refs_1_.refs_4_), channel_id=1, source_target_pairs={{0,192},{4,196},{8,200},{12,204},{16,208},{20,212},{24,216},{28,22... | collective-permute-start | bytes 786440 | tf_op jit(solution)/shard_map/ppermute | solution.py:40
  26.9 7.5 %collective-permute-start.10 = (f32[1,128]{1,0:T(1,128)S(1)}, f32[1,128]{1,0:T(1,128)S(1)}, u32[]{:S(2)}, u32[]{:S(2)}) collective-permute-start(f32[1,128]{1,0:T(1,128)S(1)} %get-tuple-element.68.refs_2_), channel_id=1, source_target_pairs={{0,2},{1,3},{2,0},{3,1},{4,6},{5,7},{6,4},{7,5},{8,10},{9,11},{10,... | collective-permute-start | bytes 1544 | tf_op jit(solution)/shard_map/ppermute | solution.py:76
  38.4 1.5 %collective-permute-start.11 = (f32[8,896]{1,0:T(8,128)S(1)}, f32[8,896]{1,0:T(8,128)S(1)}, u32[]{:S(2)}, u32[]{:S(2)}) collective-permute-start(f32[8,896]{1,0:T(8,128)S(1)} %get-tuple-element.72.refs_0_.refs_6_.refs_9_.refs_1_), channel_id=1, source_target_pairs={{0,4},{4,0},{8,12},{12,8},{16,20},{20,16},{24,28},{28,24},{32,36},... | collective-permute-start | bytes 86024 | tf_op jit(solution)/shard_map/ppermute | solution.py:40
  38.7 20.7 %collective-permute-start.12 = (f32[128,896]{1,0:T(8,128)S(1)}, f32[128,896]{1,0:T(8,128)S(1)}, u32[]{:S(2)}, u32[]{:S(2)}) collective-permute-start(f32[128,896]{1,0:T(8,128)S(1)} %get-tuple-element.73.refs_3_), channel_id=1, source_target_pairs={{0,4},{4,0},{8,12},{12,8},{16,20},{20,16},{24,28},{28,24},{32,36},... | collective-permute-start | bytes 1376264 | tf_op jit(solution)/shard_map/ppermute | solution.py:40
  39.9 3.6 %collective-permute-start.13 = (f32[1,128]{1,0:T(1,128)S(1)}, f32[1,128]{1,0:T(1,128)S(1)}, u32[]{:S(2)}, u32[]{:S(2)}) collective-permute-start(f32[1,128]{1,0:T(1,128)S(1)} %shard_map.114.refs_8_), channel_id=1, source_target_pairs={{0,1},{1,0},{2,3},{3,2},{4,5},{5,4},{6,7},{7,6},{8,9},{9,8},{10,11... | collective-permute-start | bytes 1544 | tf_op jit(solution)/shard_map/ppermute | solution.py:76
  41.6 11.0 %collective-permute-start.14 = (bf16[512,256]{1,0:T(8,128)(2,1)S(1)}, bf16[512,256]{1,0:T(8,128)(2,1)S(1)}, u32[]{:S(2)}, u32[]{:S(2)}) collective-permute-start(bf16[512,256]{1,0:T(8,128)(2,1)S(1)} %get-tuple-element.80), channel_id=1, source_target_pairs={{128,64},{132,68},{136,72},{140,76},{144,80},{148,84},{152,88},{15... | collective-permute-start | bytes 786440 | tf_op jit(solution)/shard_map/ppermute | solution.py:40
  43.6 9.1 %collective-permute-start.15 = (f32[1,128]{1,0:T(1,128)S(1)}, f32[1,128]{1,0:T(1,128)S(1)}, u32[]{:S(2)}, u32[]{:S(2)}) collective-permute-start(f32[1,128]{1,0:T(1,128)S(1)} %get-tuple-element.81.refs_2_), channel_id=1, source_target_pairs={{0,2},{1,3},{2,0},{3,1},{4,6},{5,7},{6,4},{7,5},{8,10},{9,11},{10,... | collective-permute-start | bytes 1544 | tf_op jit(solution)/shard_map/ppermute | solution.py:76
  46.9 12.5 %collective-permute-start.17 = (bf16[512,256]{1,0:T(8,128)(2,1)S(1)}, bf16[512,256]{1,0:T(8,128)(2,1)S(1)}, u32[]{:S(2)}, u32[]{:S(2)}) collective-permute-start(bf16[512,256]{1,0:T(8,128)(2,1)S(1)} %get-tuple-element.83), channel_id=1, source_target_pairs={{192,0},{196,4},{200,8},{204,12},{208,16},{212,20},{216,24},{220,2... | collective-permute-start | bytes 786440 | tf_op jit(solution)/shard_map/ppermute | solution.py:40
  52.8 4.0 %collective-permute-start.16 = (f32[8,256]{1,0:T(8,128)S(1)}, f32[8,256]{1,0:T(8,128)S(1)}, u32[]{:S(2)}, u32[]{:S(2)}) collective-permute-start(f32[8,256]{1,0:T(8,128)S(1)} %shard_map.119.refs_0_), channel_id=1, source_target_pairs={{0,64},{4,68},{8,72},{12,76},{16,80},{20,84},{24,88},{28,92},{32,9... | collective-permute-start | bytes 24584 | tf_op jit(solution)/shard_map/ppermute | solution.py:40
  52.9 11.7 %collective-permute-start.18 = (bf16[512,256]{1,0:T(8,128)(2,1)S(1)}, bf16[512,256]{1,0:T(8,128)(2,1)S(1)}, u32[]{:S(2)}, u32[]{:S(2)}) collective-permute-start(bf16[512,256]{1,0:T(8,128)(2,1)S(1)} %shard_map.118.refs_0_), channel_id=1, source_target_pairs={{64,0},{68,4},{72,8},{76,12},{80,16},{84,20},{88,24},{92,28},{96,3... | collective-permute-start | bytes 786440 | tf_op jit(solution)/shard_map/ppermute | solution.py:40
  56.9 7.8 %collective-permute-start.19 = (f32[8,256]{1,0:T(8,128)S(1)}, f32[8,256]{1,0:T(8,128)S(1)}, u32[]{:S(2)}, u32[]{:S(2)}) collective-permute-start(f32[8,256]{1,0:T(8,128)S(1)} %shard_map.120.refs_0_.refs_3_), channel_id=1, source_target_pairs={{0,128},{4,132},{8,136},{12,140},{16,144},{20,148},{24,152},{28,15... | collective-permute-start | bytes 24584 | tf_op jit(solution)/shard_map/ppermute | solution.py:40
  64.7 5.2 %collective-permute-start.20 = (bf16[272,256]{1,0:T(8,128)(2,1)S(1)}, bf16[272,256]{1,0:T(8,128)(2,1)S(1)}, u32[]{:S(2)}, u32[]{:S(2)}) collective-permute-start(bf16[272,256]{1,0:T(8,128)(2,1)S(1)} %get-tuple-element.87), channel_id=1, source_target_pairs={{0,8},{4,12},{8,0},{12,4},{16,24},{20,28},{24,16},{28,20},{32,40},... | collective-permute-start | bytes 417800 | tf_op jit(solution)/shard_map/ppermute | solution.py:40
  65.8 3.1 %collective-permute-start.22 = (f32[8,256]{1,0:T(8,128)S(1)}, f32[8,256]{1,0:T(8,128)S(1)}, u32[]{:S(2)}, u32[]{:S(2)}) collective-permute-start(f32[8,256]{1,0:T(8,128)S(1)} %get-tuple-element.88.refs_2_), channel_id=1, source_target_pairs={{0,12},{4,8},{8,4},{12,0},{16,28},{20,24},{24,20},{28,16},{32,44},... | collective-permute-start | bytes 24584 | tf_op jit(solution)/shard_map/ppermute | solution.py:40
  65.8 3.1 %collective-permute-start.21 = (f32[8,256]{1,0:T(8,128)S(1)}, f32[8,256]{1,0:T(8,128)S(1)}, u32[]{:S(2)}, u32[]{:S(2)}) collective-permute-start(f32[8,256]{1,0:T(8,128)S(1)} %get-tuple-element.88.refs_2_), channel_id=1, source_target_pairs={{0,4},{4,0},{8,12},{12,8},{16,20},{20,16},{24,28},{28,24},{32,36},... | collective-permute-start | bytes 24584 | tf_op jit(solution)/shard_map/ppermute | solution.py:40
  70.0 6.5 %collective-permute-start.23 = (f32[128,896]{1,0:T(8,128)S(1)}, f32[128,896]{1,0:T(8,128)S(1)}, u32[]{:S(2)}, u32[]{:S(2)}) collective-permute-start(f32[128,896]{1,0:T(8,128)S(1)} %get-tuple-element.90.refs_6_), channel_id=1, source_target_pairs={{0,4},{4,0},{8,12},{12,8},{16,20},{20,16},{24,28},{28,24},{32,36},... | collective-permute-start | bytes 1376264 | tf_op jit(solution)/shard_map/ppermute | solution.py:40
  70.2 7.8 %collective-permute-start.24 = (bf16[80,256]{1,0:T(8,128)(2,1)S(1)}, bf16[80,256]{1,0:T(8,128)(2,1)S(1)}, u32[]{:S(2)}, u32[]{:S(2)}) collective-permute-start(bf16[80,256]{1,0:T(8,128)(2,1)S(1)} %get-tuple-element.97), channel_id=1, source_target_pairs={{0,48},{4,52},{8,56},{12,60},{16,0},{20,4},{24,8},{28,12},{32,16},... | collective-permute-start | bytes 122888 | tf_op jit(solution)/shard_map/ppermute | solution.py:40
  71.6 9.2 %collective-permute-start.25 = (bf16[80,256]{1,0:T(8,128)(2,1)S(1)}, bf16[80,256]{1,0:T(8,128)(2,1)S(1)}, u32[]{:S(2)}, u32[]{:S(2)}) collective-permute-start(bf16[80,256]{1,0:T(8,128)(2,1)S(1)} %get-tuple-element.98), channel_id=1, source_target_pairs={{0,32},{4,36},{8,40},{12,44},{16,48},{20,52},{24,56},{28,60},{32,0... | collective-permute-start | bytes 122888 | tf_op jit(solution)/shard_map/ppermute | solution.py:40
  76.5 6.2 %collective-permute-start.26 = (bf16[80,256]{1,0:T(8,128)(2,1)S(1)}, bf16[80,256]{1,0:T(8,128)(2,1)S(1)}, u32[]{:S(2)}, u32[]{:S(2)}) collective-permute-start(bf16[80,256]{1,0:T(8,128)(2,1)S(1)} %get-tuple-element.99), channel_id=1, source_target_pairs={{0,16},{4,20},{8,24},{12,28},{16,32},{20,36},{24,40},{28,44},{32,4... | collective-permute-start | bytes 122888 | tf_op jit(solution)/shard_map/ppermute | solution.py:40
